TPU v7x, 32 devices: a whole 2x2x4 slice. The times are simulated.
32 devices in a mesh: axial: 4 (over y, x), azim: 8 (over z, core).
Axes of the slice: x: 2, y: 2, z: 4, core: 2. Of those that a mesh axis runs over, the one named last changes fastest.
Arguments:
- density: float32 [64, 64, 512], P(None, 'azim', 'axial'), may hold values from 0.5 to 2
- velocity: float32 [3, 64, 64, 512], P(None, None, 'azim', 'axial'), may hold values from -3 to 3
- pressure: float32 [64, 64, 512], P(None, 'azim', 'axial'), may hold values from 0.4 to 1.5
- axial_metric: float32 [3, 64, 64, 512], P(None, None, 'azim', 'axial'), may hold values from -4 to 4
- azim_metric: float32 [3, 64, 64, 512], P(None, None, 'azim', 'axial'), may hold values from -4 to 4
- volume: float32 [64, 64, 512], P(None, 'azim', 'axial'), may hold values from 0.5 to 2
- radial_term: float32 [5, 64, 64, 512], P(None, None, 'azim', 'axial'), may hold values from -6 to 6
- panel_area: float32 [64, 512], P('azim', 'axial'), may hold values from 0.5 to 2
- observer_ids: int32 [4, 64, 512], P(None, 'azim', 'axial'), may hold values from 0 to 511
- bin_ids: int32 [4, 64, 512], P(None, 'azim', 'axial'), may hold values from 0 to 127
- weight_ids: int32 [4, 64, 512], P(None, 'azim', 'axial'), may hold values from 0 to 255
- bin_weights: float32 [256], replicated, may hold values from 0.2 to 1
Outputs:
- new_state: float32 [5, 64, 64, 512], P(None, None, 'azim', 'axial')
- signals: float32 [512, 128], P(('axial', 'azim'))
All inputs are finite; a program needn't handle non-finite values.
Results may differ from a plain program's by a relative error of at most 0.0003.
Values sent between devices are 32-bit elements; how exact they have to be, the bound alone decides.
No kernel may reach another device: no remote copies, remote signals or barrier semaphores. Data moves between devices by JAX's collectives and lax.ppermute only.
A program may use at most 128 MiB of HBM per device.

v0:
```python
import math

import jax
import jax.numpy as jnp
from jax import lax
from jax.sharding import PartitionSpec as P

OBSERVERS = 512
TIME_BINS = 128


GAMMA = 1.4
SECTION = 0.25
DERIV_ALPHA = 1.0 / 3.0
FILTER_ALPHA = 0.499
DERIV_A = 14.0 / 9.0
DERIV_B = 1.0 / 9.0
HIGHEST = lax.Precision.HIGHEST


def padded(cells, sides, width, closed):
    for axis, dim in sides:
        count = lax.axis_size(axis)
        ends = count if closed else count - 1
        head = lax.slice_in_dim(cells, 0, width, axis=dim)
        tail = lax.slice_in_dim(cells, cells.shape[dim] - width, cells.shape[dim], axis=dim)
        cells = jnp.concatenate(
            [
                lax.ppermute(tail, axis, [(i, (i + 1) % count) for i in range(ends)]),
                cells,
                lax.ppermute(head, axis, [((i + 1) % count, i) for i in range(ends)]),
            ],
            axis=dim,
        )
    return cells


def decay_root(alpha):
    return (-1.0 + math.sqrt(1.0 - 4.0 * alpha * alpha)) / (2.0 * alpha)


def signed_power(base, exponent):
    exponent = jnp.asarray(exponent)
    parity = jnp.where(exponent % 2 == 0, 1.0, -1.0)
    return parity * jnp.exp(exponent.astype(jnp.float32) * math.log(-base))


def deriv_side(extended, dim):
    length = extended.shape[dim] - 6

    def cells(offset):
        return lax.slice_in_dim(extended, 3 + offset, 3 + offset + length, axis=dim)

    return 0.5 * DERIV_A * (cells(1) - cells(-1)) + 0.25 * DERIV_B * (cells(2) - cells(-2))


def filter_side(extended, dim):
    length = extended.shape[dim] - 6

    def cells(offset):
        return lax.slice_in_dim(extended, 3 + offset, 3 + offset + length, axis=dim)

    beta = FILTER_ALPHA
    coeffs = [
        (11.0 + 10.0 * beta) / 16.0,
        (15.0 + 34.0 * beta) / 32.0,
        (-3.0 + 6.0 * beta) / 16.0,
        (1.0 - 2.0 * beta) / 32.0,
    ]
    total = coeffs[0] * cells(0)
    for shift in range(1, 4):
        total = total + 0.5 * coeffs[shift] * (cells(shift) + cells(-shift))
    return total


def fluxes(density, velocity, pressure, energy, metric, volume):
    contra = metric[0] * velocity[0] + metric[1] * velocity[1] + metric[2] * velocity[2]
    mass_flow = density * contra
    pieces = [volume * mass_flow]
    for comp in range(3):
        pieces.append(volume * (mass_flow * velocity[comp] + metric[comp] * pressure))
    pieces.append(volume * (energy + pressure) * contra)
    return jnp.stack(pieces)


def pad_axial(field):
    return padded(field, (("axial", 3),), 3, False)


def pad_azimuth(field):
    return padded(field, (("azim", 2),), 3, True)


def open_line(rhs, alpha):
    base = decay_root(alpha)
    factor_g = -alpha / base
    scale = 1.0 / (factor_g * (1.0 - base * base))
    width_here = rhs.shape[3]
    group_size = lax.axis_size("axial")
    device_pos = lax.axis_index("axial")
    total_len = width_here * group_size
    offsets = jnp.arange(width_here, dtype=jnp.int32)
    local_matrix = signed_power(base, jnp.abs(offsets[:, None] - offsets[None, :]))
    local_part = jnp.einsum("vraj,ij->vrai", rhs, local_matrix, precision=HIGHEST)
    first_moment = jnp.einsum(
        "vraj,j->vra", rhs, signed_power(base, width_here - 1 - offsets), precision=HIGHEST
    )
    last_moment = jnp.einsum("vraj,j->vra", rhs, signed_power(base, offsets), precision=HIGHEST)
    moments = jnp.stack([first_moment, last_moment])[None]
    piece = lax.all_gather(moments, "axial", axis=0, tiled=True)
    others = jnp.arange(piece.shape[0], dtype=jnp.int32)
    gap_up = device_pos - others
    w_left = jnp.where(
        gap_up > 0, signed_power(base, width_here * jnp.maximum(gap_up - 1, 0) + 1), 0.0
    )
    w_right = jnp.where(
        gap_up < 0, signed_power(base, width_here * jnp.maximum(-gap_up - 1, 0) + 1), 0.0
    )
    w_end = signed_power(base, width_here * (group_size - 1 - others))
    left_sum = jnp.einsum("k,kvra->vra", w_left, piece[:, 0], precision=HIGHEST)
    right_sum = jnp.einsum("k,kvra->vra", w_right, piece[:, 1], precision=HIGHEST)
    end_sum = jnp.einsum("k,kvra->vra", w_end, piece[:, 0], precision=HIGHEST)
    left_sum, right_sum, end_sum = (left_sum, right_sum, end_sum)
    position = device_pos * width_here + offsets
    result = local_part + signed_power(base, offsets) * left_sum[..., None]
    result = result + signed_power(base, width_here - 1 - offsets) * right_sum[..., None]
    result = result - signed_power(base, total_len + 1 - position) * end_sum[..., None]
    return scale * result


def cycle_line(rhs, alpha):
    base = decay_root(alpha)
    factor_g = -alpha / base
    width_here = rhs.shape[2]
    group_size = lax.axis_size("azim")
    device_pos = lax.axis_index("azim")
    total_len = width_here * group_size
    scale = 1.0 / (factor_g * (1.0 - base * base) * (1.0 - base**total_len))
    offsets = jnp.arange(width_here, dtype=jnp.int32)
    gap = jnp.abs(offsets[:, None] - offsets[None, :])
    local_matrix = scale * (signed_power(base, gap) + signed_power(base, total_len - gap))
    local_part = jnp.einsum("vrjx,ij->vrix", rhs, local_matrix, precision=HIGHEST)
    first_moment = jnp.einsum(
        "vrjx,j->vrx", rhs, signed_power(base, width_here - 1 - offsets), precision=HIGHEST
    )
    last_moment = jnp.einsum("vrjx,j->vrx", rhs, signed_power(base, offsets), precision=HIGHEST)
    moments = jnp.stack([first_moment, last_moment])[None]
    piece = lax.all_gather(moments, "azim", axis=0, tiled=True)
    others = jnp.arange(piece.shape[0], dtype=jnp.int32)
    shift = (device_pos - others) % group_size
    w_first = jnp.where(
        shift > 0, signed_power(base, width_here * jnp.maximum(shift - 1, 0) + 1), 0.0
    )
    w_last = jnp.where(
        shift > 0, signed_power(base, width_here * jnp.maximum(group_size - shift - 1, 0) + 1), 0.0
    )
    first_sum = jnp.einsum("k,kvrx->vrx", w_first, piece[:, 0], precision=HIGHEST)
    last_sum = jnp.einsum("k,kvrx->vrx", w_last, piece[:, 1], precision=HIGHEST)
    outer = signed_power(base, offsets)[:, None] * first_sum[:, :, None, :]
    outer = outer + signed_power(base, width_here - 1 - offsets)[:, None] * last_sum[:, :, None, :]
    return local_part + scale * outer


def per_device(
    density,
    velocity,
    pressure,
    axial_metric,
    azim_metric,
    volume,
    radial_term,
    panel_area,
    observer_ids,
    bin_ids,
    weight_ids,
    bin_weights,
):
    energy = pressure / (GAMMA - 1.0) + 0.5 * density * (
        velocity[0] ** 2 + velocity[1] ** 2 + velocity[2] ** 2
    )
    state = jnp.concatenate([density[None], density[None] * velocity, energy[None]], axis=0)
    axial_flux = fluxes(density, velocity, pressure, energy, axial_metric, volume)
    azim_flux = fluxes(density, velocity, pressure, energy, azim_metric, volume)
    axial_deriv = open_line(deriv_side(pad_axial(axial_flux), 3), DERIV_ALPHA)
    azim_deriv = cycle_line(deriv_side(pad_azimuth(azim_flux), 2), DERIV_ALPHA)
    sectioned = state + SECTION * (radial_term - (axial_deriv + azim_deriv) / volume)
    smoothed = open_line(filter_side(pad_axial(sectioned), 3), FILTER_ALPHA)
    new_state = cycle_line(filter_side(pad_azimuth(smoothed), 2), FILTER_ALPHA)
    surface = new_state[:, 0]
    source = panel_area * (surface[2] + surface[0] - 1.0)
    table_size = bin_weights.shape[0]
    one_hot = (
        weight_ids.reshape(-1)[:, None] == jnp.arange(table_size, dtype=jnp.int32)[None, :]
    ).astype(jnp.float32)
    entry_weight = jnp.dot(one_hot, bin_weights, precision=HIGHEST)
    values = entry_weight * jnp.broadcast_to(source[None], weight_ids.shape).reshape(-1)
    bucket = (observer_ids * TIME_BINS + bin_ids).reshape(-1)
    partial_signals = jax.ops.segment_sum(
        values, bucket, num_segments=OBSERVERS * TIME_BINS
    ).reshape(OBSERVERS, TIME_BINS)
    signals = lax.psum_scatter(partial_signals, ("axial", "azim"), scatter_dimension=0, tiled=True)
    return (new_state, signals)


def solution(mesh):
    placed = (
        P(None, "azim", "axial"),
        P(None, None, "azim", "axial"),
        P(None, "azim", "axial"),
        P(None, None, "azim", "axial"),
        P(None, None, "azim", "axial"),
        P(None, "azim", "axial"),
        P(None, None, "azim", "axial"),
        P("azim", "axial"),
        P(None, "azim", "axial"),
        P(None, "azim", "axial"),
        P(None, "azim", "axial"),
        P(),
    )
    return jax.shard_map(
        per_device,
        mesh=mesh,
        in_specs=placed,
        out_specs=(P(None, None, "azim", "axial"), P(("axial", "azim"), None)),
        check_vma=False,
    )
```

profile of v0, /device:TPU:0, one launch (start us, length us, event | category | flops | bytes accessed | tf_op | source)
XLA Modules:
  0.0 400.8 jit_solution(456449613454082127)
XLA Ops:
  7.3 2.7 bitcast_dynamic-update-slice_fusion.4
  12.7 4.5 %collective-permute-start.2 = (f32[5,64,3,128]{3,1,2,0:T(8,128)S(1)}, f32[5,64,3,128]{3,1,2,0:T(8,128)S(1)}, u32[]{:S(2)}, u32[]{:S(2)}) collective-permute-start(f32[5,64,3,128]{3,1,2,0:T(8,128)S(1)} %copy.18), channel_id=1, source_target_pairs={{1,0},{2,1},{3,2},{4,3},{5,4},{6,5},{7,6},{0,7},{9,8},{10,9},{11,1... | collective-permute-start | bytes 1474568 | tf_op jit(solution)/shard_map/ppermute | solution.py:31
  17.3 9.6 %collective-permute-done.2 = f32[5,64,3,128]{3,1,2,0:T(8,128)S(1)} collective-permute-done((f32[5,64,3,128]{3,1,2,0:T(8,128)S(1)}, f32[5,64,3,128]{3,1,2,0:T(8,128)S(1)}, u32[]{:S(2)}, u32[]{:S(2)}) %collective-permute-start.2) | collective-permute-done | bytes 491552 | tf_op jit(solution)/shard_map/ppermute | solution.py:31
  27.3 2.6 collective-permute-done.3
  40.3 4.7 %collective-permute-start.1 = (f32[5,64,8,3]{1,2,3,0:T(8,128)}, f32[5,64,8,3]{1,2,3,0:T(8,128)S(1)}, u32[]{:S(2)}, u32[]{:S(2)}) collective-permute-start(f32[5,64,8,3]{1,2,3,0:T(8,128)} %copy.16), channel_id=1, source_target_pairs={{0,8},{8,16},{16,24},{1,9},{9,17},{17,25},{2,10},{10,18},{18,26},{... | collective-permute-start | bytes 92168 | tf_op jit(solution)/shard_map/ppermute | solution.py:29
  45.7 1.9 broadcast_multiply_fusion.1
  50.8 5.8 %fusion.22 = f32[5,64,8,128]{3,2,1,0:T(8,128)S(1)} fusion(f32[5,64,8,3]{3,2,1,0:T(8,128)} %copy.17, f32[5,64,8,128]{3,2,1,0:T(8,128)S(1)} %bitcast_dynamic-update-slice_fusion.5, f32[5,64,8,3]{3,2,1,0:T(8,128)} %copy.15), kind=kLoop, calls=%fused_computation.52 | loop fusion | flops 2949120 | bytes 2682880 | tf_op jit(solution)/shard_map/add | solution.py:54
  56.6 17.3 %fusion.215 = f32[1,5,64,8]{3,0,2,1:T(1,128)S(1)} fusion(f32[5,64,8,128]{3,2,1,0:T(8,128)S(1)} %fusion.22), kind=kOutput, calls=%fused_computation.350 | convolution fusion | flops 3934336 | bytes 1320960 | tf_op jit(solution)/shard_map/vraj,j->vra/dot_general | solution.py:105
  74.0 17.7 %fusion.213 = f32[1,5,64,8]{3,0,2,1:T(1,128)S(1)} fusion(f32[5,64,8,128]{3,2,1,0:T(8,128)S(1)} %fusion.22), kind=kOutput, calls=%fused_computation.348 | convolution fusion | flops 3933568 | bytes 1320960 | tf_op jit(solution)/shard_map/vraj,j->vra/dot_general | solution.py:108
  91.8 9.4 %all-gather = f32[8,5,64,8]{2,3,1,0:T(8,128)S(1)} all-gather(f32[2,5,64,8]{2,3,1,0:T(8,128)S(1)} %pad_maximum_fusion.10), channel_id=2, replica_groups=mesh['axial'=4,'azim'=8] {'axial'}, dimensions={0}, use_global_device_ids=true | all-gather | bytes 102400 | tf_op jit(solution)/shard_map/all_gather | solution.py:110
  102.5 2.5 fusion.11
  105.1 2.0 slice_bitcast_fusion.3
  107.2 1.8 fusion.60
  117.7 4.6 %collective-permute-start.5 = (f32[5,64,8,3]{1,2,3,0:T(8,128)S(1)}, f32[5,64,8,3]{1,2,3,0:T(8,128)S(1)}, u32[]{:S(2)}, u32[]{:S(2)}) collective-permute-start(f32[5,64,8,3]{1,2,3,0:T(8,128)S(1)} %copy.24), channel_id=1, source_target_pairs={{0,8},{8,16},{16,24},{1,9},{9,17},{17,25},{2,10},{10,18},{18,26},{... | collective-permute-start | bytes 92168 | tf_op jit(solution)/shard_map/ppermute | solution.py:29
  125.7 6.4 %fusion.39 = f32[5,64,8,128]{3,2,1,0:T(8,128)S(1)} fusion(f32[5,64,8,3]{3,2,1,0:T(8,128)} %copy.25, f32[5,64,8,128]{3,2,1,0:T(8,128)S(1)} %fusion.13, f32[5,64,8,3]{3,2,1,0:T(8,128)} %copy.23), kind=kLoop, calls=%fused_computation.69 | loop fusion | flops 5242880 | bytes 2682880 | tf_op jit(solution)/shard_map/add | solution.py:72
  132.1 17.3 %fusion.204 = f32[1,5,64,8]{3,0,2,1:T(1,128)S(1)} fusion(f32[5,64,8,128]{3,2,1,0:T(8,128)S(1)} %fusion.39), kind=kOutput, calls=%fused_computation.339 | convolution fusion | flops 3934336 | bytes 1320960 | tf_op jit(solution)/shard_map/vraj,j->vra/dot_general | solution.py:105
  149.4 17.5 %fusion.202 = f32[1,5,64,8]{3,0,2,1:T(1,128)S(1)} fusion(f32[5,64,8,128]{3,2,1,0:T(8,128)S(1)} %fusion.39), kind=kOutput, calls=%fused_computation.337 | convolution fusion | flops 3933568 | bytes 1320960 | tf_op jit(solution)/shard_map/vraj,j->vra/dot_general | solution.py:108
  167.1 9.8 %all-gather.2 = f32[8,5,64,8]{2,3,1,0:T(8,128)S(1)} all-gather(f32[2,5,64,8]{2,3,1,0:T(8,128)S(1)} %pad_maximum_fusion.11), channel_id=4, replica_groups=mesh['axial'=4,'azim'=8] {'axial'}, dimensions={0}, use_global_device_ids=true | all-gather | bytes 102400 | tf_op jit(solution)/shard_map/all_gather | solution.py:110
  180.8 10.9 %collective-permute-done.6 = f32[5,64,3,128]{3,1,2,0:T(8,128)S(1)} collective-permute-done((f32[5,64,3,128]{3,1,2,0:T(8,128)S(1)}, f32[5,64,3,128]{3,1,2,0:T(8,128)S(1)}, u32[]{:S(2)}, u32[]{:S(2)}) %collective-permute-start.6) | collective-permute-done | bytes 491552 | tf_op jit(solution)/shard_map/ppermute | solution.py:31
  199.2 2.4 fusion
  201.6 30.2 %all-gather.9.cloned.1.call-done = f32[16,5,64,128]{3,2,1,0:T(8,128)} async-done(((f32[2,5,64,128]{3,2,1,0:T(8,128)}), f32[16,5,64,128]{3,2,1,0:T(8,128)}) %all-gather.9.cloned.1.call-update) | async-done | bytes 2621456 | tf_op jit(solution)/shard_map/all_gather | solution.py:148
  231.9 1.9 slice_bitcast_fusion.1
  238.9 22.6 %scatter_custom_fusion = f32[65536]{0:T(1024)} fusion(s32[4096]{0:T(1024)S(1)} %add_bitcast_fusion, f32[4096]{0:T(1024)S(1)} %bitcast_multiply_fusion.21, f32[]{:T(128)} %constant.246.clone.1), kind=kCustom, calls=%fused_computation.160 | custom fusion | flops 4096 | bytes 262148 | tf_op jit(solution)/shard_map/scatter-add | solution.py:198
  261.5 132.6 %reduce-scatter.2.cloned.1.call-done = f32[16,128]{1,0:T(8,128)} async-done(((f32[512,128]{1,0:T(8,128)}), f32[16,128]{1,0:T(8,128)}) %reduce-scatter.2.cloned.1.call-update) | async-done | bytes 8208 | tf_op jit(solution)/shard_map/reduce_scatter | solution.py:201
  (131 shorter events, 47.2 us)
Async XLA Ops:
  7.2 192.0 %copy-start = (f32[256]{0:T(256)S(1)}, f32[256]{0:T(256)}, u32[]{:S(2)}) copy-start(f32[256]{0:T(256)} %param.23) | copy-start | bytes 3076
  7.2 97.8 %all-gather.7.cloned.1.call-start = ((), (), s32[]{:S(2)}) async-start(), calls=%async_computation.2 | async-start | bytes 2949120 | tf_op jit(solution)/shard_map/all_gather | solution.py:148
  12.4 22.2 %copy-start.12 = (f32[64,8,128]{2,1,0:T(8,128)}, f32[64,8,128]{2,1,0:T(8,128)S(1)}, u32[]{:S(2)}) copy-start(f32[64,8,128]{2,1,0:T(8,128)S(1)} %get-tuple-element.3) | copy-start | bytes 786436
  12.7 14.3 %collective-permute-start.2 = (f32[5,64,3,128]{3,1,2,0:T(8,128)S(1)}, f32[5,64,3,128]{3,1,2,0:T(8,128)S(1)}, u32[]{:S(2)}, u32[]{:S(2)}) collective-permute-start(f32[5,64,3,128]{3,1,2,0:T(8,128)S(1)} %copy.18), channel_id=1, source_target_pairs={{1,0},{2,1},{3,2},{4,3},{5,4},{6,5},{7,6},{0,7},{9,8},{10,9},{11,1... | collective-permute-start | bytes 1474568 | tf_op jit(solution)/shard_map/ppermute | solution.py:31
  17.3 12.6 %collective-permute-start.3 = (f32[5,64,3,128]{3,1,2,0:T(8,128)S(1)}, f32[5,64,3,128]{3,1,2,0:T(8,128)S(1)}, u32[]{:S(2)}, u32[]{:S(2)}) collective-permute-start(f32[5,64,3,128]{3,1,2,0:T(8,128)S(1)} %copy.20), channel_id=1, source_target_pairs={{0,1},{1,2},{2,3},{3,4},{4,5},{5,6},{6,7},{7,0},{8,9},{9,10},{10,1... | collective-permute-start | bytes 1474568 | tf_op jit(solution)/shard_map/ppermute | solution.py:29
  34.6 197.3 %all-gather.9.cloned.1.call-start = ((), (), s32[]{:S(2)}) async-start(), calls=%async_computation.3 | async-start | bytes 2949120 | tf_op jit(solution)/shard_map/all_gather | solution.py:148
  38.0 9.7 %collective-permute-start = (f32[5,64,8,3]{1,2,3,0:T(8,128)S(1)}, f32[5,64,8,3]{1,2,3,0:T(8,128)S(1)}, u32[]{:S(2)}, u32[]{:S(2)}) collective-permute-start(f32[5,64,8,3]{1,2,3,0:T(8,128)S(1)} %copy.14), channel_id=1, source_target_pairs={{8,0},{16,8},{24,16},{9,1},{17,9},{25,17},{10,2},{18,10},{26,18},{... | collective-permute-start | bytes 92168 | tf_op jit(solution)/shard_map/ppermute | solution.py:31
  40.3 8.9 %collective-permute-start.1 = (f32[5,64,8,3]{1,2,3,0:T(8,128)}, f32[5,64,8,3]{1,2,3,0:T(8,128)S(1)}, u32[]{:S(2)}, u32[]{:S(2)}) collective-permute-start(f32[5,64,8,3]{1,2,3,0:T(8,128)} %copy.16), channel_id=1, source_target_pairs={{0,8},{8,16},{16,24},{1,9},{9,17},{17,25},{2,10},{10,18},{18,26},{... | collective-permute-start | bytes 92168 | tf_op jit(solution)/shard_map/ppermute | solution.py:29
  105.1 5.8 %copy-start.19 = (f32[5,64,8,128]{3,2,1,0:T(8,128)S(1)}, f32[5,64,8,128]{3,2,1,0:T(8,128)}, u32[]{:S(2)}) copy-start(f32[5,64,8,128]{3,2,1,0:T(8,128)} %param.18) | copy-start | bytes 3932164
  105.1 5.8 %copy-start.22 = (f32[5,64,8,128]{3,2,1,0:T(8,128)S(1)}, f32[5,64,8,128]{3,2,1,0:T(8,128)}, u32[]{:S(2)}) copy-start(f32[5,64,8,128]{3,2,1,0:T(8,128)} %fusion.11) | copy-start | bytes 3932164
  107.1 3.8 copy-start.3
  107.1 3.8 copy-start.5
  107.1 3.8 copy-start.10
  107.1 3.8 copy-start.13
  107.2 3.8 copy-start.15
  107.2 3.8 copy-start.21
  116.0 6.3 %collective-permute-start.4 = (f32[5,64,8,3]{1,2,3,0:T(8,128)S(1)}, f32[5,64,8,3]{1,2,3,0:T(8,128)S(1)}, u32[]{:S(2)}, u32[]{:S(2)}) collective-permute-start(f32[5,64,8,3]{1,2,3,0:T(8,128)S(1)} %copy.22), channel_id=1, source_target_pairs={{8,0},{16,8},{24,16},{9,1},{17,9},{25,17},{10,2},{18,10},{26,18},{... | collective-permute-start | bytes 92168 | tf_op jit(solution)/shard_map/ppermute | solution.py:31
  117.7 6.4 %collective-permute-start.5 = (f32[5,64,8,3]{1,2,3,0:T(8,128)S(1)}, f32[5,64,8,3]{1,2,3,0:T(8,128)S(1)}, u32[]{:S(2)}, u32[]{:S(2)}) collective-permute-start(f32[5,64,8,3]{1,2,3,0:T(8,128)S(1)} %copy.24), channel_id=1, source_target_pairs={{0,8},{8,16},{16,24},{1,9},{9,17},{17,25},{2,10},{10,18},{18,26},{... | collective-permute-start | bytes 92168 | tf_op jit(solution)/shard_map/ppermute | solution.py:29
  180.1 11.6 %collective-permute-start.6 = (f32[5,64,3,128]{3,1,2,0:T(8,128)S(1)}, f32[5,64,3,128]{3,1,2,0:T(8,128)S(1)}, u32[]{:S(2)}, u32[]{:S(2)}) collective-permute-start(f32[5,64,3,128]{3,1,2,0:T(8,128)S(1)} %copy.26), channel_id=1, source_target_pairs={{1,0},{2,1},{3,2},{4,3},{5,4},{6,5},{7,6},{0,7},{9,8},{10,9},{11,1... | collective-permute-start | bytes 1474568 | tf_op jit(solution)/shard_map/ppermute | solution.py:31
  180.2 13.6 %collective-permute-start.7 = (f32[5,64,3,128]{3,1,2,0:T(8,128)S(1)}, f32[5,64,3,128]{3,1,2,0:T(8,128)S(1)}, u32[]{:S(2)}, u32[]{:S(2)}) collective-permute-start(f32[5,64,3,128]{3,1,2,0:T(8,128)S(1)} %copy.28), channel_id=1, source_target_pairs={{0,1},{1,2},{2,3},{3,4},{4,5},{5,6},{6,7},{7,0},{8,9},{9,10},{10,1... | collective-permute-start | bytes 1474568 | tf_op jit(solution)/shard_map/ppermute | solution.py:29
  198.3 3.3 copy-start.16
  198.3 3.3 copy-start.17
  199.1 194.9 %reduce-scatter.2.cloned.1.call-start = ((), (), s32[]{:S(2)}) async-start(), calls=%async_computation.1 | async-start | bytes 270336 | tf_op jit(solution)/shard_map/reduce_scatter | solution.py:201
  238.9 155.2 %copy-start.11 = (f32[5,64,8,128]{3,2,1,0:T(8,128)}, f32[5,64,8,128]{3,2,1,0:T(8,128)S(1)}, u32[]{:S(2)}) copy-start(f32[5,64,8,128]{3,2,1,0:T(8,128)S(1)} %fusion.9) | copy-start | bytes 3932164
  (10 other events, 21.4 us)
Sparse Core Ops, SparseCore 0:
  34.7 33.0 all-gather.6
  199.3 32.5 all-gather.8
  261.6 132.3 reduce-scatter.1
where the time goes:
time: 407 us; the launch traced here: 401 us
  waiting for transfers between devices  188 us (46%)
  matrix products  93.5 us (23%)
  other arithmetic  45.1 us (11%)
  local copies, waits for them, and re-layouts  23.2 us (6%)
  blocking collectives  19.2 us (5%)
  starting transfers between devices  17.2 us (4%)
  between operations  14.7 us (4%)
    reduce_scatter x1, waiting for transfers between devices, per_device(): lax.psum_scatter(partial_signals, ('axial', 'azim'), scatter_dimension=0,...  133 us
    dot_general x2, matrix products, open_line(): jnp.einsum('vraj,j->vra', rhs, signed_power(base, offsets), precision=HIG...  35.2 us
    dot_general x2, matrix products, open_line(): jnp.einsum('vraj,j->vra', rhs, signed_power(base, width_here - 1 - offset...  34.6 us
    all_gather x2, waiting for transfers between devices, cycle_line(): piece = lax.all_gather(moments, 'azim', axis=0, tiled=True)  30.2 us
    scatter-add x1, other arithmetic, per_device(): jax.ops.segment_sum(values, bucket, num_segments=OBSERVERS * TIME_BINS)  22.6 us
    ppermute x4, waiting for transfers between devices, padded(): lax.ppermute(head, axis, [((i + 1) % count, i) for i in range(ends)])  20.6 us
    all_gather x2, blocking collectives, open_line(): piece = lax.all_gather(moments, 'axial', axis=0, tiled=True)  19.2 us
    ppermute x4, starting transfers between devices, padded(): lax.ppermute(tail, axis, [(i, (i + 1) % count) for i in range(ends)])  9.9 us
  transfers between devices with their start and end apart: 11, of which 7 were waited for; matrix products, arithmetic and copies ran while one was open for 15% of the time, Pallas kernels for 0%

commit v1 on v0

v1 whole, which is shorter than its diff:
```python
import functools
import math

import jax
import jax.numpy as jnp
import numpy as np
from jax import lax
from jax.experimental import pallas as pl
from jax.experimental.pallas import tpu as pltpu
from jax.sharding import PartitionSpec as P

OBSERVERS = 512
TIME_BINS = 128

GAMMA = 1.4
SECTION = 0.25
DERIV_ALPHA = 1.0 / 3.0
FILTER_ALPHA = 0.499
FIELDS = 5
CHUNK = 16
BASIS = 8
VMEM_LIMIT = 48 * 1024 * 1024


def decay_root(alpha):
    return (-1.0 + math.sqrt(1.0 - 4.0 * alpha * alpha)) / (2.0 * alpha)


DERIV_ROOT = decay_root(DERIV_ALPHA)
FILTER_ROOT = decay_root(FILTER_ALPHA)

DERIV_NEAR = 1.0 / 12.0
DERIV_FAR = (
    (25.0 / 36.0) * (DERIV_ROOT - 1.0 / DERIV_ROOT) / (1.0 + 2.0 * DERIV_ALPHA * DERIV_ROOT)
)

_B = FILTER_ALPHA
_EDGE = (1.0 - 2.0 * _B) / 64.0
_Q2 = 1.0 / _B
_Q1 = (-6.0 - _Q2) / _B
_Q0 = (12.0 - _Q1) / _B
_RHO = -8.0 - _Q0
FILTER_MID = _EDGE * (_Q0 + 2.0 * _Q2)
FILTER_ONE = _EDGE * _Q1
FILTER_TWO = _EDGE * _Q2
FILTER_FAR = _EDGE * _RHO / (1.0 + 2.0 * _B * FILTER_ROOT)


def open_operator(length, alpha, side):
    base = decay_root(alpha)
    tri = np.eye(length) + alpha * (np.eye(length, k=1) + np.eye(length, k=-1))
    tri[0, 0] = -alpha / base
    return np.linalg.solve(tri, side)


def deriv_matrix(length):
    return (7.0 / 9.0) * (np.eye(length, k=1) - np.eye(length, k=-1)) + (1.0 / 36.0) * (
        np.eye(length, k=2) - np.eye(length, k=-2)
    )


def filter_matrix(length):
    beta = FILTER_ALPHA
    coeffs = [
        (11.0 + 10.0 * beta) / 16.0,
        (15.0 + 34.0 * beta) / 32.0,
        (-3.0 + 6.0 * beta) / 16.0,
        (1.0 - 2.0 * beta) / 32.0,
    ]
    total = coeffs[0] * np.eye(length)
    for shift in range(1, 4):
        total = total + 0.5 * coeffs[shift] * (np.eye(length, k=shift) + np.eye(length, k=-shift))
    return total


def axial_tables(count, width, alpha, kind):
    length = count * width
    side = deriv_matrix(length) if kind == "deriv" else filter_matrix(length)
    whole = open_operator(length, alpha, side)
    base = decay_root(alpha)
    basis = np.zeros((BASIS, width))
    for edge in range(3):
        basis[edge, edge] = 1.0
        basis[3 + edge, width - 3 + edge] = 1.0
    basis[6] = base ** np.arange(width - 1, -1, -1, dtype=np.float64)
    basis[7] = base ** np.arange(width, dtype=np.float64)
    inverse = np.linalg.pinv(basis)
    own = np.zeros((count, width, width))
    far = np.zeros((count, max(count - 1, 1) * BASIS, width))
    for here in range(count):
        rows = whole[here * width : (here + 1) * width]
        own[here] = rows[:, here * width : (here + 1) * width].T
        if kind == "filter":
            own[here] -= np.eye(width)
        for shift in range(1, count):
            there = (here - shift) % count
            block = rows[:, there * width : (there + 1) * width]
            far[here, (shift - 1) * BASIS : shift * BASIS] = (block @ inverse).T
    return own, basis, far


def halves(table):
    high = np.asarray(table, np.float32).astype(jnp.bfloat16)
    low = (np.asarray(table, np.float64) - high.astype(np.float64)).astype(jnp.bfloat16)
    return np.stack([high, low], axis=-3)


def split(values):
    high = values.astype(jnp.bfloat16)
    return high, (values - high.astype(jnp.float32)).astype(jnp.bfloat16)


def dots(left, right, dims):
    out = None
    for a, b in ((0, 0), (1, 0), (0, 1)):
        part = lax.dot_general(
            left[a], right[b], (dims, ((), ())), preferred_element_type=jnp.float32
        )
        out = part if out is None else out + part
    return out


def outgoing(basis_ref, lines):
    return dots((basis_ref[0], basis_ref[1]), split(lines), ((1,), (1,)))


def incoming(parts, far_ref):
    return dots(split(jnp.concatenate(parts, axis=0)), (far_ref[0], far_ref[1]), ((0,), (0,)))


def own_block(lines, own_ref):
    return dots(split(lines), (own_ref[0], own_ref[1]), ((1,), (0,)))


def tile_state(density, velocity, pressure):
    energy = pressure * (1.0 / (GAMMA - 1.0)) + 0.5 * density * (
        velocity[0] * velocity[0] + velocity[1] * velocity[1] + velocity[2] * velocity[2]
    )
    return energy


def tile_flux(density, velocity, pressure, energy, metric, volume):
    contra = metric[0] * velocity[0] + metric[1] * velocity[1] + metric[2] * velocity[2]
    volume_contra = volume * contra
    mass = density * volume_contra
    push = volume * pressure
    pieces = [mass]
    for comp in range(3):
        pieces.append(mass * velocity[comp] + metric[comp] * push)
    pieces.append((energy + pressure) * volume_contra)
    return pieces


def flux_send_kernel(
    core_ref, density, velocity, pressure, axial_metric, azim_metric, volume, basis, edge, pair, odd, flux
):
    rows = density.shape[1]
    first_core = core_ref[0] == 0
    head = [None] * FIELDS
    tail = [None] * FIELDS
    for row in range(rows):
        rho = density[:, row, :]
        vel = [velocity[c, :, row, :] for c in range(3)]
        pres = pressure[:, row, :]
        vol = volume[:, row, :]
        energy = tile_state(rho, vel, pres)
        axial = tile_flux(rho, vel, pres, energy, [axial_metric[c, :, row, :] for c in range(3)], vol)
        azim = tile_flux(rho, vel, pres, energy, [azim_metric[c, :, row, :] for c in range(3)], vol)
        for f in range(FIELDS):
            flux[f, row] = axial[f]
            if row == 0:
                head[f] = azim[f]
                tail[f] = azim[f]
                start = azim[f]
                pair[0, 2, f] = start
                odd[0, f] = start
            else:
                head[f] = azim[f] + DERIV_ROOT * head[f]
                tail[f] = tail[f] + (DERIV_ROOT**row) * azim[f]
            if row == rows - 1:
                start = pair[0, 2, f]
                pair[0, 2, f] = jnp.where(first_core, azim[f], start)
                odd[0, f] = jnp.where(first_core, start, azim[f])
    for f in range(FIELDS):
        pair[0, 0, f] = head[f]
        pair[0, 1, f] = tail[f]
    edge[...] = outgoing(basis, flux[...].reshape(-1, flux.shape[-1]))


def section_local_kernel(
    density,
    velocity,
    pressure,
    axial_metric,
    azim_metric,
    volume,
    radial,
    own,
    base_out,
    scale_out,
    axial_flux,
    azim_flux,
):
    rows = density.shape[1]
    lanes = density.shape[2]
    for row in range(rows):
        rho = density[:, row, :]
        vel = [velocity[c, :, row, :] for c in range(3)]
        pres = pressure[:, row, :]
        vol = volume[:, row, :]
        energy = tile_state(rho, vel, pres)
        axial = tile_flux(rho, vel, pres, energy, [axial_metric[c, :, row, :] for c in range(3)], vol)
        azim = tile_flux(rho, vel, pres, energy, [azim_metric[c, :, row, :] for c in range(3)], vol)
        state = [rho, rho * vel[0], rho * vel[1], rho * vel[2], energy]
        scale_out[0, row] = SECTION / vol
        for f in range(FIELDS):
            axial_flux[f, row] = axial[f]
            azim_flux[f, row] = azim[f]
            base_out[0, f, row] = state[f] + SECTION * radial[f, :, row, :]
    deriv = own_block(axial_flux[...].reshape(-1, lanes), own)
    axial_flux[...] = deriv.reshape(axial_flux.shape)
    for f in range(FIELDS):
        down = [None] * rows
        down[rows - 1] = azim_flux[f, rows - 1]
        for row in range(rows - 2, -1, -1):
            down[row] = azim_flux[f, row] + DERIV_ROOT * down[row + 1]
        up = None
        for row in range(rows):
            here = azim_flux[f, row]
            up = here if row == 0 else here + DERIV_ROOT * up
            total = axial_flux[f, row] + DERIV_FAR * (up - down[row])
            if row > 0:
                total = total - DERIV_NEAR * azim_flux[f, row - 1]
            if row < rows - 1:
                total = total + DERIV_NEAR * azim_flux[f, row + 1]
            base_out[0, f, row] = base_out[0, f, row] - scale_out[0, row] * total


def pick(core, zero, one):
    return jnp.where(core == 0, jnp.float32(zero), jnp.float32(one))


def ring_sums(core, mine, chunk, own_sums, sib_sums, sib_pair, root, rows):
    half = own_sums.shape[0]
    local = lax.rem(chunk, half)
    left = jnp.where(mine, own_sums[local, 0], sib_sums[local, 0])
    right = jnp.where(mine, own_sums[local, 1], sib_sums[local, 1])
    decay = root**rows
    left = pick(core, 1.0, decay) * left + pick(core, 0.0, 1.0) * sib_pair[0, 0]
    right = pick(core, decay, 1.0) * right + pick(core, 1.0, 0.0) * sib_pair[0, 1]
    return left, right


def section_join_kernel(
    count, core_ref, base, scale, own_sums, sib_sums, sib_pair, odd, far, basis, *rest
):
    edges, (out, edge_out) = rest[:count], rest[count:]
    rows = scale.shape[1]
    lanes = scale.shape[3]
    core = core_ref[0]
    chunk = pl.program_id(0)
    mine = (chunk // own_sums.shape[0]) == core
    left, right = ring_sums(core, mine, chunk, own_sums, sib_sums, sib_pair, DERIV_ROOT, rows)
    facing = sib_pair[0, 2]
    before = jnp.where(core == 0, odd[0], facing)
    after = jnp.where(core == 0, facing, odd[0])
    if count:
        axial = incoming([ref[...] for ref in edges], far).reshape(out.shape[1:])
    else:
        axial = jnp.zeros(out.shape[1:], jnp.float32)
    for row in range(rows):
        azim = (DERIV_FAR * DERIV_ROOT ** (row + 1)) * left - (
            DERIV_FAR * DERIV_ROOT ** (rows - row)
        ) * right
        if row == 0:
            azim = azim - DERIV_NEAR * before
        if row == rows - 1:
            azim = azim + DERIV_NEAR * after
        out[0, :, row] = base[0, :, row] - scale[0, row][None] * (axial[:, row] + azim)
    edge_out[...] = outgoing(basis, out[0].reshape(-1, lanes))


def axial_local_kernel(values, own, out):
    lines = values[0].reshape(-1, values.shape[-1])
    out[0] = (lines + own_block(lines, own)).reshape(out.shape[1:])


def axial_join_kernel(count, core_ref, local, far, *rest):
    edges, (out, pair, odd) = rest[:count], rest[count:]
    rows = local.shape[2]
    core = core_ref[0]
    if count:
        out[0] = local[0] + incoming([ref[...] for ref in edges], far).reshape(out.shape[1:])
    else:
        out[0] = local[0]
    first = core == 0
    for f in range(FIELDS):
        head = out[0, f, 0]
        tail = out[0, f, 0]
        for row in range(1, rows):
            head = out[0, f, row] + FILTER_ROOT * head
            tail = tail + (FILTER_ROOT**row) * out[0, f, row]
        pair[0, 0, f] = head
        pair[0, 1, f] = tail
        for near in range(2):
            low, high = out[0, f, near], out[0, f, rows - 2 + near]
            pair[0, 2 + near, f] = jnp.where(first, high, low)
            odd[0, near, f] = jnp.where(first, low, high)


def azim_local_kernel(values, out):
    rows = values.shape[2]
    for f in range(FIELDS):
        down = [None] * rows
        down[rows - 1] = values[0, f, rows - 1]
        for row in range(rows - 2, -1, -1):
            down[row] = values[0, f, row] + FILTER_ROOT * down[row + 1]
        up = None
        for row in range(rows):
            here = values[0, f, row]
            up = here if row == 0 else here + FILTER_ROOT * up
            total = (1.0 + FILTER_MID - FILTER_FAR) * here + FILTER_FAR * (up + down[row])
            for step, weight in ((1, FILTER_ONE), (2, FILTER_TWO)):
                if row >= step:
                    total = total + weight * values[0, f, row - step]
                if row + step < rows:
                    total = total + weight * values[0, f, row + step]
            out[0, f, row] = total


def azim_join_kernel(core_ref, local, own_sums, sib_sums, sib_pair, odd, out, surface):
    rows = local.shape[2]
    core = core_ref[0]
    chunk = pl.program_id(0)
    mine = (chunk // own_sums.shape[0]) == core
    left, right = ring_sums(core, mine, chunk, own_sums, sib_sums, sib_pair, FILTER_ROOT, rows)
    for row in range(rows):
        total = (
            local[0, :, row]
            + (FILTER_FAR * FILTER_ROOT ** (row + 1)) * left
            + (FILTER_FAR * FILTER_ROOT ** (rows - row)) * right
        )
        if row < 2:
            before = [jnp.where(core == 0, odd[0, n], sib_pair[0, 2 + n]) for n in range(2)]
            total = total + FILTER_TWO * before[row]
            if row == 0:
                total = total + FILTER_ONE * before[1]
        if row >= rows - 2:
            after = [jnp.where(core == 0, sib_pair[0, 2 + n], odd[0, n]) for n in range(2)]
            total = total + FILTER_TWO * after[row - (rows - 2)]
            if row == rows - 1:
                total = total + FILTER_ONE * after[0]
        out[:, :, row, :] = total

    @pl.when(chunk == 0)
    def _():
        surface[...] = out[2, 0] + out[0, 0] - 1.0


def weights_kernel(table, ids, area, out):
    entries = ids.shape[0]
    for entry in range(entries):
        chosen = ids[entry]
        found = jnp.zeros(chosen.shape, jnp.float32)
        for t in range(table.shape[0]):
            found = jnp.where(chosen == t, table[t], found)
        out[entry] = found * area[...]


def signals_kernel(weights, surface, observers, bins, out):
    entries, rows, lanes = weights.shape
    observer_rows = lax.broadcasted_iota(jnp.int32, (out.shape[0], lanes), 0)
    bin_rows = lax.broadcasted_iota(jnp.int32, (out.shape[1], lanes), 0)
    out[...] = jnp.zeros_like(out)
    for row in range(rows):
        left, right = [], []
        for entry in range(entries):
            value = weights[entry, row : row + 1, :] * surface[row : row + 1, :]
            hit = observer_rows == observers[entry, row : row + 1, :]
            left.append(jnp.where(hit, 1.0, 0.0).astype(jnp.bfloat16))
            right.append(jnp.where(bin_rows == bins[entry, row : row + 1, :], value, 0.0))
        one_hot = jnp.concatenate(left, axis=1)
        high, low = split(jnp.concatenate(right, axis=1))
        for part in (high, low):
            out[...] += lax.dot_general(
                one_hot, part, (((1,), (1,)), ((), ())), preferred_element_type=jnp.float32
            )


def params():
    return pltpu.CompilerParams(vmem_limit_bytes=VMEM_LIMIT)


def cost(flops, moved):
    return pl.CostEstimate(flops=int(flops), bytes_accessed=int(moved), transcendentals=0)


def rotate(values, axis, count, shift):
    return lax.ppermute(values, axis, [(i, (i + shift) % count) for i in range(count)])


def azim_exchange(pair, odd, core, count, root, rows):
    sib = lax.ppermute(pair, "azim", [(i, i ^ 1) for i in range(count)])
    odd_in = lax.ppermute(
        odd, "azim", [(i, (i + 1) % count if i % 2 else (i - 1) % count) for i in range(count)]
    )
    chips = count // 2
    half = pair.shape[0] // 2
    decay = root**rows
    mine = lax.dynamic_slice_in_dim(pair[:, :2], core * half, half, axis=0)
    other = lax.dynamic_slice_in_dim(sib[:, :2], core * half, half, axis=0)
    first = core == 0
    low = jnp.where(first, mine, other)
    high = jnp.where(first, other, mine)
    chip = jnp.stack([high[:, 0] + decay * low[:, 0], low[:, 1] + decay * high[:, 1]], axis=1)
    wide = root ** (2 * rows)
    close = 1.0 / (1.0 - root ** (rows * count))
    left = wide ** (chips - 1) * chip[:, 0]
    right = wide ** (chips - 1) * chip[:, 1]
    for shift in range(1, chips):
        there = rotate(chip, "azim", count, 2 * shift)
        left = left + wide ** (shift - 1) * there[:, 0]
        right = right + wide ** (chips - shift - 1) * there[:, 1]
    sums = close * jnp.stack([left, right], axis=1)
    sib_sums = lax.ppermute(sums, "azim", [(i, i ^ 1) for i in range(count)])
    return sib, odd_in, sums, sib_sums


def per_device(
    density,
    velocity,
    pressure,
    axial_metric,
    azim_metric,
    volume,
    radial_term,
    panel_area,
    observer_ids,
    bin_ids,
    weight_ids,
    bin_weights,
):
    planes, rows, lanes = density.shape
    along = lax.axis_size("axial")
    around = lax.axis_size("azim")
    steps = planes // CHUNK
    lines = FIELDS * rows * CHUNK
    place = lax.axis_index("axial")
    core = lax.axis_index("azim") % 2
    core_ref = core.astype(jnp.int32).reshape(1)
    f32 = jnp.float32

    tables = {}
    for kind, alpha in (("deriv", DERIV_ALPHA), ("filter", FILTER_ALPHA)):
        own, basis, far = axial_tables(along, lanes, alpha, kind)
        tables[kind] = (
            jnp.asarray(halves(own))[place],
            jnp.asarray(halves(basis)),
            jnp.asarray(halves(far))[place],
        )

    smem = pl.BlockSpec(memory_space=pltpu.SMEM)
    field = pl.BlockSpec((CHUNK, rows, lanes), lambda k: (k, 0, 0))
    vector = pl.BlockSpec((3, CHUNK, rows, lanes), lambda k: (0, k, 0, 0))
    wide_in = pl.BlockSpec((FIELDS, CHUNK, rows, lanes), lambda k: (0, k, 0, 0))
    inner = pl.BlockSpec((1, FIELDS, rows, CHUNK, lanes), lambda k: (k, 0, 0, 0, 0))
    inner_one = pl.BlockSpec((1, rows, CHUNK, lanes), lambda k: (k, 0, 0, 0))
    edge = pl.BlockSpec((BASIS, lines), lambda k: (0, k))

    def fixed(shape):
        return pl.BlockSpec(shape, lambda k: (0,) * len(shape))

    def packed(*lead):
        return pl.BlockSpec(
            (1,) + lead + (FIELDS, CHUNK, lanes), lambda k: (k,) + (0,) * (len(lead) + 3)
        )

    def packed_shape(*lead):
        return jax.ShapeDtypeStruct((steps,) + lead + (FIELDS, CHUNK, lanes), f32)

    inner_shape = jax.ShapeDtypeStruct((steps, FIELDS, rows, CHUNK, lanes), f32)
    one_shape = jax.ShapeDtypeStruct((steps, rows, CHUNK, lanes), f32)
    edge_shape = jax.ShapeDtypeStruct((BASIS, steps * lines), f32)
    flux_scratch = pltpu.VMEM((FIELDS, rows, CHUNK, lanes), f32)
    block = planes * rows * lanes
    sums_shape = (steps // 2, 2, FIELDS, CHUNK, lanes)

    own_d, basis_d, far_d = tables["deriv"]
    own_f, basis_f, far_f = tables["filter"]

    edge_d, pair_d, odd_d = pl.pallas_call(
        flux_send_kernel,
        grid=(steps,),
        in_specs=[smem, field, vector, field, vector, vector, field, fixed(basis_d.shape)],
        out_specs=[edge, packed(3), packed()],
        out_shape=[edge_shape, packed_shape(3), packed_shape()],
        scratch_shapes=[flux_scratch],
        compiler_params=params(),
        cost_estimate=cost(200 * block, 52 * block),
        name="flux_send",
    )(core_ref, density, velocity, pressure, axial_metric, azim_metric, volume, basis_d)

    weights = pl.pallas_call(
        weights_kernel,
        in_specs=[smem] + [pl.BlockSpec(memory_space=pltpu.VMEM)] * 2,
        out_specs=pl.BlockSpec(memory_space=pltpu.VMEM),
        out_shape=jax.ShapeDtypeStruct(weight_ids.shape, f32),
        compiler_params=params(),
        name="entry_weights",
    )(bin_weights, weight_ids, panel_area)

    edges_d = [rotate(edge_d, "axial", along, s) for s in range(1, along)]
    sib_d, odd_d, sums_d, sib_sums_d = azim_exchange(pair_d, odd_d, core, around, DERIV_ROOT, rows)

    base, scale = pl.pallas_call(
        section_local_kernel,
        grid=(steps,),
        in_specs=[field, vector, field, vector, vector, field, wide_in, fixed(own_d.shape)],
        out_specs=[inner, inner_one],
        out_shape=[inner_shape, one_shape],
        scratch_shapes=[flux_scratch, flux_scratch],
        compiler_params=params(),
        cost_estimate=cost(4000 * block, 100 * block),
        name="section_local",
    )(density, velocity, pressure, axial_metric, azim_metric, volume, radial_term, own_d)

    sectioned, edge_f = pl.pallas_call(
        functools.partial(section_join_kernel, along - 1),
        grid=(steps,),
        in_specs=[
            smem,
            inner,
            inner_one,
            fixed(sums_shape),
            fixed(sums_shape),
            packed(3),
            packed(),
            fixed(far_d.shape),
            fixed(basis_f.shape),
        ]
        + [edge] * (along - 1),
        out_specs=[inner, edge],
        out_shape=[inner_shape, edge_shape],
        compiler_params=params(),
        cost_estimate=cost(500 * block, 48 * block),
        name="section_join",
    )(core_ref, base, scale, sums_d, sib_sums_d, sib_d, odd_d, far_d, basis_f, *edges_d)

    edges_f = [rotate(edge_f, "axial", along, s) for s in range(1, along)]

    axial_local = pl.pallas_call(
        axial_local_kernel,
        grid=(steps,),
        in_specs=[inner, fixed(own_f.shape)],
        out_specs=inner,
        out_shape=inner_shape,
        compiler_params=params(),
        cost_estimate=cost(4000 * block, 40 * block),
        name="axial_local",
    )(sectioned, own_f)

    smoothed, pair_f, odd_f = pl.pallas_call(
        functools.partial(axial_join_kernel, along - 1),
        grid=(steps,),
        in_specs=[smem, inner, fixed(far_f.shape)] + [edge] * (along - 1),
        out_specs=[inner, packed(4), packed(2)],
        out_shape=[inner_shape, packed_shape(4), packed_shape(2)],
        compiler_params=params(),
        cost_estimate=cost(500 * block, 48 * block),
        name="axial_join",
    )(core_ref, axial_local, far_f, *edges_f)

    sib_f, odd_f, sums_f, sib_sums_f = azim_exchange(pair_f, odd_f, core, around, FILTER_ROOT, rows)

    azim_local = pl.pallas_call(
        azim_local_kernel,
        grid=(steps,),
        in_specs=[inner],
        out_specs=inner,
        out_shape=inner_shape,
        compiler_params=params(),
        cost_estimate=cost(100 * block, 40 * block),
        name="azim_local",
    )(smoothed)

    new_state, surface = pl.pallas_call(
        azim_join_kernel,
        grid=(steps,),
        in_specs=[smem, inner, fixed(sums_shape), fixed(sums_shape), packed(4), packed(2)],
        out_specs=[wide_in, fixed((rows, lanes))],
        out_shape=[
            jax.ShapeDtypeStruct((FIELDS, planes, rows, lanes), f32),
            jax.ShapeDtypeStruct((rows, lanes), f32),
        ],
        compiler_params=params(),
        cost_estimate=cost(100 * block, 48 * block),
        name="azim_join",
    )(core_ref, azim_local, sums_f, sib_sums_f, sib_f, odd_f)

    partial = pl.pallas_call(
        signals_kernel,
        out_shape=jax.ShapeDtypeStruct((OBSERVERS, TIME_BINS), f32),
        compiler_params=params(),
        name="signals",
    )(weights, surface, observer_ids, bin_ids)
    devices = along * around
    shares = lax.all_to_all(
        partial.reshape(devices, OBSERVERS // devices, TIME_BINS),
        ("axial", "azim"),
        0,
        0,
        tiled=True,
    )
    return (new_state, jnp.sum(shares, axis=0))


def solution(mesh):
    placed = (
        P(None, "azim", "axial"),
        P(None, None, "azim", "axial"),
        P(None, "azim", "axial"),
        P(None, None, "azim", "axial"),
        P(None, None, "azim", "axial"),
        P(None, "azim", "axial"),
        P(None, None, "azim", "axial"),
        P("azim", "axial"),
        P(None, "azim", "axial"),
        P(None, "azim", "axial"),
        P(None, "azim", "axial"),
        P(),
    )
    return jax.shard_map(
        per_device,
        mesh=mesh,
        in_specs=placed,
        out_specs=(P(None, None, "azim", "axial"), P(("axial", "azim"), None)),
        check_vma=False,
    )
```

time: 407 us -> 115 us (0.28); the launches traced: 401 us -> 114 us
  waiting for transfers between devices: 188 us -> 24.2 us
  matrix products: 93.5 us -> 0 us
  other arithmetic: 45.1 us -> 3.82 us
  Pallas kernels: 0 us -> 30.4 us
  between operations: 14.7 us -> 1.02 us
  local copies, waits for them, and re-layouts: 23.2 us -> 13.9 us
  starting transfers between devices: 17.2 us -> 25.2 us
    reduce_scatter x1 -> x0, waiting for transfers between devices: 133 us -> none  [per_device(): lax.psum_scatter(partial_signals, ('axial', 'azim'), scatter_dimension=0,...]
    dot_general x23 -> x0, matrix products: 93.5 us -> none  [the longest x2 35.2 us: open_line(): jnp.einsum('vraj,j->vra', rhs, signed_power(base, offsets), precision=HIG...]
    pallas_call x0 -> x9, Pallas kernels: none -> 30.4 us  [the longest x1 9.78 us: per_device(): pl.pallas_call(flux_send_kernel, grid=(steps,), in_specs=[smem, field, ve...]
    all_gather x2 -> x0, waiting for transfers between devices: 30.2 us -> none  [cycle_line(): piece = lax.all_gather(moments, 'azim', axis=0, tiled=True)]
    scatter-add x1 -> x0, other arithmetic: 22.6 us -> none  [per_device(): jax.ops.segment_sum(values, bucket, num_segments=OBSERVERS * TIME_BINS)]
    all_gather x2 -> x0, blocking collectives: 19.2 us -> none  [open_line(): piece = lax.all_gather(moments, 'axial', axis=0, tiled=True)]
    all_to_all x0 -> x1, blocking collectives: none -> 15.9 us  [per_device(): lax.all_to_all(partial.reshape(devices, OBSERVERS // devices, TIME_BINS),...]
    add x4, other arithmetic: 15.1 us -> 1.31 us  [the longest x2 1.26 us: azim_exchange(): left = left + wide ** (shift - 1) * there[:, 0]]
  transfers between devices with their start and end apart: 11 -> 18, of which waited for: 7 -> 8; matrix products, arithmetic and copies ran while one was open for 15% -> 5% of each run, Pallas kernels for 0% -> 10%
where the time goes in v1:
time: 115 us; the launch traced here: 114 us
  Pallas kernels  30.4 us (26%)
  starting transfers between devices  25.2 us (22%)
  waiting for transfers between devices  24.2 us (21%)
  blocking collectives  15.9 us (14%)
  local copies, waits for them, and re-layouts  13.9 us (12%)
  other arithmetic  3.82 us (3%)
    ppermute x12, starting transfers between devices, rotate(): lax.ppermute(values, axis, [(i, (i + shift) % count) for i in range(count)])  20.5 us
    ppermute x12, waiting for transfers between devices, rotate(): lax.ppermute(values, axis, [(i, (i + shift) % count) for i in range(count)])  17.9 us
    all_to_all x1, blocking collectives, per_device(): lax.all_to_all(partial.reshape(devices, OBSERVERS // devices, TIME_BINS),...  15.9 us
    unnamed x46, local copies, waits for them, and re-layouts  9.93 us
    pallas_call x1, Pallas kernels, per_device(): pl.pallas_call(flux_send_kernel, grid=(steps,), in_specs=[smem, field, ve...  9.78 us
    pallas_call x1, Pallas kernels, per_device(): pl.pallas_call(section_local_kernel, grid=(steps,), in_specs=[field, vect...  8.43 us
    ppermute x2, starting transfers between devices, azim_exchange(): lax.ppermute(odd, 'azim', [(i, (i + 1) % count if i % 2 else (i - 1) % co...  3.96 us
    ppermute x2, waiting for transfers between devices, azim_exchange(): lax.ppermute(odd, 'azim', [(i, (i + 1) % count if i % 2 else (i - 1) % co...  3.55 us
  transfers between devices with their start and end apart: 18, of which 8 were waited for; matrix products, arithmetic and copies ran while one was open for 5% of the time, Pallas kernels for 10%

profile of v1, /device:TPU:0, one launch (start us, length us, event | category | flops | bytes accessed | tf_op | source)
XLA Modules:
  0.0 114.4 jit_solution(9863591216484433708)
XLA Ops:
  7.6 9.8 %flux_send.1 = (f32[8,2560]{1,0:T(8,128)}, f32[4,3,5,16,128]{4,3,2,1,0:T(8,128)S(1)}, f32[4,5,16,128]{3,2,1,0:T(8,128)S(1)}) custom-call(s32[1]{0:T(128)} %bitcast.core_ref, f32[64,8,128]{2,1,0:T(8,128)S(1)} %copy-done.7, f32[3,64,8,128]{3,2,1,0:T(8,128)S(1)} %copy-done, f32[64,8,128]{2,1,0:T(8,128)S(1)} %copy-done.9, f32[3,64,8,128]{3,2,1,0:T(8,128)S(1)} %copy-done.2, ...), custom_call_target="tpu_custom_call" | custom-call | flops 13107200 | bytes 3407872 | tf_op jit(solution)/shard_map/flux_send/pallas_call | solution.py:491
  21.9 2.9 %collective-permute-start.1 = (f32[2,2,5,16,128]{4,3,2,1,0:T(8,128)}, f32[2,2,5,16,128]{4,3,2,1,0:T(8,128)}, u32[]{:S(2)}, u32[]{:S(2)}) collective-permute-start(f32[2,2,5,16,128]{4,3,2,1,0:T(8,128)} %pad_maximum_fusion), channel_id=1, source_target_pairs={{0,2},{1,3},{2,4},{3,5},{4,6},{5,7},{6,0},{7,1},{8,10},{9,11},{10,... | collective-permute-start | bytes 491528 | tf_op jit(solution)/shard_map/ppermute | solution.py:399
  24.9 2.6 %collective-permute-start.2 = (f32[2,2,5,16,128]{4,3,2,1,0:T(8,128)}, f32[2,2,5,16,128]{4,3,2,1,0:T(8,128)}, u32[]{:S(2)}, u32[]{:S(2)}) collective-permute-start(f32[2,2,5,16,128]{4,3,2,1,0:T(8,128)} %pad_maximum_fusion), channel_id=1, source_target_pairs={{0,4},{1,5},{2,6},{3,7},{4,0},{5,1},{6,2},{7,3},{8,12},{9,13},{10,... | collective-permute-start | bytes 491528 | tf_op jit(solution)/shard_map/ppermute | solution.py:399
  27.5 1.3 %collective-permute-start.3 = (f32[2,2,5,16,128]{4,3,2,1,0:T(8,128)}, f32[2,2,5,16,128]{4,3,2,1,0:T(8,128)}, u32[]{:S(2)}, u32[]{:S(2)}) collective-permute-start(f32[2,2,5,16,128]{4,3,2,1,0:T(8,128)} %pad_maximum_fusion), channel_id=1, source_target_pairs={{0,6},{1,7},{2,0},{3,1},{4,2},{5,3},{6,4},{7,5},{8,14},{9,15},{10,... | collective-permute-start | bytes 491528 | tf_op jit(solution)/shard_map/ppermute | solution.py:399
  28.8 1.5 %collective-permute-start.6 = (f32[8,2560]{1,0:T(8,128)}, f32[8,2560]{1,0:T(8,128)S(1)}, u32[]{:S(2)}, u32[]{:S(2)}) collective-permute-start(f32[8,2560]{1,0:T(8,128)} %get-tuple-element.18), channel_id=1, source_target_pairs={{0,8},{8,16},{16,24},{24,0},{1,9},{9,17},{17,25},{25,1},{2,10},{10... | collective-permute-start | bytes 245768 | tf_op jit(solution)/shard_map/ppermute | solution.py:399
  30.3 1.5 %collective-permute-start.7 = (f32[8,2560]{1,0:T(8,128)}, f32[8,2560]{1,0:T(8,128)S(1)}, u32[]{:S(2)}, u32[]{:S(2)}) collective-permute-start(f32[8,2560]{1,0:T(8,128)} %get-tuple-element.18), channel_id=1, source_target_pairs={{0,16},{8,24},{16,0},{24,8},{1,17},{9,25},{17,1},{25,9},{2,18},{10... | collective-permute-start | bytes 245768 | tf_op jit(solution)/shard_map/ppermute | solution.py:399
  32.7 2.3 %collective-permute-start.8 = (f32[8,2560]{1,0:T(8,128)}, f32[8,2560]{1,0:T(8,128)S(1)}, u32[]{:S(2)}, u32[]{:S(2)}) collective-permute-start(f32[8,2560]{1,0:T(8,128)} %get-tuple-element.18), channel_id=1, source_target_pairs={{0,24},{8,0},{16,8},{24,16},{1,25},{9,1},{17,9},{25,17},{2,26},{10... | collective-permute-start | bytes 245768 | tf_op jit(solution)/shard_map/ppermute | solution.py:399
  35.0 3.8 %collective-permute-done.2 = f32[2,2,5,16,128]{4,3,2,1,0:T(8,128)} collective-permute-done((f32[2,2,5,16,128]{4,3,2,1,0:T(8,128)}, f32[2,2,5,16,128]{4,3,2,1,0:T(8,128)}, u32[]{:S(2)}, u32[]{:S(2)}) %collective-permute-start.2) | collective-permute-done | bytes 163872 | tf_op jit(solution)/shard_map/ppermute | solution.py:399
  38.8 4.0 %collective-permute-start.5 = (f32[4,5,16,128]{3,2,1,0:T(8,128)}, f32[4,5,16,128]{3,2,1,0:T(8,128)S(1)}, u32[]{:S(2)}, u32[]{:S(2)}) collective-permute-start(f32[4,5,16,128]{3,2,1,0:T(8,128)} %copy-done.20), channel_id=1, source_target_pairs={{0,7},{1,2},{2,1},{3,4},{4,3},{5,6},{6,5},{7,0},{8,15},{9,10},{10,... | collective-permute-start | bytes 491528 | tf_op jit(solution)/shard_map/ppermute | solution.py:404
  47.3 8.4 %section_local.1 = (f32[4,5,8,16,128]{4,3,2,1,0:T(8,128)S(1)}, f32[4,8,16,128]{3,2,1,0:T(8,128)S(1)}) custom-call(f32[64,8,128]{2,1,0:T(8,128)S(1)} %copy-done.8, f32[3,64,8,128]{3,2,1,0:T(8,128)S(1)} %copy-done.1, f32[64,8,128]{2,1,0:T(8,128)S(1)} %copy-done.10, f32[3,64,8,128]{3,2,1,0:T(8,128)S(1)} %copy-done.3, f32[3,64,8,128]{3,2,1,0:T(8,128)S(1)} %copy-done.5, ...), custom_call_target="tpu_custom_call" | custom-call | flops 262144000 | bytes 6553600 | tf_op jit(solution)/shard_map/section_local/pallas_call | solution.py:515
  56.5 3.2 %section_join.1 = (f32[4,5,8,16,128]{4,3,2,1,0:T(8,128)S(1)}, f32[8,2560]{1,0:T(8,128)S(1)}) custom-call(s32[1]{0:T(128)} %bitcast.core_ref, f32[4,5,8,16,128]{4,3,2,1,0:T(8,128)S(1)} %get-tuple-element.14.base, f32[4,8,16,128]{3,2,1,0:T(8,128)S(1)} %get-tuple-element.15.scale, f32[2,2,5,16,128]{4,3,2,1,0:T(8,128)S(1)} %pad_maximum_fusion.1.own_sums, ...), custom_call_target="tpu_custom_call" | custom-call | flops 32768000 | bytes 3145728 | tf_op jit(solution)/shard_map/section_join/pallas_call | solution.py:527
  59.6 1.6 %collective-permute-start.10 = (f32[8,2560]{1,0:T(8,128)S(1)}, f32[8,2560]{1,0:T(8,128)S(1)}, u32[]{:S(2)}, u32[]{:S(2)}) collective-permute-start(f32[8,2560]{1,0:T(8,128)S(1)} %get-tuple-element.20), channel_id=1, source_target_pairs={{0,16},{8,24},{16,0},{24,8},{1,17},{9,25},{17,1},{25,9},{2,18},{10... | collective-permute-start | bytes 245768 | tf_op jit(solution)/shard_map/ppermute | solution.py:399
  61.2 1.4 %collective-permute-start.11 = (f32[8,2560]{1,0:T(8,128)S(1)}, f32[8,2560]{1,0:T(8,128)S(1)}, u32[]{:S(2)}, u32[]{:S(2)}) collective-permute-start(f32[8,2560]{1,0:T(8,128)S(1)} %get-tuple-element.20), channel_id=1, source_target_pairs={{0,24},{8,0},{16,8},{24,16},{1,25},{9,1},{17,9},{25,17},{2,26},{10... | collective-permute-start | bytes 245768 | tf_op jit(solution)/shard_map/ppermute | solution.py:399
  65.8 2.2 %collective-permute-done.9.rest_0_ = f32[8,2560]{1,0:T(8,128)S(1)} collective-permute-done((f32[8,2560]{1,0:T(8,128)S(1)}, f32[8,2560]{1,0:T(8,128)S(1)}, u32[]{:S(2)}, u32[]{:S(2)}) %collective-permute-start.9) | collective-permute-done | bytes 81952 | tf_op jit(solution)/shard_map/ppermute | solution.py:399
  68.0 1.4 %axial_join.1 = (f32[4,5,8,16,128]{4,3,2,1,0:T(8,128)S(1)}, f32[4,4,5,16,128]{4,3,2,1,0:T(8,128)S(1)}, f32[4,2,5,16,128]{4,3,2,1,0:T(8,128)S(1)}) custom-call(s32[1]{0:T(128)} %bitcast.core_ref, f32[4,5,8,16,128]{4,3,2,1,0:T(8,128)S(1)} %axial_local.1.local, bf16[2,24,128]{2,1,0:T(8,128)(2,1)S(1)} %dynamic-slice_bitcast_fusion.2.far, ...), custom_call_target="tpu_custom_call" | custom-call | flops 32768000 | bytes 3145728 | tf_op jit(solution)/shard_map/axial_join/pallas_call | solution.py:562
  69.4 2.1 %collective-permute-done.12.sib_pair = f32[4,4,5,16,128]{4,3,2,1,0:T(8,128)S(1)} collective-permute-done((f32[4,4,5,16,128]{4,3,2,1,0:T(8,128)S(1)}, f32[4,4,5,16,128]{4,3,2,1,0:T(8,128)S(1)}, u32[]{:S(2)}, u32[]{:S(2)}) %collective-permute-start.12) | collective-permute-done | bytes 655392 | tf_op jit(solution)/shard_map/ppermute | solution.py:403
  71.7 1.8 %collective-permute-start.14 = (f32[2,2,5,16,128]{4,3,2,1,0:T(8,128)S(1)}, f32[2,2,5,16,128]{4,3,2,1,0:T(8,128)S(1)}, u32[]{:S(2)}, u32[]{:S(2)}) collective-permute-start(f32[2,2,5,16,128]{4,3,2,1,0:T(8,128)S(1)} %pad_maximum_fusion.2), channel_id=1, source_target_pairs={{0,4},{1,5},{2,6},{3,7},{4,0},{5,1},{6,2},{7,3},{8,12},{9,13},{10,... | collective-permute-start | bytes 491528 | tf_op jit(solution)/shard_map/ppermute | solution.py:399
  73.5 2.8 %collective-permute-start.15 = (f32[2,2,5,16,128]{4,3,2,1,0:T(8,128)S(1)}, f32[2,2,5,16,128]{4,3,2,1,0:T(8,128)S(1)}, u32[]{:S(2)}, u32[]{:S(2)}) collective-permute-start(f32[2,2,5,16,128]{4,3,2,1,0:T(8,128)S(1)} %pad_maximum_fusion.2), channel_id=1, source_target_pairs={{0,6},{1,7},{2,0},{3,1},{4,2},{5,3},{6,4},{7,5},{8,14},{9,15},{10,... | collective-permute-start | bytes 491528 | tf_op jit(solution)/shard_map/ppermute | solution.py:399
  76.4 4.3 %collective-permute-done.13 = f32[2,2,5,16,128]{4,3,2,1,0:T(8,128)S(1)} collective-permute-done((f32[2,2,5,16,128]{4,3,2,1,0:T(8,128)S(1)}, f32[2,2,5,16,128]{4,3,2,1,0:T(8,128)S(1)}, u32[]{:S(2)}, u32[]{:S(2)}) %collective-permute-start.13) | collective-permute-done | bytes 163872 | tf_op jit(solution)/shard_map/ppermute | solution.py:399
  80.7 6.9 %collective-permute-done.14 = f32[2,2,5,16,128]{4,3,2,1,0:T(8,128)S(1)} collective-permute-done((f32[2,2,5,16,128]{4,3,2,1,0:T(8,128)S(1)}, f32[2,2,5,16,128]{4,3,2,1,0:T(8,128)S(1)}, u32[]{:S(2)}, u32[]{:S(2)}) %collective-permute-start.14) | collective-permute-done | bytes 163872 | tf_op jit(solution)/shard_map/ppermute | solution.py:399
  89.5 3.5 %collective-permute-done.17.odd = f32[4,2,5,16,128]{4,3,2,1,0:T(8,128)S(1)} collective-permute-done((f32[4,2,5,16,128]{4,3,2,1,0:T(8,128)S(1)}, f32[4,2,5,16,128]{4,3,2,1,0:T(8,128)S(1)}, u32[]{:S(2)}, u32[]{:S(2)}) %collective-permute-start.17) | collective-permute-done | bytes 327712 | tf_op jit(solution)/shard_map/ppermute | solution.py:404
  93.1 2.3 %azim_join.1 = (f32[5,64,8,128]{3,2,1,0:T(8,128)}, f32[8,128]{1,0:T(8,128)S(1)}) custom-call(s32[1]{0:T(128)} %bitcast.core_ref, f32[4,5,8,16,128]{4,3,2,1,0:T(8,128)S(1)} %azim_local.1.local, f32[2,2,5,16,128]{4,3,2,1,0:T(8,128)S(1)} %maximum_multiply_fusion.own_sums, f32[2,2,5,16,128]{4,3,2,1,0:T(8,128)S(1)} %collective-permute-done.16.sib_sums, ...), custom_call_target="tpu_custom_call" | custom-call | flops 6553600 | bytes 3145728 | tf_op jit(solution)/shard_map/azim_join/pallas_call | solution.py:586
  95.3 2.5 %signals.1 = f32[512,128]{1,0:T(8,128)S(1)} custom-call(f32[4,8,128]{2,1,0:T(8,128)S(1)} %entry_weights.1.weights, f32[8,128]{1,0:T(8,128)S(1)} %get-tuple-element.25.surface, s32[4,8,128]{2,1,0:T(8,128)S(1)} %copy-done.13, s32[4,8,128]{2,1,0:T(8,128)S(1)} %copy-done.14), custom_call_target="tpu_custom_call" | custom-call | tf_op jit(solution)/shard_map/signals/pallas_call | solution.py:600
  97.8 15.9 %all_to_all.5 = f32[32,16,128]{2,1,0:T(8,128)S(1)} all-to-all(f32[32,16,128]{2,1,0:T(8,128)S(1)} %bitcast.10), channel_id=1, replica_groups=mesh['axial'=4,'azim'=8] {'axial','azim'}, dimensions={0} | all-to-all | bytes 524288 | tf_op jit(solution)/shard_map/all_to_all | solution.py:607
  (87 shorter events, 23.3 us)
Async XLA Ops:
  18.0 1.9 %collective-permute-start = (f32[4,3,5,16,128]{4,3,2,1,0:T(8,128)S(1)}, f32[4,3,5,16,128]{4,3,2,1,0:T(8,128)S(1)}, u32[]{:S(2)}, u32[]{:S(2)}) collective-permute-start(f32[4,3,5,16,128]{4,3,2,1,0:T(8,128)S(1)} %get-tuple-element.16), channel_id=1, source_target_pairs={{0,1},{1,0},{2,3},{3,2},{4,5},{5,4},{6,7},{7,6},{8,9},{9,8},{10,11... | collective-permute-start | bytes 1474568 | tf_op jit(solution)/shard_map/ppermute | solution.py:403
  20.0 25.0 %copy-start.1 = (f32[3,64,8,128]{3,2,1,0:T(8,128)S(1)}, f32[3,64,8,128]{3,2,1,0:T(8,128)}, u32[]{:S(2)}) copy-start(f32[3,64,8,128]{3,2,1,0:T(8,128)} %velocity.3) | copy-start | bytes 2359300
  20.0 24.9 %copy-start.3 = (f32[3,64,8,128]{3,2,1,0:T(8,128)S(1)}, f32[3,64,8,128]{3,2,1,0:T(8,128)}, u32[]{:S(2)}) copy-start(f32[3,64,8,128]{3,2,1,0:T(8,128)} %axial_metric.3) | copy-start | bytes 2359300
  20.0 24.9 %copy-start.5 = (f32[3,64,8,128]{3,2,1,0:T(8,128)S(1)}, f32[3,64,8,128]{3,2,1,0:T(8,128)}, u32[]{:S(2)}) copy-start(f32[3,64,8,128]{3,2,1,0:T(8,128)} %azim_metric.3) | copy-start | bytes 2359300
  20.0 24.9 %copy-start.8 = (f32[64,8,128]{2,1,0:T(8,128)S(1)}, f32[64,8,128]{2,1,0:T(8,128)}, u32[]{:S(2)}) copy-start(f32[64,8,128]{2,1,0:T(8,128)} %density.3) | copy-start | bytes 786436
  20.1 24.9 %copy-start.10 = (f32[64,8,128]{2,1,0:T(8,128)S(1)}, f32[64,8,128]{2,1,0:T(8,128)}, u32[]{:S(2)}) copy-start(f32[64,8,128]{2,1,0:T(8,128)} %pressure.3) | copy-start | bytes 786436
  21.9 10.7 %collective-permute-start.1 = (f32[2,2,5,16,128]{4,3,2,1,0:T(8,128)}, f32[2,2,5,16,128]{4,3,2,1,0:T(8,128)}, u32[]{:S(2)}, u32[]{:S(2)}) collective-permute-start(f32[2,2,5,16,128]{4,3,2,1,0:T(8,128)} %pad_maximum_fusion), channel_id=1, source_target_pairs={{0,2},{1,3},{2,4},{3,5},{4,6},{5,7},{6,0},{7,1},{8,10},{9,11},{10,... | collective-permute-start | bytes 491528 | tf_op jit(solution)/shard_map/ppermute | solution.py:399
  24.9 14.0 %collective-permute-start.2 = (f32[2,2,5,16,128]{4,3,2,1,0:T(8,128)}, f32[2,2,5,16,128]{4,3,2,1,0:T(8,128)}, u32[]{:S(2)}, u32[]{:S(2)}) collective-permute-start(f32[2,2,5,16,128]{4,3,2,1,0:T(8,128)} %pad_maximum_fusion), channel_id=1, source_target_pairs={{0,4},{1,5},{2,6},{3,7},{4,0},{5,1},{6,2},{7,3},{8,12},{9,13},{10,... | collective-permute-start | bytes 491528 | tf_op jit(solution)/shard_map/ppermute | solution.py:399
  27.5 15.3 %collective-permute-start.3 = (f32[2,2,5,16,128]{4,3,2,1,0:T(8,128)}, f32[2,2,5,16,128]{4,3,2,1,0:T(8,128)}, u32[]{:S(2)}, u32[]{:S(2)}) collective-permute-start(f32[2,2,5,16,128]{4,3,2,1,0:T(8,128)} %pad_maximum_fusion), channel_id=1, source_target_pairs={{0,6},{1,7},{2,0},{3,1},{4,2},{5,3},{6,4},{7,5},{8,14},{9,15},{10,... | collective-permute-start | bytes 491528 | tf_op jit(solution)/shard_map/ppermute | solution.py:399
  28.8 27.6 %collective-permute-start.6 = (f32[8,2560]{1,0:T(8,128)}, f32[8,2560]{1,0:T(8,128)S(1)}, u32[]{:S(2)}, u32[]{:S(2)}) collective-permute-start(f32[8,2560]{1,0:T(8,128)} %get-tuple-element.18), channel_id=1, source_target_pairs={{0,8},{8,16},{16,24},{24,0},{1,9},{9,17},{17,25},{25,1},{2,10},{10... | collective-permute-start | bytes 245768 | tf_op jit(solution)/shard_map/ppermute | solution.py:399
  30.3 26.1 %collective-permute-start.7 = (f32[8,2560]{1,0:T(8,128)}, f32[8,2560]{1,0:T(8,128)S(1)}, u32[]{:S(2)}, u32[]{:S(2)}) collective-permute-start(f32[8,2560]{1,0:T(8,128)} %get-tuple-element.18), channel_id=1, source_target_pairs={{0,16},{8,24},{16,0},{24,8},{1,17},{9,25},{17,1},{25,9},{2,18},{10... | collective-permute-start | bytes 245768 | tf_op jit(solution)/shard_map/ppermute | solution.py:399
  32.7 23.8 %collective-permute-start.8 = (f32[8,2560]{1,0:T(8,128)}, f32[8,2560]{1,0:T(8,128)S(1)}, u32[]{:S(2)}, u32[]{:S(2)}) collective-permute-start(f32[8,2560]{1,0:T(8,128)} %get-tuple-element.18), channel_id=1, source_target_pairs={{0,24},{8,0},{16,8},{24,16},{1,25},{9,1},{17,9},{25,17},{2,26},{10... | collective-permute-start | bytes 245768 | tf_op jit(solution)/shard_map/ppermute | solution.py:399
  38.8 17.6 %collective-permute-start.5 = (f32[4,5,16,128]{3,2,1,0:T(8,128)}, f32[4,5,16,128]{3,2,1,0:T(8,128)S(1)}, u32[]{:S(2)}, u32[]{:S(2)}) collective-permute-start(f32[4,5,16,128]{3,2,1,0:T(8,128)} %copy-done.20), channel_id=1, source_target_pairs={{0,7},{1,2},{2,1},{3,4},{4,3},{5,6},{6,5},{7,0},{8,15},{9,10},{10,... | collective-permute-start | bytes 491528 | tf_op jit(solution)/shard_map/ppermute | solution.py:404
  44.0 12.4 %collective-permute-start.4 = (f32[2,2,5,16,128]{4,3,2,1,0:T(8,128)S(1)}, f32[2,2,5,16,128]{4,3,2,1,0:T(8,128)S(1)}, u32[]{:S(2)}, u32[]{:S(2)}) collective-permute-start(f32[2,2,5,16,128]{4,3,2,1,0:T(8,128)S(1)} %pad_maximum_fusion.1.own_sums), channel_id=1, source_target_pairs={{0,1},{1,0},{2,3},{3,2},{4,5},{5,4},{6,7},{7,6},{8,9},{9,8},{10,11... | collective-permute-start | bytes 491528 | tf_op jit(solution)/shard_map/ppermute | solution.py:425
  59.6 5.5 %collective-permute-start.10 = (f32[8,2560]{1,0:T(8,128)S(1)}, f32[8,2560]{1,0:T(8,128)S(1)}, u32[]{:S(2)}, u32[]{:S(2)}) collective-permute-start(f32[8,2560]{1,0:T(8,128)S(1)} %get-tuple-element.20), channel_id=1, source_target_pairs={{0,16},{8,24},{16,0},{24,8},{1,17},{9,25},{17,1},{25,9},{2,18},{10... | collective-permute-start | bytes 245768 | tf_op jit(solution)/shard_map/ppermute | solution.py:399
  61.2 4.6 %collective-permute-start.11 = (f32[8,2560]{1,0:T(8,128)S(1)}, f32[8,2560]{1,0:T(8,128)S(1)}, u32[]{:S(2)}, u32[]{:S(2)}) collective-permute-start(f32[8,2560]{1,0:T(8,128)S(1)} %get-tuple-element.20), channel_id=1, source_target_pairs={{0,24},{8,0},{16,8},{24,16},{1,25},{9,1},{17,9},{25,17},{2,26},{10... | collective-permute-start | bytes 245768 | tf_op jit(solution)/shard_map/ppermute | solution.py:399
  62.6 5.3 %collective-permute-start.9 = (f32[8,2560]{1,0:T(8,128)S(1)}, f32[8,2560]{1,0:T(8,128)S(1)}, u32[]{:S(2)}, u32[]{:S(2)}) collective-permute-start(f32[8,2560]{1,0:T(8,128)S(1)} %get-tuple-element.20), channel_id=1, source_target_pairs={{0,8},{8,16},{16,24},{24,0},{1,9},{9,17},{17,25},{25,1},{2,10},{10... | collective-permute-start | bytes 245768 | tf_op jit(solution)/shard_map/ppermute | solution.py:399
  69.3 2.2 %collective-permute-start.12 = (f32[4,4,5,16,128]{4,3,2,1,0:T(8,128)S(1)}, f32[4,4,5,16,128]{4,3,2,1,0:T(8,128)S(1)}, u32[]{:S(2)}, u32[]{:S(2)}) collective-permute-start(f32[4,4,5,16,128]{4,3,2,1,0:T(8,128)S(1)} %get-tuple-element.22), channel_id=1, source_target_pairs={{0,1},{1,0},{2,3},{3,2},{4,5},{5,4},{6,7},{7,6},{8,9},{9,8},{10,11... | collective-permute-start | bytes 1966088 | tf_op jit(solution)/shard_map/ppermute | solution.py:403
  71.5 16.2 %copy-start.15 = (s32[4,8,128]{2,1,0:T(8,128)S(1)}, s32[4,8,128]{2,1,0:T(8,128)}, u32[]{:S(2)}) copy-start(s32[4,8,128]{2,1,0:T(8,128)} %ids.1) | copy-start | bytes 49156
  71.7 9.0 %collective-permute-start.13 = (f32[2,2,5,16,128]{4,3,2,1,0:T(8,128)S(1)}, f32[2,2,5,16,128]{4,3,2,1,0:T(8,128)S(1)}, u32[]{:S(2)}, u32[]{:S(2)}) collective-permute-start(f32[2,2,5,16,128]{4,3,2,1,0:T(8,128)S(1)} %pad_maximum_fusion.2), channel_id=1, source_target_pairs={{0,2},{1,3},{2,4},{3,5},{4,6},{5,7},{6,0},{7,1},{8,10},{9,11},{10,... | collective-permute-start | bytes 491528 | tf_op jit(solution)/shard_map/ppermute | solution.py:399
  71.7 15.9 %collective-permute-start.14 = (f32[2,2,5,16,128]{4,3,2,1,0:T(8,128)S(1)}, f32[2,2,5,16,128]{4,3,2,1,0:T(8,128)S(1)}, u32[]{:S(2)}, u32[]{:S(2)}) collective-permute-start(f32[2,2,5,16,128]{4,3,2,1,0:T(8,128)S(1)} %pad_maximum_fusion.2), channel_id=1, source_target_pairs={{0,4},{1,5},{2,6},{3,7},{4,0},{5,1},{6,2},{7,3},{8,12},{9,13},{10,... | collective-permute-start | bytes 491528 | tf_op jit(solution)/shard_map/ppermute | solution.py:399
  73.5 14.1 %collective-permute-start.15 = (f32[2,2,5,16,128]{4,3,2,1,0:T(8,128)S(1)}, f32[2,2,5,16,128]{4,3,2,1,0:T(8,128)S(1)}, u32[]{:S(2)}, u32[]{:S(2)}) collective-permute-start(f32[2,2,5,16,128]{4,3,2,1,0:T(8,128)S(1)} %pad_maximum_fusion.2), channel_id=1, source_target_pairs={{0,6},{1,7},{2,0},{3,1},{4,2},{5,3},{6,4},{7,5},{8,14},{9,15},{10,... | collective-permute-start | bytes 491528 | tf_op jit(solution)/shard_map/ppermute | solution.py:399
  76.4 16.7 %collective-permute-start.17 = (f32[4,2,5,16,128]{4,3,2,1,0:T(8,128)S(1)}, f32[4,2,5,16,128]{4,3,2,1,0:T(8,128)S(1)}, u32[]{:S(2)}, u32[]{:S(2)}) collective-permute-start(f32[4,2,5,16,128]{4,3,2,1,0:T(8,128)S(1)} %get-tuple-element.23), channel_id=1, source_target_pairs={{0,7},{1,2},{2,1},{3,4},{4,3},{5,6},{6,5},{7,0},{8,15},{9,10},{10,... | collective-permute-start | bytes 983048 | tf_op jit(solution)/shard_map/ppermute | solution.py:404
  87.7 5.4 %collective-permute-start.16 = (f32[2,2,5,16,128]{4,3,2,1,0:T(8,128)S(1)}, f32[2,2,5,16,128]{4,3,2,1,0:T(8,128)S(1)}, u32[]{:S(2)}, u32[]{:S(2)}) collective-permute-start(f32[2,2,5,16,128]{4,3,2,1,0:T(8,128)S(1)} %maximum_multiply_fusion.own_sums), channel_id=1, source_target_pairs={{0,1},{1,0},{2,3},{3,2},{4,5},{5,4},{6,7},{7,6},{8,9},{9,8},{10,11... | collective-permute-start | bytes 491528 | tf_op jit(solution)/shard_map/ppermute | solution.py:425
  (17 other events, 79.9 us)

commit v2 on v1

v2 whole, which is shorter than its diff:
```python
import functools
import math

import jax
import jax.numpy as jnp
import numpy as np
from jax import lax
from jax.experimental import pallas as pl
from jax.experimental.pallas import tpu as pltpu
from jax.sharding import PartitionSpec as P

OBSERVERS = 512
TIME_BINS = 128

GAMMA = 1.4
SECTION = 0.25
DERIV_ALPHA = 1.0 / 3.0
FILTER_ALPHA = 0.499
FIELDS = 5
CHUNK = 16
BASIS = 8
VMEM_LIMIT = 32 * 1024 * 1024
INPUT_LIMIT = 60 * 1024 * 1024


def decay_root(alpha):
    return (-1.0 + math.sqrt(1.0 - 4.0 * alpha * alpha)) / (2.0 * alpha)


DERIV_ROOT = decay_root(DERIV_ALPHA)
FILTER_ROOT = decay_root(FILTER_ALPHA)

DERIV_NEAR = 1.0 / 12.0
DERIV_FAR = (
    (25.0 / 36.0) * (DERIV_ROOT - 1.0 / DERIV_ROOT) / (1.0 + 2.0 * DERIV_ALPHA * DERIV_ROOT)
)

_B = FILTER_ALPHA
_EDGE = (1.0 - 2.0 * _B) / 64.0
_Q2 = 1.0 / _B
_Q1 = (-6.0 - _Q2) / _B
_Q0 = (12.0 - _Q1) / _B
_RHO = -8.0 - _Q0
FILTER_MID = _EDGE * (_Q0 + 2.0 * _Q2)
FILTER_ONE = _EDGE * _Q1
FILTER_TWO = _EDGE * _Q2
FILTER_FAR = _EDGE * _RHO / (1.0 + 2.0 * _B * FILTER_ROOT)


def open_operator(length, alpha, side):
    base = decay_root(alpha)
    tri = np.eye(length) + alpha * (np.eye(length, k=1) + np.eye(length, k=-1))
    tri[0, 0] = -alpha / base
    return np.linalg.solve(tri, side)


def deriv_matrix(length):
    return (7.0 / 9.0) * (np.eye(length, k=1) - np.eye(length, k=-1)) + (1.0 / 36.0) * (
        np.eye(length, k=2) - np.eye(length, k=-2)
    )


def filter_matrix(length):
    beta = FILTER_ALPHA
    coeffs = [
        (11.0 + 10.0 * beta) / 16.0,
        (15.0 + 34.0 * beta) / 32.0,
        (-3.0 + 6.0 * beta) / 16.0,
        (1.0 - 2.0 * beta) / 32.0,
    ]
    total = coeffs[0] * np.eye(length)
    for shift in range(1, 4):
        total = total + 0.5 * coeffs[shift] * (np.eye(length, k=shift) + np.eye(length, k=-shift))
    return total


def axial_tables(count, width, alpha, kind):
    length = count * width
    side = deriv_matrix(length) if kind == "deriv" else filter_matrix(length)
    whole = open_operator(length, alpha, side)
    base = decay_root(alpha)
    basis = np.zeros((BASIS, width))
    for edge in range(3):
        basis[edge, edge] = 1.0
        basis[3 + edge, width - 3 + edge] = 1.0
    basis[6] = base ** np.arange(width - 1, -1, -1, dtype=np.float64)
    basis[7] = base ** np.arange(width, dtype=np.float64)
    inverse = np.linalg.pinv(basis)
    own = np.zeros((count, width, width))
    far = np.zeros((count, max(count - 1, 1) * BASIS, width))
    for here in range(count):
        rows = whole[here * width : (here + 1) * width]
        own[here] = rows[:, here * width : (here + 1) * width].T
        if kind == "filter":
            own[here] -= np.eye(width)
        for shift in range(1, count):
            there = (here - shift) % count
            block = rows[:, there * width : (there + 1) * width]
            far[here, (shift - 1) * BASIS : shift * BASIS] = (block @ inverse).T
    return own, basis, far


def surface_tables(along, width, around, rows):
    axial = open_operator(along * width, FILTER_ALPHA, filter_matrix(along * width))
    axial = axial.reshape(along, width, along * width).transpose(0, 2, 1)
    length = around * rows
    turn = np.roll(np.eye(length), 1, axis=1)
    beta = FILTER_ALPHA
    side = (11.0 + 10.0 * beta) / 16.0 * np.eye(length)
    coeffs = [(15.0 + 34.0 * beta) / 32.0, (-3.0 + 6.0 * beta) / 16.0, (1.0 - 2.0 * beta) / 32.0]
    for shift in range(1, 4):
        step = np.linalg.matrix_power(turn, shift)
        side = side + 0.5 * coeffs[shift - 1] * (step + step.T)
    cycle = np.linalg.solve(np.eye(length) + beta * (turn + turn.T), side)
    return axial.astype(np.float32), cycle.reshape(around, rows, length).astype(np.float32)


def halves(table):
    high = np.asarray(table, np.float32).astype(jnp.bfloat16)
    low = (np.asarray(table, np.float64) - high.astype(np.float64)).astype(jnp.bfloat16)
    return np.stack([high, low], axis=-3)


def split(values):
    high = values.astype(jnp.bfloat16)
    return high, (values - high.astype(jnp.float32)).astype(jnp.bfloat16)


def dots(left, right, dims):
    out = None
    for a, b in ((0, 0), (1, 0), (0, 1)):
        part = lax.dot_general(
            left[a], right[b], (dims, ((), ())), preferred_element_type=jnp.float32
        )
        out = part if out is None else out + part
    return out


def outgoing(basis_ref, lines):
    return dots((basis_ref[0], basis_ref[1]), split(lines), ((1,), (1,)))


def incoming(parts, far_ref):
    return dots(split(jnp.concatenate(parts, axis=0)), (far_ref[0], far_ref[1]), ((0,), (0,)))


def own_block(lines, own_ref):
    return dots(split(lines), (own_ref[0], own_ref[1]), ((1,), (0,)))


def tile_energy(density, velocity, pressure):
    return pressure * (1.0 / (GAMMA - 1.0)) + 0.5 * density * (
        velocity[0] * velocity[0] + velocity[1] * velocity[1] + velocity[2] * velocity[2]
    )


def tile_flux(density, velocity, pressure, energy, metric, volume):
    contra = metric[0] * velocity[0] + metric[1] * velocity[1] + metric[2] * velocity[2]
    volume_contra = volume * contra
    mass = density * volume_contra
    push = volume * pressure
    pieces = [mass]
    for comp in range(3):
        pieces.append(mass * velocity[comp] + metric[comp] * push)
    pieces.append((energy + pressure) * volume_contra)
    return pieces


def pack_rows(tiles, root, near, pack):
    rows = len(tiles)
    head = tail = tiles[0]
    for row in range(1, rows):
        head = tiles[row] + root * head
        tail = tail + (root**row) * tiles[row]
    pack[0] = head
    pack[1] = tail
    for n in range(near):
        pack[2 + n] = tiles[n]
        pack[2 + near + n] = tiles[rows - near + n]


def azim_flux_kernel(density, velocity, pressure, azim_metric, volume, pack, flux):
    planes, rows, _ = density.shape
    for plane in range(planes):
        rho = density[plane]
        vel = [velocity[c, plane] for c in range(3)]
        pres = pressure[plane]
        energy = tile_energy(rho, vel, pres)
        metric = [azim_metric[c, plane] for c in range(3)]
        for f, piece in enumerate(tile_flux(rho, vel, pres, energy, metric, volume[plane])):
            flux[f, plane] = piece
    for f in range(FIELDS):
        turned = jnp.swapaxes(flux[f], 0, 1)
        pack_rows([turned[row] for row in range(rows)], DERIV_ROOT, 1, pack.at[0, :, f])


def section_local_kernel(
    place,
    density,
    velocity,
    pressure,
    axial_metric,
    azim_metric,
    volume,
    radial,
    own,
    basis,
    base_out,
    scale_out,
    edge_out,
    axial_flux,
    azim_flux,
    start,
):
    planes, rows, lanes = density.shape
    for plane in range(planes):
        rho = density[plane]
        vel = [velocity[c, plane] for c in range(3)]
        pres = pressure[plane]
        vol = volume[plane]
        energy = tile_energy(rho, vel, pres)
        axial = tile_flux(rho, vel, pres, energy, [axial_metric[c, plane] for c in range(3)], vol)
        azim = tile_flux(rho, vel, pres, energy, [azim_metric[c, plane] for c in range(3)], vol)
        state = [rho, rho * vel[0], rho * vel[1], rho * vel[2], energy]
        for f in range(FIELDS):
            axial_flux[f, plane] = axial[f]
            azim_flux[f, plane] = azim[f]
            start[f, plane] = state[f] + SECTION * radial[f, plane]
    scale = SECTION / volume[...]
    turned_scale = jnp.swapaxes(scale, 0, 1)
    scale_out[0] = turned_scale
    for f in range(FIELDS):
        flux = jnp.swapaxes(axial_flux[f], 0, 1).reshape(rows * planes, lanes)
        edge_out[:, f * rows * planes : (f + 1) * rows * planes] = outgoing(basis, flux)
        deriv = own_block(flux, own).reshape(rows, planes, lanes)
        azim = jnp.swapaxes(azim_flux[f], 0, 1)
        first = jnp.swapaxes(start[f], 0, 1)
        down = [None] * rows
        down[rows - 1] = azim[rows - 1]
        for row in range(rows - 2, -1, -1):
            down[row] = azim[row] + DERIV_ROOT * down[row + 1]
        up = None
        for row in range(rows):
            up = azim[row] if row == 0 else azim[row] + DERIV_ROOT * up
            total = deriv[row] + DERIV_FAR * (up - down[row])
            if row > 0:
                total = total - DERIV_NEAR * azim[row - 1]
            if row < rows - 1:
                total = total + DERIV_NEAR * azim[row + 1]
            base_out[0, f, row] = first[row] - turned_scale[row] * total


def chip_kernel(near, rows, root, place, mine, other, ahead, back, far):
    core = place[0]
    decay = root**rows

    def low(n):
        return jnp.where(core == 0, mine[0, n], other[0, n])

    def high(n):
        return jnp.where(core == 0, other[0, n], mine[0, n])

    head = high(0) + decay * low(0)
    tail = low(1) + decay * high(1)
    for out in (ahead, back, far):
        out[0, 0] = head
        out[0, 1] = tail
    for n in range(near):
        ahead[0, 2 + n] = high(2 + near + n)
        back[0, 2 + n] = low(2 + n)


def ring_kernel(chips, near, rows, root, place, own, left_in, right_in, *rest):
    far, (mine, theirs) = rest[: chips - 3], rest[chips - 3 :]
    core = place[0]
    wide = root ** (2 * rows)
    close = 1.0 / (1.0 - root ** (2 * rows * chips))
    left = wide ** (chips - 1) * own[0, 0]
    right = wide ** (chips - 1) * own[0, 1]
    for shift, there in enumerate([left_in, *far, right_in], start=1):
        left = left + wide ** (shift - 1) * there[0, 0]
        right = right + wide ** (chips - shift - 1) * there[0, 1]
    for out in (mine, theirs):
        out[0, 0] = close * left
        out[0, 1] = close * right
    for n in range(near):
        before, after = left_in[0, 2 + n], right_in[0, 2 + n]
        mine[0, 2 + n] = jnp.where(core == 0, before, after)
        theirs[0, 2 + n] = jnp.where(core == 0, after, before)


def surroundings(place, half, own, sib, sib_pack, near, root, rows):
    core = place[0]
    mine = (pl.program_id(0) // half) == core
    ring = [jnp.where(mine, own[0, n], sib[0, n]) for n in range(2 + near)]
    decay = root**rows
    zero, one = jnp.float32(0.0), jnp.float32(1.0)
    first = core == 0
    left = jnp.where(first, one, decay) * ring[0] + jnp.where(first, zero, one) * sib_pack[0, 0]
    right = jnp.where(first, decay, one) * ring[1] + jnp.where(first, one, zero) * sib_pack[0, 1]
    before = [jnp.where(first, ring[2 + n], sib_pack[0, 2 + near + n]) for n in range(near)]
    after = [jnp.where(first, sib_pack[0, 2 + n], ring[2 + n]) for n in range(near)]
    return left, right, before, after


def section_join_kernel(half, place, base, scale, own, sib, sib_pack, far, basis, *rest):
    edges, (out, edge_out, front) = rest[:-3], rest[-3:]
    rows, planes, lanes = scale.shape[1:]
    left, right, (before,), (after,) = surroundings(
        place, half, own, sib, sib_pack, 1, DERIV_ROOT, rows
    )
    for f in range(FIELDS):
        spot = slice(f * rows * planes, (f + 1) * rows * planes)
        axial = incoming([ref[:, spot] for ref in edges], far).reshape(rows, planes, lanes)
        for row in range(rows):
            azim = (DERIV_FAR * DERIV_ROOT ** (row + 1)) * left[f] - (
                DERIV_FAR * DERIV_ROOT ** (rows - row)
            ) * right[f]
            if row == 0:
                azim = azim - DERIV_NEAR * before[f]
            if row == rows - 1:
                azim = azim + DERIV_NEAR * after[f]
            out[0, f, row] = base[0, f, row] - scale[0, row] * (axial[row] + azim)
        edge_out[:, spot] = outgoing(basis, out[0, f].reshape(rows * planes, lanes))

    @pl.when(pl.program_id(0) == 0)
    def _():
        for row in range(rows):
            front[row : row + 1, :] = out[0, 2, row, 0:1, :] + out[0, 0, row, 0:1, :]


def axial_local_kernel(place, values, own, out):
    lines = values[0].reshape(-1, values.shape[-1])
    out[0] = (lines + own_block(lines, own)).reshape(out.shape[1:])


def axial_join_kernel(local, far, *rest):
    edges, (out, pack) = rest[:-2], rest[-2:]
    rows, planes, lanes = local.shape[2:]
    for f in range(FIELDS):
        spot = slice(f * rows * planes, (f + 1) * rows * planes)
        axial = incoming([ref[:, spot] for ref in edges], far).reshape(rows, planes, lanes)
        tiles = [local[0, f, row] + axial[row] for row in range(rows)]
        for row in range(rows):
            out[0, f, row] = tiles[row]
        pack_rows(tiles, FILTER_ROOT, 2, pack.at[0, :, f])


def azim_local_kernel(values, out):
    rows = values.shape[2]
    for f in range(FIELDS):
        down = [None] * rows
        down[rows - 1] = values[0, f, rows - 1]
        for row in range(rows - 2, -1, -1):
            down[row] = values[0, f, row] + FILTER_ROOT * down[row + 1]
        up = None
        for row in range(rows):
            here = values[0, f, row]
            up = here if row == 0 else here + FILTER_ROOT * up
            total = (1.0 + FILTER_MID - FILTER_FAR) * here + FILTER_FAR * (up + down[row])
            for step, weight in ((1, FILTER_ONE), (2, FILTER_TWO)):
                if row >= step:
                    total = total + weight * values[0, f, row - step]
                if row + step < rows:
                    total = total + weight * values[0, f, row + step]
            out[0, f, row] = total


def azim_join_kernel(half, place, local, own, sib, sib_pack, out):
    rows = local.shape[2]
    left, right, before, after = surroundings(
        place, half, own, sib, sib_pack, 2, FILTER_ROOT, rows
    )
    for f in range(FIELDS):
        tiles = []
        for row in range(rows):
            total = (
                local[0, f, row]
                + (FILTER_FAR * FILTER_ROOT ** (row + 1)) * left[f]
                + (FILTER_FAR * FILTER_ROOT ** (rows - row)) * right[f]
            )
            if row < 2:
                total = total + FILTER_TWO * before[row][f]
            if row == 0:
                total = total + FILTER_ONE * before[1][f]
            if row >= rows - 2:
                total = total + FILTER_TWO * after[row - (rows - 2)][f]
            if row == rows - 1:
                total = total + FILTER_ONE * after[0][f]
            tiles.append(total)
        out[f] = jnp.swapaxes(jnp.stack(tiles), 0, 1)


def weights_kernel(table, ids, area, out):
    entries = ids.shape[0]
    for entry in range(entries):
        chosen = ids[entry]
        found = jnp.zeros(chosen.shape, jnp.float32)
        for t in range(table.shape[0]):
            found = jnp.where(chosen == t, table[t], found)
        out[entry] = found * area[...]


def signals_kernel(place, fronts, around, along, weights, observers, bins, out):
    entries, rows, lanes = weights.shape
    columns = around.shape[2] // rows
    surface = jnp.full((rows, lanes), -1.0, jnp.float32)
    for a in range(fronts.shape[0] // columns):
        ring = fronts[a * columns : (a + 1) * columns].reshape(columns * rows, lanes)
        smooth = jnp.dot(
            around[0], ring, precision=lax.Precision.HIGHEST, preferred_element_type=jnp.float32
        )
        surface = surface + jnp.dot(
            smooth,
            along[0, a * lanes : (a + 1) * lanes],
            precision=lax.Precision.HIGHEST,
            preferred_element_type=jnp.float32,
        )
    observer_rows = lax.broadcasted_iota(jnp.int32, (out.shape[0], lanes), 0)
    bin_rows = lax.broadcasted_iota(jnp.int32, (out.shape[1], lanes), 0)
    out[...] = jnp.zeros_like(out)
    for row in range(rows):
        left, right = [], []
        for entry in range(entries):
            value = weights[entry, row : row + 1, :] * surface[row : row + 1, :]
            hit = observer_rows == observers[entry, row : row + 1, :]
            left.append(jnp.where(hit, 1.0, 0.0).astype(jnp.bfloat16))
            right.append(jnp.where(bin_rows == bins[entry, row : row + 1, :], value, 0.0))
        one_hot = jnp.concatenate(left, axis=1)
        high, low = split(jnp.concatenate(right, axis=1))
        for part in (high, low):
            out[...] += lax.dot_general(
                one_hot, part, (((1,), (1,)), ((), ())), preferred_element_type=jnp.float32
            )


def params(limit=VMEM_LIMIT):
    return pltpu.CompilerParams(vmem_limit_bytes=limit)


def cost(flops, moved):
    return pl.CostEstimate(flops=int(flops), bytes_accessed=int(moved), transcendentals=0)


def rotate(values, axis, count, shift):
    return lax.ppermute(values, axis, [(i, (i + shift) % count) for i in range(count)])


def sibling(values, count):
    return lax.ppermute(values, "azim", [(i, i ^ 1) for i in range(count)])


def azim_exchange(place, pack, count, near, root, rows):
    steps, values, fields, planes, lanes = pack.shape
    chips = count // 2
    half = steps // 2
    f32 = jnp.float32

    def block(size, start):
        if start:
            return pl.BlockSpec(
                (1, size, fields, planes, lanes), lambda k, at: (k + at[0] * half, 0, 0, 0, 0)
            )
        return pl.BlockSpec((1, size, fields, planes, lanes), lambda k, at: (k, 0, 0, 0, 0))

    def shape(size):
        return jax.ShapeDtypeStruct((half, size, fields, planes, lanes), f32)

    sib = sibling(pack, count)
    wide = 2 + near
    ahead, back, far = pl.pallas_call(
        functools.partial(chip_kernel, near, rows, root),
        grid_spec=pltpu.PrefetchScalarGridSpec(
            num_scalar_prefetch=1,
            grid=(half,),
            in_specs=[block(values, True)] * 2,
            out_specs=[block(wide, False)] * 2 + [block(2, False)],
        ),
        out_shape=[shape(wide)] * 2 + [shape(2)],
        compiler_params=params(),
        name="chip_moments",
    )(place, pack, sib)
    left_in = rotate(ahead, "azim", count, 2)
    right_in = rotate(back, "azim", count, -2)
    between = [rotate(far, "azim", count, 2 * shift) for shift in range(2, chips - 1)]
    return sib, far, left_in, right_in, between


def ring_join(place, far, left_in, right_in, between, count, near, root, rows):
    half, _, fields, planes, lanes = far.shape
    chips = count // 2
    wide = 2 + near

    def block(size):
        return pl.BlockSpec((1, size, fields, planes, lanes), lambda k, at: (k, 0, 0, 0, 0))

    out = jax.ShapeDtypeStruct((half, wide, fields, planes, lanes), jnp.float32)
    mine, theirs = pl.pallas_call(
        functools.partial(ring_kernel, chips, near, rows, root),
        grid_spec=pltpu.PrefetchScalarGridSpec(
            num_scalar_prefetch=1,
            grid=(half,),
            in_specs=[block(2), block(wide), block(wide)] + [block(2)] * (chips - 3),
            out_specs=[block(wide)] * 2,
        ),
        out_shape=[out, out],
        compiler_params=params(),
        name="ring_sums",
    )(place, far, left_in, right_in, *between)
    return mine, sibling(theirs, count)


def per_device(
    density,
    velocity,
    pressure,
    axial_metric,
    azim_metric,
    volume,
    radial_term,
    panel_area,
    observer_ids,
    bin_ids,
    weight_ids,
    bin_weights,
):
    planes, rows, lanes = density.shape
    along = lax.axis_size("axial")
    around = lax.axis_size("azim")
    devices = along * around
    steps = planes // CHUNK
    half = steps // 2
    lines = FIELDS * rows * CHUNK
    f32 = jnp.float32
    azim_at = lax.axis_index("azim")
    place = jnp.stack([azim_at % 2, lax.axis_index("axial"), azim_at]).astype(jnp.int32)

    own_d, basis_d, far_d = map(halves, axial_tables(along, lanes, DERIV_ALPHA, "deriv"))
    own_f, basis_f, far_f = map(halves, axial_tables(along, lanes, FILTER_ALPHA, "filter"))
    filter_along, filter_around = surface_tables(along, lanes, around, rows)

    def spec(shape, index):
        return pl.BlockSpec(shape, index)

    smem = pl.BlockSpec(memory_space=pltpu.SMEM)
    field = spec((CHUNK, rows, lanes), lambda k, at: (k, 0, 0))
    vector = spec((3, CHUNK, rows, lanes), lambda k, at: (0, k, 0, 0))
    wide = spec((FIELDS, CHUNK, rows, lanes), lambda k, at: (0, k, 0, 0))
    inner = spec((1, FIELDS, rows, CHUNK, lanes), lambda k, at: (k, 0, 0, 0, 0))
    inner_one = spec((1, rows, CHUNK, lanes), lambda k, at: (k, 0, 0, 0))
    edge = spec((BASIS, lines), lambda k, at: (0, k))

    def table(array):
        return spec((None,) + array.shape[1:], lambda k, at: (at[1],) + (0,) * (array.ndim - 1))

    def fixed(shape):
        return spec(shape, lambda k, at: (0,) * len(shape))

    def packed(size):
        return spec((1, size, FIELDS, CHUNK, lanes), lambda k, at: (k, 0, 0, 0, 0))

    def ring(size):
        return spec((1, size, FIELDS, CHUNK, lanes), lambda k, at: (k % half, 0, 0, 0, 0))

    def packed_shape(size):
        return jax.ShapeDtypeStruct((steps, size, FIELDS, CHUNK, lanes), f32)

    def call(kernel, name, ins, outs, shapes, args, flops, moved, scratch=(), limit=VMEM_LIMIT):
        return pl.pallas_call(
            kernel,
            grid_spec=pltpu.PrefetchScalarGridSpec(
                num_scalar_prefetch=1,
                grid=(steps,),
                in_specs=ins,
                out_specs=outs,
                scratch_shapes=scratch,
            ),
            out_shape=shapes,
            compiler_params=params(limit),
            cost_estimate=cost(flops, moved),
            name=name,
        )(place, *args)

    def unplaced(kernel):
        return lambda at, *refs: kernel(*refs)

    inner_shape = jax.ShapeDtypeStruct((steps, FIELDS, rows, CHUNK, lanes), f32)
    one_shape = jax.ShapeDtypeStruct((steps, rows, CHUNK, lanes), f32)
    edge_shape = jax.ShapeDtypeStruct((BASIS, steps * lines), f32)
    flux_scratch = pltpu.VMEM((FIELDS, CHUNK, rows, lanes), f32)
    block = planes * rows * lanes

    pack_d = call(
        unplaced(azim_flux_kernel),
        "azim_flux",
        [field, vector, field, vector, field],
        packed(4),
        packed_shape(4),
        (density, velocity, pressure, azim_metric, volume),
        100 * block,
        40 * block,
        scratch=[flux_scratch],
        limit=INPUT_LIMIT,
    )
    sib_d, far_m, left_in, right_in, between = azim_exchange(
        place, pack_d, around, 1, DERIV_ROOT, rows
    )

    weights = pl.pallas_call(
        weights_kernel,
        in_specs=[smem] + [pl.BlockSpec(memory_space=pltpu.VMEM)] * 2,
        out_specs=pl.BlockSpec(memory_space=pltpu.VMEM),
        out_shape=jax.ShapeDtypeStruct(weight_ids.shape, f32),
        compiler_params=params(),
        name="entry_weights",
    )(bin_weights, weight_ids, panel_area)

    base, scale, edge_d = call(
        section_local_kernel,
        "section_local",
        [field, vector, field, vector, vector, field, wide, table(own_d), fixed(basis_d.shape)],
        [inner, inner_one, edge],
        [inner_shape, one_shape, edge_shape],
        (
            density,
            velocity,
            pressure,
            axial_metric,
            azim_metric,
            volume,
            radial_term,
            own_d,
            basis_d,
        ),
        4000 * block,
        100 * block,
        scratch=[flux_scratch] * 3,
    )
    edges_d = [rotate(edge_d, "axial", along, s) for s in range(1, along)]
    mine, sib = ring_join(place, far_m, left_in, right_in, between, around, 1, DERIV_ROOT, rows)

    sectioned, edge_f, front = call(
        functools.partial(section_join_kernel, half),
        "section_join",
        [inner, inner_one, ring(3), ring(3), packed(4), table(far_d), fixed(basis_f.shape)]
        + [edge] * (along - 1),
        [inner, edge, fixed((rows, lanes))],
        [inner_shape, edge_shape, jax.ShapeDtypeStruct((rows, lanes), f32)],
        (base, scale, mine, sib, sib_d, far_d, basis_f, *edges_d),
        500 * block,
        48 * block,
    )
    edges_f = [rotate(edge_f, "axial", along, s) for s in range(1, along)]
    fronts = lax.all_to_all(
        jnp.broadcast_to(front[None], (devices, rows, lanes)), ("axial", "azim"), 0, 0, tiled=True
    )

    axial_local = call(
        axial_local_kernel,
        "axial_local",
        [inner, table(own_f)],
        inner,
        inner_shape,
        (sectioned, own_f),
        4000 * block,
        40 * block,
    )
    smoothed, pack_f = call(
        unplaced(axial_join_kernel),
        "axial_join",
        [inner, table(far_f)] + [edge] * (along - 1),
        [inner, packed(6)],
        [inner_shape, packed_shape(6)],
        (axial_local, far_f, *edges_f),
        500 * block,
        48 * block,
    )
    sib_f, far_m, left_in, right_in, between = azim_exchange(
        place, pack_f, around, 2, FILTER_ROOT, rows
    )

    azim_local = call(
        unplaced(azim_local_kernel),
        "azim_local",
        [inner],
        inner,
        inner_shape,
        (smoothed,),
        100 * block,
        40 * block,
    )

    whole = pl.BlockSpec(memory_space=pltpu.VMEM)
    partial = pl.pallas_call(
        signals_kernel,
        grid_spec=pltpu.PrefetchScalarGridSpec(
            num_scalar_prefetch=1,
            grid=(1,),
            in_specs=[
                fixed(fronts.shape),
                spec((1,) + filter_around.shape[1:], lambda k, at: (at[2], 0, 0)),
                spec((1,) + filter_along.shape[1:], lambda k, at: (at[1], 0, 0)),
                fixed(weights.shape),
                fixed(observer_ids.shape),
                fixed(bin_ids.shape),
            ],
            out_specs=fixed((OBSERVERS, TIME_BINS)),
        ),
        out_shape=jax.ShapeDtypeStruct((OBSERVERS, TIME_BINS), f32),
        compiler_params=params(),
        name="signals",
    )(place, fronts, filter_around, filter_along, weights, observer_ids, bin_ids)
    shares = lax.all_to_all(
        partial.reshape(devices, OBSERVERS // devices, TIME_BINS),
        ("axial", "azim"),
        0,
        0,
        tiled=True,
    )
    signals = jnp.sum(shares, axis=0)

    mine, sib = ring_join(place, far_m, left_in, right_in, between, around, 2, FILTER_ROOT, rows)
    new_state = call(
        functools.partial(azim_join_kernel, half),
        "azim_join",
        [inner, ring(4), ring(4), packed(6)],
        wide,
        jax.ShapeDtypeStruct((FIELDS, planes, rows, lanes), f32),
        (azim_local, mine, sib, sib_f),
        100 * block,
        48 * block,
    )
    return (new_state, signals)


def solution(mesh):
    placed = (
        P(None, "azim", "axial"),
        P(None, None, "azim", "axial"),
        P(None, "azim", "axial"),
        P(None, None, "azim", "axial"),
        P(None, None, "azim", "axial"),
        P(None, "azim", "axial"),
        P(None, None, "azim", "axial"),
        P("azim", "axial"),
        P(None, "azim", "axial"),
        P(None, "azim", "axial"),
        P(None, "azim", "axial"),
        P(),
    )
    return jax.shard_map(
        per_device,
        mesh=mesh,
        in_specs=placed,
        out_specs=(P(None, None, "azim", "axial"), P(("axial", "azim"), None)),
        check_vma=False,
    )
```

time: 115 us -> 107 us (0.930)
  blocking collectives: 15.9 us -> 0 us
  waiting for transfers between devices: 24.2 us -> 39.9 us
  local copies, waits for them, and re-layouts: 13.9 us -> 5.59 us
  starting transfers between devices: 25.2 us -> 28.5 us
  other arithmetic: 3.82 us -> 2.2 us
    ppermute x12, waiting for transfers between devices: 17.9 us -> 37.5 us  [rotate(): lax.ppermute(values, axis, [(i, (i + shift) % count) for i in range(count)])]
    all_to_all x1 -> x0, blocking collectives: 15.9 us -> none  [per_device(): lax.all_to_all(partial.reshape(devices, OBSERVERS // devices, TIME_BINS),...]
    all_to_all x0 -> x2, starting transfers between devices: none -> 7.19 us  [the longest x1 3.77 us: per_device(): lax.all_to_all(partial.reshape(devices, OBSERVERS // devices, TIME_BINS),...]
    unnamed x46 -> x52, local copies, waits for them, and re-layouts: 9.93 us -> 4.94 us
    ppermute x6 -> x4, waiting for transfers between devices: 6.34 us -> 1.94 us  [sibling(): return lax.ppermute(values, 'azim', [(i, i ^ 1) for i in range(count)])]
    ppermute x6 -> x4, starting transfers between devices: 4.63 us -> 0.73 us  [sibling(): return lax.ppermute(values, 'azim', [(i, i ^ 1) for i in range(count)])]
    squeeze x4 -> x0, local copies, waits for them, and re-layouts: 3.12 us -> none  [the longest x2 1.7 us: per_device(): jnp.asarray(halves(own))[place]]
    add x4 -> x0, other arithmetic: 1.31 us -> none  [the longest x2 1.26 us: azim_exchange(): left = left + wide ** (shift - 1) * there[:, 0]]
  transfers between devices with their start and end apart: 18 -> 18, of which waited for: 8 -> 8; matrix products, arithmetic and copies ran while one was open for 5% -> 2% of each run, Pallas kernels for 10% -> 14%
where the time goes in v2:
time: 107 us; the launch traced here: 106 us
  waiting for transfers between devices  39.9 us (37%)
  Pallas kernels  29.4 us (27%)
  starting transfers between devices  28.5 us (27%)
  local copies, waits for them, and re-layouts  5.59 us (5%)
  other arithmetic  2.2 us (2%)
    ppermute x12, waiting for transfers between devices, rotate(): lax.ppermute(values, axis, [(i, (i + shift) % count) for i in range(count)])  37.5 us
    ppermute x12, starting transfers between devices, rotate(): lax.ppermute(values, axis, [(i, (i + shift) % count) for i in range(count)])  20.6 us
    pallas_call x7, Pallas kernels, call(): pl.pallas_call(kernel, grid_spec=pltpu.PrefetchScalarGridSpec(num_scalar_...  19.6 us
    unnamed x52, local copies, waits for them, and re-layouts  4.94 us
    pallas_call x1, Pallas kernels, per_device(): pl.pallas_call(signals_kernel, grid_spec=pltpu.PrefetchScalarGridSpec(num...  4.65 us
    all_to_all x1, starting transfers between devices, per_device(): lax.all_to_all(partial.reshape(devices, OBSERVERS // devices, TIME_BINS),...  3.77 us
    all_to_all x1, starting transfers between devices, per_device(): lax.all_to_all(jnp.broadcast_to(front[None], (devices, rows, lanes)), ('a...  3.42 us
  transfers between devices with their start and end apart: 18, of which 8 were waited for; matrix products, arithmetic and copies ran while one was open for 2% of the time, Pallas kernels for 14%

profile of v2, /device:TPU:0, one launch (start us, length us, event | category | flops | bytes accessed | tf_op | source)
XLA Modules:
  0.0 106.4 jit_solution(15049830204447068427)
XLA Ops:
  1.3 4.7 %azim_flux.1.mine = f32[4,4,5,16,128]{4,3,2,1,0:T(8,128)} custom-call(s32[3]{0:T(128)} %pad_add_fusion.place.at, f32[64,8,128]{2,1,0:T(8,128)} %refs_0_.1, f32[3,64,8,128]{3,2,1,0:T(8,128)} %refs_1_.2, f32[64,8,128]{2,1,0:T(8,128)} %refs_2_.1, f32[3,64,8,128]{3,2,1,0:T(8,128)} %refs_3_.1, f32[64,8,128]{2,1,0:T(8,128)} %refs_4_.1), custom_call_target="tpu_custom_call" | custom-call | flops 6553600 | bytes 2621440 | tf_op jit(solution)/shard_map/azim_flux/pallas_call | solution.py:569
  6.5 1.9 %collective-permute-done.other.sib_pack = f32[4,4,5,16,128]{4,3,2,1,0:T(8,128)S(1)} collective-permute-done((f32[4,4,5,16,128]{4,3,2,1,0:T(8,128)}, f32[4,4,5,16,128]{4,3,2,1,0:T(8,128)S(1)}, u32[]{:S(2)}, u32[]{:S(2)}) %collective-permute-start) | collective-permute-done | bytes 655392 | tf_op jit(solution)/shard_map/ppermute | solution.py:450
  10.2 3.0 %collective-permute-start.1 = (f32[2,3,5,16,128]{4,3,2,1,0:T(8,128)S(1)}, f32[2,3,5,16,128]{4,3,2,1,0:T(8,128)S(1)}, u32[]{:S(2)}, u32[]{:S(2)}) collective-permute-start(f32[2,3,5,16,128]{4,3,2,1,0:T(8,128)S(1)} %get-tuple-element.23), channel_id=1, source_target_pairs={{0,2},{1,3},{2,4},{3,5},{4,6},{5,7},{6,0},{7,1},{8,10},{9,11},{10,... | collective-permute-start | bytes 737288 | tf_op jit(solution)/shard_map/ppermute | solution.py:446
  13.2 2.1 %collective-permute-start.2 = (f32[2,3,5,16,128]{4,3,2,1,0:T(8,128)S(1)}, f32[2,3,5,16,128]{4,3,2,1,0:T(8,128)S(1)}, u32[]{:S(2)}, u32[]{:S(2)}) collective-permute-start(f32[2,3,5,16,128]{4,3,2,1,0:T(8,128)S(1)} %get-tuple-element.24), channel_id=1, source_target_pairs={{0,6},{1,7},{2,0},{3,1},{4,2},{5,3},{6,4},{7,5},{8,14},{9,15},{10,... | collective-permute-start | bytes 737288 | tf_op jit(solution)/shard_map/ppermute | solution.py:446
  16.2 17.5 %collective-permute-done.3.rest_0_ = f32[2,2,5,16,128]{4,3,2,1,0:T(8,128)S(1)} collective-permute-done((f32[2,2,5,16,128]{4,3,2,1,0:T(8,128)S(1)}, f32[2,2,5,16,128]{4,3,2,1,0:T(8,128)S(1)}, u32[]{:S(2)}, u32[]{:S(2)}) %collective-permute-start.3) | collective-permute-done | bytes 163872 | tf_op jit(solution)/shard_map/ppermute | solution.py:446
  34.6 3.3 %section_local.1 = (f32[4,5,8,16,128]{4,3,2,1,0:T(8,128)S(1)}, f32[4,8,16,128]{3,2,1,0:T(8,128)S(1)}, f32[8,2560]{1,0:T(8,128)S(1)}) custom-call(s32[3]{0:T(128)S(1)} %copy-done.15, f32[64,8,128]{2,1,0:T(8,128)S(1)} %copy-done.6, f32[3,64,8,128]{3,2,1,0:T(8,128)S(1)} %copy-done, f32[64,8,128]{2,1,0:T(8,128)S(1)} %copy-done.7, ...), custom_call_target="tpu_custom_call" | custom-call | flops 262144000 | bytes 6553600 | tf_op jit(solution)/shard_map/section_local/pallas_call | solution.py:569
  37.9 1.5 %collective-permute-start.5 = (f32[8,2560]{1,0:T(8,128)S(1)}, f32[8,2560]{1,0:T(8,128)S(1)}, u32[]{:S(2)}, u32[]{:S(2)}) collective-permute-start(f32[8,2560]{1,0:T(8,128)S(1)} %get-tuple-element.27), channel_id=1, source_target_pairs={{0,8},{8,16},{16,24},{24,0},{1,9},{9,17},{17,25},{25,1},{2,10},{10... | collective-permute-start | bytes 245768 | tf_op jit(solution)/shard_map/ppermute | solution.py:446
  39.4 1.5 %collective-permute-start.6 = (f32[8,2560]{1,0:T(8,128)S(1)}, f32[8,2560]{1,0:T(8,128)S(1)}, u32[]{:S(2)}, u32[]{:S(2)}) collective-permute-start(f32[8,2560]{1,0:T(8,128)S(1)} %get-tuple-element.27), channel_id=1, source_target_pairs={{0,16},{8,24},{16,0},{24,8},{1,17},{9,25},{17,1},{25,9},{2,18},{10... | collective-permute-start | bytes 245768 | tf_op jit(solution)/shard_map/ppermute | solution.py:446
  42.4 1.5 %collective-permute-done.5.rest_0_ = f32[8,2560]{1,0:T(8,128)S(1)} collective-permute-done((f32[8,2560]{1,0:T(8,128)S(1)}, f32[8,2560]{1,0:T(8,128)S(1)}, u32[]{:S(2)}, u32[]{:S(2)}) %collective-permute-start.5) | collective-permute-done | bytes 81952 | tf_op jit(solution)/shard_map/ppermute | solution.py:446
  43.9 1.5 %collective-permute-done.6.rest_1_ = f32[8,2560]{1,0:T(8,128)S(1)} collective-permute-done((f32[8,2560]{1,0:T(8,128)S(1)}, f32[8,2560]{1,0:T(8,128)S(1)}, u32[]{:S(2)}, u32[]{:S(2)}) %collective-permute-start.6) | collective-permute-done | bytes 81952 | tf_op jit(solution)/shard_map/ppermute | solution.py:446
  45.5 4.3 %section_join.1 = (f32[4,5,8,16,128]{4,3,2,1,0:T(8,128)S(1)}, f32[8,2560]{1,0:T(8,128)S(1)}, f32[8,128]{1,0:T(8,128)S(1)}) custom-call(s32[3]{0:T(128)S(1)} %copy-done.15, f32[4,5,8,16,128]{4,3,2,1,0:T(8,128)S(1)} %get-tuple-element.20.base, f32[4,8,16,128]{3,2,1,0:T(8,128)S(1)} %get-tuple-element.21.scale, f32[2,3,5,16,128]{4,3,2,1,0:T(8,128)S(1)} %get-tuple-element.25.own, ...), custom_call_target="tpu_custom_call" | custom-call | flops 32768000 | bytes 3145728 | tf_op jit(solution)/shard_map/section_join/pallas_call | solution.py:569
  49.8 2.3 %collective-permute-start.10 = (f32[8,2560]{1,0:T(8,128)S(1)}, f32[8,2560]{1,0:T(8,128)S(1)}, u32[]{:S(2)}, u32[]{:S(2)}) collective-permute-start(f32[8,2560]{1,0:T(8,128)S(1)} %get-tuple-element.29), channel_id=1, source_target_pairs={{0,24},{8,0},{16,8},{24,16},{1,25},{9,1},{17,9},{25,17},{2,26},{10... | collective-permute-start | bytes 245768 | tf_op jit(solution)/shard_map/ppermute | solution.py:446
  53.3 1.7 %axial_local.1.refs_0_ = f32[4,5,8,16,128]{4,3,2,1,0:T(8,128)S(1)} custom-call(s32[3]{0:T(128)S(1)} %copy-done.15, f32[4,5,8,16,128]{4,3,2,1,0:T(8,128)S(1)} %get-tuple-element.28.values, bf16[4,2,128,128]{3,2,1,0:T(8,128)(2,1)S(1)} %copy-done.11), custom_call_target="tpu_custom_call" | custom-call | flops 262144000 | bytes 2621440 | tf_op jit(solution)/shard_map/axial_local/pallas_call | solution.py:569
  55.1 2.4 %collective-permute-done.8.refs_2_ = f32[8,2560]{1,0:T(8,128)S(1)} collective-permute-done((f32[8,2560]{1,0:T(8,128)S(1)}, f32[8,2560]{1,0:T(8,128)S(1)}, u32[]{:S(2)}, u32[]{:S(2)}) %collective-permute-start.8) | collective-permute-done | bytes 81952 | tf_op jit(solution)/shard_map/ppermute | solution.py:446
  57.6 1.9 %axial_join.1 = (f32[4,5,8,16,128]{4,3,2,1,0:T(8,128)S(1)}, f32[4,6,5,16,128]{4,3,2,1,0:T(8,128)S(1)}) custom-call(s32[3]{0:T(128)S(1)} %copy-done.15, f32[4,5,8,16,128]{4,3,2,1,0:T(8,128)S(1)} %axial_local.1.refs_0_, bf16[4,2,24,128]{3,2,1,0:T(8,128)(2,1)S(1)} %copy-done.16, f32[8,2560]{1,0:T(8,128)S(1)} %collective-permute-done.8.refs_2_, ...), custom_call_target="tpu_custom_call" | custom-call | flops 32768000 | bytes 3145728 | tf_op jit(solution)/shard_map/axial_join/pallas_call | solution.py:569
  61.3 3.4 %all-to-all-start = ((f32[32,8,128]{2,1,0:T(8,128)}), f32[32,8,128]{2,1,0:T(8,128)S(1)}, u32[]{:S(2)}, u32[]{:S(2)}) async-start(f32[32,8,128]{2,1,0:T(8,128)} %broadcast_in_dim.2), calls=%async_computation | async-start | bytes 262144 | tf_op jit(solution)/shard_map/all_to_all | solution.py:654
  66.9 1.8 %collective-permute-start.12 = (f32[2,4,5,16,128]{4,3,2,1,0:T(8,128)}, f32[2,4,5,16,128]{4,3,2,1,0:T(8,128)S(1)}, u32[]{:S(2)}, u32[]{:S(2)}) collective-permute-start(f32[2,4,5,16,128]{4,3,2,1,0:T(8,128)} %get-tuple-element.33), channel_id=1, source_target_pairs={{0,2},{1,3},{2,4},{3,5},{4,6},{5,7},{6,0},{7,1},{8,10},{9,11},{10,... | collective-permute-start | bytes 983048 | tf_op jit(solution)/shard_map/ppermute | solution.py:446
  68.7 2.1 %collective-permute-start.13 = (f32[2,4,5,16,128]{4,3,2,1,0:T(8,128)}, f32[2,4,5,16,128]{4,3,2,1,0:T(8,128)S(1)}, u32[]{:S(2)}, u32[]{:S(2)}) collective-permute-start(f32[2,4,5,16,128]{4,3,2,1,0:T(8,128)} %get-tuple-element.34), channel_id=1, source_target_pairs={{0,6},{1,7},{2,0},{3,1},{4,2},{5,3},{6,4},{7,5},{8,14},{9,15},{10,... | collective-permute-start | bytes 983048 | tf_op jit(solution)/shard_map/ppermute | solution.py:446
  72.9 4.6 %signals.1 = f32[512,128]{1,0:T(8,128)} custom-call(s32[3]{0:T(128)S(1)} %copy-done.15, f32[32,8,128]{2,1,0:T(8,128)S(1)} %all-to-all-done.fronts, f32[8,8,64]{2,1,0:T(8,128)S(1)} %copy-done.18, f32[4,512,128]{2,1,0:T(8,128)S(1)} %copy-done.9, f32[4,8,128]{2,1,0:T(8,128)S(1)} %entry_weights.1.weights, s32[4,8,128]{2,1,0:T(8,128)S(1)} %copy-done.19, ...), custom_call_target="tpu_custom_call" | custom-call | tf_op jit(solution)/shard_map/signals/pallas_call | solution.py:694
  77.6 3.8 %all-to-all-start.1 = ((f32[32,16,128]{2,1,0:T(8,128)}), f32[32,16,128]{2,1,0:T(8,128)}, u32[]{:S(2)}, u32[]{:S(2)}) async-start(f32[32,16,128]{2,1,0:T(8,128)} %bitcast.3), calls=%async_computation.1 | async-start | bytes 524288 | tf_op jit(solution)/shard_map/all_to_all | solution.py:713
  81.4 2.7 %collective-permute-start.14 = (f32[2,2,5,16,128]{4,3,2,1,0:T(8,128)S(1)}, f32[2,2,5,16,128]{4,3,2,1,0:T(8,128)S(1)}, u32[]{:S(2)}, u32[]{:S(2)}) collective-permute-start(f32[2,2,5,16,128]{4,3,2,1,0:T(8,128)S(1)} %copy-done.14), channel_id=1, source_target_pairs={{0,4},{1,5},{2,6},{3,7},{4,0},{5,1},{6,2},{7,3},{8,12},{9,13},{10,... | collective-permute-start | bytes 491528 | tf_op jit(solution)/shard_map/ppermute | solution.py:446
  84.0 14.4 %collective-permute-done.14.rest_0_ = f32[2,2,5,16,128]{4,3,2,1,0:T(8,128)S(1)} collective-permute-done((f32[2,2,5,16,128]{4,3,2,1,0:T(8,128)S(1)}, f32[2,2,5,16,128]{4,3,2,1,0:T(8,128)S(1)}, u32[]{:S(2)}, u32[]{:S(2)}) %collective-permute-start.14) | collective-permute-done | bytes 163872 | tf_op jit(solution)/shard_map/ppermute | solution.py:446
  102.4 1.6 %reduce_sum.9 = f32[16,128]{1,0:T(8,128)} reduce(f32[32,16,128]{2,1,0:T(8,128)} %all-to-all-done.1, f32[]{:T(128)} %constant.38.clone.1), dimensions={0}, to_apply=%region_0.1 | reduce | flops 63488 | bytes 270340 | tf_op jit(solution)/shard_map/reduce_sum | solution.py:720
  104.0 2.5 %azim_join.1 = f32[5,64,8,128]{3,2,1,0:T(8,128)} custom-call(s32[3]{0:T(128)S(1)} %copy-done.15, f32[4,5,8,16,128]{4,3,2,1,0:T(8,128)S(1)} %azim_local.1.local, f32[2,4,5,16,128]{4,3,2,1,0:T(8,128)S(1)} %get-tuple-element.35.own, f32[2,4,5,16,128]{4,3,2,1,0:T(8,128)S(1)} %collective-permute-done.15.sib, ...), custom_call_target="tpu_custom_call" | custom-call | flops 6553600 | bytes 3145728 | tf_op jit(solution)/shard_map/azim_join/pallas_call | solution.py:569
  (80 shorter events, 17.4 us)
Async XLA Ops:
  1.3 33.3 %copy-start.5 = (f32[5,64,8,128]{3,2,1,0:T(8,128)S(1)}, f32[5,64,8,128]{3,2,1,0:T(8,128)}, u32[]{:S(2)}) copy-start(f32[5,64,8,128]{3,2,1,0:T(8,128)} %radial.1) | copy-start | bytes 3932164
  1.3 33.3 %copy-start.6 = (f32[64,8,128]{2,1,0:T(8,128)S(1)}, f32[64,8,128]{2,1,0:T(8,128)}, u32[]{:S(2)}) copy-start(f32[64,8,128]{2,1,0:T(8,128)} %refs_0_.1) | copy-start | bytes 786436
  1.3 33.3 %copy-start.7 = (f32[64,8,128]{2,1,0:T(8,128)S(1)}, f32[64,8,128]{2,1,0:T(8,128)}, u32[]{:S(2)}) copy-start(f32[64,8,128]{2,1,0:T(8,128)} %refs_2_.1) | copy-start | bytes 786436
  1.3 33.3 %copy-start.8 = (f32[64,8,128]{2,1,0:T(8,128)S(1)}, f32[64,8,128]{2,1,0:T(8,128)}, u32[]{:S(2)}) copy-start(f32[64,8,128]{2,1,0:T(8,128)} %refs_4_.1) | copy-start | bytes 786436
  1.3 33.3 %copy-start.10 = (f32[3,64,8,128]{3,2,1,0:T(8,128)S(1)}, f32[3,64,8,128]{3,2,1,0:T(8,128)}, u32[]{:S(2)}) copy-start(f32[3,64,8,128]{3,2,1,0:T(8,128)} %axial_metric.1) | copy-start | bytes 2359300
  1.3 33.3 %copy-start.24 = (bf16[2,8,128]{2,1,0:T(8,128)(2,1)S(1)}, bf16[2,8,128]{2,1,0:T(8,128)(2,1)}, u32[]{:S(2)}) copy-start(bf16[2,8,128]{2,1,0:T(8,128)(2,1)} %constant.40.clone.basis) | copy-start | bytes 12292
  6.0 2.4 %collective-permute-start = (f32[4,4,5,16,128]{4,3,2,1,0:T(8,128)}, f32[4,4,5,16,128]{4,3,2,1,0:T(8,128)S(1)}, u32[]{:S(2)}, u32[]{:S(2)}) collective-permute-start(f32[4,4,5,16,128]{4,3,2,1,0:T(8,128)} %azim_flux.1.mine), channel_id=1, source_target_pairs={{0,1},{1,0},{2,3},{3,2},{4,5},{5,4},{6,7},{7,6},{8,9},{9,8},{10,11... | collective-permute-start | bytes 1966088 | tf_op jit(solution)/shard_map/ppermute | solution.py:450
  10.2 23.6 %collective-permute-start.1 = (f32[2,3,5,16,128]{4,3,2,1,0:T(8,128)S(1)}, f32[2,3,5,16,128]{4,3,2,1,0:T(8,128)S(1)}, u32[]{:S(2)}, u32[]{:S(2)}) collective-permute-start(f32[2,3,5,16,128]{4,3,2,1,0:T(8,128)S(1)} %get-tuple-element.23), channel_id=1, source_target_pairs={{0,2},{1,3},{2,4},{3,5},{4,6},{5,7},{6,0},{7,1},{8,10},{9,11},{10,... | collective-permute-start | bytes 737288 | tf_op jit(solution)/shard_map/ppermute | solution.py:446
  13.2 20.6 %collective-permute-start.2 = (f32[2,3,5,16,128]{4,3,2,1,0:T(8,128)S(1)}, f32[2,3,5,16,128]{4,3,2,1,0:T(8,128)S(1)}, u32[]{:S(2)}, u32[]{:S(2)}) collective-permute-start(f32[2,3,5,16,128]{4,3,2,1,0:T(8,128)S(1)} %get-tuple-element.24), channel_id=1, source_target_pairs={{0,6},{1,7},{2,0},{3,1},{4,2},{5,3},{6,4},{7,5},{8,14},{9,15},{10,... | collective-permute-start | bytes 737288 | tf_op jit(solution)/shard_map/ppermute | solution.py:446
  15.3 18.5 %collective-permute-start.3 = (f32[2,2,5,16,128]{4,3,2,1,0:T(8,128)S(1)}, f32[2,2,5,16,128]{4,3,2,1,0:T(8,128)S(1)}, u32[]{:S(2)}, u32[]{:S(2)}) collective-permute-start(f32[2,2,5,16,128]{4,3,2,1,0:T(8,128)S(1)} %get-tuple-element.22.own), channel_id=1, source_target_pairs={{0,4},{1,5},{2,6},{3,7},{4,0},{5,1},{6,2},{7,3},{8,12},{9,13},{10,... | collective-permute-start | bytes 491528 | tf_op jit(solution)/shard_map/ppermute | solution.py:446
  34.4 11.0 %collective-permute-start.4 = (f32[2,3,5,16,128]{4,3,2,1,0:T(8,128)S(1)}, f32[2,3,5,16,128]{4,3,2,1,0:T(8,128)S(1)}, u32[]{:S(2)}, u32[]{:S(2)}) collective-permute-start(f32[2,3,5,16,128]{4,3,2,1,0:T(8,128)S(1)} %get-tuple-element.26), channel_id=1, source_target_pairs={{0,1},{1,0},{2,3},{3,2},{4,5},{5,4},{6,7},{7,6},{8,9},{9,8},{10,11... | collective-permute-start | bytes 737288 | tf_op jit(solution)/shard_map/ppermute | solution.py:450
  37.9 6.0 %collective-permute-start.5 = (f32[8,2560]{1,0:T(8,128)S(1)}, f32[8,2560]{1,0:T(8,128)S(1)}, u32[]{:S(2)}, u32[]{:S(2)}) collective-permute-start(f32[8,2560]{1,0:T(8,128)S(1)} %get-tuple-element.27), channel_id=1, source_target_pairs={{0,8},{8,16},{16,24},{24,0},{1,9},{9,17},{17,25},{25,1},{2,10},{10... | collective-permute-start | bytes 245768 | tf_op jit(solution)/shard_map/ppermute | solution.py:446
  39.4 6.0 %collective-permute-start.6 = (f32[8,2560]{1,0:T(8,128)S(1)}, f32[8,2560]{1,0:T(8,128)S(1)}, u32[]{:S(2)}, u32[]{:S(2)}) collective-permute-start(f32[8,2560]{1,0:T(8,128)S(1)} %get-tuple-element.27), channel_id=1, source_target_pairs={{0,16},{8,24},{16,0},{24,8},{1,17},{9,25},{17,1},{25,9},{2,18},{10... | collective-permute-start | bytes 245768 | tf_op jit(solution)/shard_map/ppermute | solution.py:446
  41.0 4.5 %collective-permute-start.7 = (f32[8,2560]{1,0:T(8,128)S(1)}, f32[8,2560]{1,0:T(8,128)S(1)}, u32[]{:S(2)}, u32[]{:S(2)}) collective-permute-start(f32[8,2560]{1,0:T(8,128)S(1)} %get-tuple-element.27), channel_id=1, source_target_pairs={{0,24},{8,0},{16,8},{24,16},{1,25},{9,1},{17,9},{25,17},{2,26},{10... | collective-permute-start | bytes 245768 | tf_op jit(solution)/shard_map/ppermute | solution.py:446
  49.8 5.3 %collective-permute-start.10 = (f32[8,2560]{1,0:T(8,128)S(1)}, f32[8,2560]{1,0:T(8,128)S(1)}, u32[]{:S(2)}, u32[]{:S(2)}) collective-permute-start(f32[8,2560]{1,0:T(8,128)S(1)} %get-tuple-element.29), channel_id=1, source_target_pairs={{0,24},{8,0},{16,8},{24,16},{1,25},{9,1},{17,9},{25,17},{2,26},{10... | collective-permute-start | bytes 245768 | tf_op jit(solution)/shard_map/ppermute | solution.py:446
  52.1 5.4 %collective-permute-start.8 = (f32[8,2560]{1,0:T(8,128)S(1)}, f32[8,2560]{1,0:T(8,128)S(1)}, u32[]{:S(2)}, u32[]{:S(2)}) collective-permute-start(f32[8,2560]{1,0:T(8,128)S(1)} %get-tuple-element.29), channel_id=1, source_target_pairs={{0,8},{8,16},{16,24},{24,0},{1,9},{9,17},{17,25},{25,1},{2,10},{10... | collective-permute-start | bytes 245768 | tf_op jit(solution)/shard_map/ppermute | solution.py:446
  52.1 5.5 %collective-permute-start.9 = (f32[8,2560]{1,0:T(8,128)S(1)}, f32[8,2560]{1,0:T(8,128)S(1)}, u32[]{:S(2)}, u32[]{:S(2)}) collective-permute-start(f32[8,2560]{1,0:T(8,128)S(1)} %get-tuple-element.29), channel_id=1, source_target_pairs={{0,16},{8,24},{16,0},{24,8},{1,17},{9,25},{17,1},{25,9},{2,18},{10... | collective-permute-start | bytes 245768 | tf_op jit(solution)/shard_map/ppermute | solution.py:446
  60.6 4.2 %collective-permute-start.11 = (f32[4,6,5,16,128]{4,3,2,1,0:T(8,128)S(1)}, f32[4,6,5,16,128]{4,3,2,1,0:T(8,128)S(1)}, u32[]{:S(2)}, u32[]{:S(2)}) collective-permute-start(f32[4,6,5,16,128]{4,3,2,1,0:T(8,128)S(1)} %get-tuple-element.31.mine), channel_id=1, source_target_pairs={{0,1},{1,0},{2,3},{3,2},{4,5},{5,4},{6,7},{7,6},{8,9},{9,8},{10,11... | collective-permute-start | bytes 2949128 | tf_op jit(solution)/shard_map/ppermute | solution.py:450
  61.3 11.6 %all-to-all-start = ((f32[32,8,128]{2,1,0:T(8,128)}), f32[32,8,128]{2,1,0:T(8,128)S(1)}, u32[]{:S(2)}, u32[]{:S(2)}) async-start(f32[32,8,128]{2,1,0:T(8,128)} %broadcast_in_dim.2), calls=%async_computation | async-start | bytes 262144 | tf_op jit(solution)/shard_map/all_to_all | solution.py:654
  66.9 31.5 %collective-permute-start.12 = (f32[2,4,5,16,128]{4,3,2,1,0:T(8,128)}, f32[2,4,5,16,128]{4,3,2,1,0:T(8,128)S(1)}, u32[]{:S(2)}, u32[]{:S(2)}) collective-permute-start(f32[2,4,5,16,128]{4,3,2,1,0:T(8,128)} %get-tuple-element.33), channel_id=1, source_target_pairs={{0,2},{1,3},{2,4},{3,5},{4,6},{5,7},{6,0},{7,1},{8,10},{9,11},{10,... | collective-permute-start | bytes 983048 | tf_op jit(solution)/shard_map/ppermute | solution.py:446
  68.7 29.8 %collective-permute-start.13 = (f32[2,4,5,16,128]{4,3,2,1,0:T(8,128)}, f32[2,4,5,16,128]{4,3,2,1,0:T(8,128)S(1)}, u32[]{:S(2)}, u32[]{:S(2)}) collective-permute-start(f32[2,4,5,16,128]{4,3,2,1,0:T(8,128)} %get-tuple-element.34), channel_id=1, source_target_pairs={{0,6},{1,7},{2,0},{3,1},{4,2},{5,3},{6,4},{7,5},{8,14},{9,15},{10,... | collective-permute-start | bytes 983048 | tf_op jit(solution)/shard_map/ppermute | solution.py:446
  77.6 24.8 %all-to-all-start.1 = ((f32[32,16,128]{2,1,0:T(8,128)}), f32[32,16,128]{2,1,0:T(8,128)}, u32[]{:S(2)}, u32[]{:S(2)}) async-start(f32[32,16,128]{2,1,0:T(8,128)} %bitcast.3), calls=%async_computation.1 | async-start | bytes 524288 | tf_op jit(solution)/shard_map/all_to_all | solution.py:713
  81.4 17.1 %collective-permute-start.14 = (f32[2,2,5,16,128]{4,3,2,1,0:T(8,128)S(1)}, f32[2,2,5,16,128]{4,3,2,1,0:T(8,128)S(1)}, u32[]{:S(2)}, u32[]{:S(2)}) collective-permute-start(f32[2,2,5,16,128]{4,3,2,1,0:T(8,128)S(1)} %copy-done.14), channel_id=1, source_target_pairs={{0,4},{1,5},{2,6},{3,7},{4,0},{5,1},{6,2},{7,3},{8,12},{9,13},{10,... | collective-permute-start | bytes 491528 | tf_op jit(solution)/shard_map/ppermute | solution.py:446
  99.8 4.2 %collective-permute-start.15 = (f32[2,4,5,16,128]{4,3,2,1,0:T(8,128)}, f32[2,4,5,16,128]{4,3,2,1,0:T(8,128)S(1)}, u32[]{:S(2)}, u32[]{:S(2)}) collective-permute-start(f32[2,4,5,16,128]{4,3,2,1,0:T(8,128)} %get-tuple-element.36), channel_id=1, source_target_pairs={{0,1},{1,0},{2,3},{3,2},{4,5},{5,4},{6,7},{7,6},{8,9},{9,8},{10,11... | collective-permute-start | bytes 983048 | tf_op jit(solution)/shard_map/ppermute | solution.py:450
  (20 other events, 212.8 us)

commit v3 on v0

v3 whole, which is shorter than its diff:
```python
import functools
import math

import jax
import jax.numpy as jnp
import numpy as np
from jax import lax
from jax.experimental import pallas as pl
from jax.experimental.pallas import tpu as pltpu
from jax.sharding import PartitionSpec as P

OBSERVERS = 512
TIME_BINS = 128

GAMMA = 1.4
SECTION = 0.25
DERIV_ALPHA = 1.0 / 3.0
FILTER_ALPHA = 0.499
FIELDS = 5
BASIS = 8
VMEM_LIMIT = 16 * 1024 * 1024
INPUT_LIMIT = 60 * 1024 * 1024


def decay_root(alpha):
    return (-1.0 + math.sqrt(1.0 - 4.0 * alpha * alpha)) / (2.0 * alpha)


DERIV_ROOT = decay_root(DERIV_ALPHA)
FILTER_ROOT = decay_root(FILTER_ALPHA)

DERIV_NEAR = 1.0 / 12.0
DERIV_FAR = (
    (25.0 / 36.0) * (DERIV_ROOT - 1.0 / DERIV_ROOT) / (1.0 + 2.0 * DERIV_ALPHA * DERIV_ROOT)
)

_B = FILTER_ALPHA
_EDGE = (1.0 - 2.0 * _B) / 64.0
_Q2 = 1.0 / _B
_Q1 = (-6.0 - _Q2) / _B
_Q0 = (12.0 - _Q1) / _B
_RHO = -8.0 - _Q0
FILTER_MID = _EDGE * (_Q0 + 2.0 * _Q2)
FILTER_ONE = _EDGE * _Q1
FILTER_TWO = _EDGE * _Q2
FILTER_FAR = _EDGE * _RHO / (1.0 + 2.0 * _B * FILTER_ROOT)


def open_operator(length, alpha, side):
    base = decay_root(alpha)
    tri = np.eye(length) + alpha * (np.eye(length, k=1) + np.eye(length, k=-1))
    tri[0, 0] = -alpha / base
    return np.linalg.solve(tri, side)


def deriv_matrix(length):
    return (7.0 / 9.0) * (np.eye(length, k=1) - np.eye(length, k=-1)) + (1.0 / 36.0) * (
        np.eye(length, k=2) - np.eye(length, k=-2)
    )


def filter_matrix(length):
    beta = FILTER_ALPHA
    coeffs = [
        (11.0 + 10.0 * beta) / 16.0,
        (15.0 + 34.0 * beta) / 32.0,
        (-3.0 + 6.0 * beta) / 16.0,
        (1.0 - 2.0 * beta) / 32.0,
    ]
    total = coeffs[0] * np.eye(length)
    for shift in range(1, 4):
        total = total + 0.5 * coeffs[shift] * (np.eye(length, k=shift) + np.eye(length, k=-shift))
    return total


def axial_tables(count, width, alpha, kind):
    length = count * width
    side = deriv_matrix(length) if kind == "deriv" else filter_matrix(length)
    whole = open_operator(length, alpha, side)
    base = decay_root(alpha)
    basis = np.zeros((BASIS, width))
    for edge in range(3):
        basis[edge, edge] = 1.0
        basis[3 + edge, width - 3 + edge] = 1.0
    basis[6] = base ** np.arange(width - 1, -1, -1, dtype=np.float64)
    basis[7] = base ** np.arange(width, dtype=np.float64)
    inverse = np.linalg.pinv(basis)
    own = np.zeros((count, width, width))
    far = np.zeros((count, max(count - 1, 1) * BASIS, width))
    for here in range(count):
        rows = whole[here * width : (here + 1) * width]
        own[here] = rows[:, here * width : (here + 1) * width].T
        if kind == "filter":
            own[here] -= np.eye(width)
        for shift in range(1, count):
            there = (here - shift) % count
            block = rows[:, there * width : (there + 1) * width]
            far[here, (shift - 1) * BASIS : shift * BASIS] = (block @ inverse).T
    return own, basis, far


def cycle_operator(length, alpha, coeffs, sign):
    turn = np.roll(np.eye(length), 1, axis=1)
    side = coeffs[0] * np.eye(length)
    for shift in range(1, len(coeffs)):
        step = np.linalg.matrix_power(turn, shift)
        side = side + coeffs[shift] * (step + sign * step.T)
    return np.linalg.solve(np.eye(length) + alpha * (turn + turn.T), side)


def surface_tables(along, width, around, rows):
    length, ring = along * width, around * rows
    deriv_along = open_operator(length, DERIV_ALPHA, deriv_matrix(length)).T
    deriv_around = cycle_operator(ring, DERIV_ALPHA, [0.0, 7.0 / 9.0, 1.0 / 36.0], -1.0)
    filter_along = open_operator(length, FILTER_ALPHA, filter_matrix(length))
    filter_along = filter_along.reshape(along, width, length).transpose(0, 2, 1)
    beta = FILTER_ALPHA
    coeffs = [
        (11.0 + 10.0 * beta) / 16.0,
        (15.0 + 34.0 * beta) / 64.0,
        (-3.0 + 6.0 * beta) / 32.0,
        (1.0 - 2.0 * beta) / 64.0,
    ]
    filter_around = cycle_operator(ring, beta, coeffs, 1.0).reshape(around, rows, ring)
    return (
        halves(deriv_along),
        halves(deriv_around),
        filter_along.astype(np.float32),
        filter_around.astype(np.float32),
    )


def halves(table):
    high = np.asarray(table, np.float32).astype(jnp.bfloat16)
    low = (np.asarray(table, np.float64) - high.astype(np.float64)).astype(jnp.bfloat16)
    return np.stack([high, low], axis=-3)


def split(values):
    high = values.astype(jnp.bfloat16)
    return high, (values - high.astype(jnp.float32)).astype(jnp.bfloat16)


def dots(left, right, dims):
    out = None
    for a, b in ((0, 0), (1, 0), (0, 1)):
        part = lax.dot_general(
            left[a], right[b], (dims, ((), ())), preferred_element_type=jnp.float32
        )
        out = part if out is None else out + part
    return out


def outgoing(basis_ref, lines):
    return dots((basis_ref[0], basis_ref[1]), split(lines), ((1,), (1,)))


def incoming(parts, far_ref):
    return dots(split(jnp.concatenate(parts, axis=0)), (far_ref[0], far_ref[1]), ((0,), (0,)))


def own_block(lines, own_ref):
    return dots(split(lines), (own_ref[0], own_ref[1]), ((1,), (0,)))


def tile_energy(density, velocity, pressure):
    return pressure * (1.0 / (GAMMA - 1.0)) + 0.5 * density * (
        velocity[0] * velocity[0] + velocity[1] * velocity[1] + velocity[2] * velocity[2]
    )


def tile_flux(density, velocity, pressure, energy, metric, volume):
    contra = metric[0] * velocity[0] + metric[1] * velocity[1] + metric[2] * velocity[2]
    volume_contra = volume * contra
    mass = density * volume_contra
    push = volume * pressure
    pieces = [mass]
    for comp in range(3):
        pieces.append(mass * velocity[comp] + metric[comp] * push)
    pieces.append((energy + pressure) * volume_contra)
    return pieces


def core_index():
    return lax.rem(lax.axis_index("azim"), 2)


def chip_index():
    return lax.div(lax.axis_index("azim"), 2)


def ring_weights(chips, turn, wide):
    levels = chips.bit_length() - 1
    size = 2 * (levels + 1)
    sends = np.zeros((levels, 2, chips, size))
    sums = np.zeros((2, chips, size))
    unit = np.eye(size)
    for chip in range(chips):
        spot = (chip + turn) % chips
        head, tail = unit[0], unit[1]
        left = right = np.zeros(size)
        for level in range(levels):
            group = 1 << level
            inside = spot % group
            sends[level, :, chip] = head, tail
            head_in, tail_in = unit[2 * level + 2], unit[2 * level + 3]
            if (spot >> level) & 1:
                left = left + wide**inside * head_in
                head, tail = head + wide**group * head_in, tail_in + wide**group * tail
            else:
                right = right + wide ** (group - 1 - inside) * tail_in
                head, tail = head_in + wide**group * head, tail + wide**group * tail_in
        close = 1.0 / (1.0 - wide**chips)
        sums[0, chip] = left + close * wide**spot * head
        sums[1, chip] = right + close * wide ** (chips - 1 - spot) * tail
    return sends, sums


def chosen(index, values):
    if not np.any(values):
        return None
    out = jnp.float32(values[0])
    for at in range(1, len(values)):
        if values[at] != values[at - 1] or np.any(values != values[0]):
            out = jnp.where(index == at, jnp.float32(values[at]), out)
    return out


def slot(value, field, height):
    start = (value * FIELDS + field) * height
    return slice(start, start + height)


def mixed(chip, table, sources, field, height):
    total = None
    for at, source in enumerate(sources):
        for part in range(2):
            weight = chosen(chip, table[:, 2 * at + part])
            if weight is not None:
                term = weight * source[slot(part, field, height)]
                total = term if total is None else total + term
    return total


def moments(tiles, root):
    head = tail = tiles[0]
    for row in range(1, len(tiles)):
        head = tiles[row] + root * head
        tail = tail + (root**row) * tiles[row]
    return head, tail


def fetched(sources, buffers, sem, pieces):
    copies = [
        [
            pltpu.make_async_copy(source.at[where], buffer.at[there], sem.at[at, n])
            for n, (source, buffer, (where, there)) in enumerate(zip(sources, buffers, piece))
        ]
        for at, piece in enumerate(pieces)
    ]
    for group in copies:
        for copy in group:
            copy.start()
    return copies


def azim_flux_kernel(mine, density, velocity, pressure, azim_metric, volume, out, pack, *scratch):
    *buffers, flux, sem = scratch
    chunks, _, rows, planes, _ = out.shape
    core = core_index()
    start = (core if mine else 1 - core) * chunks * planes
    pieces = []
    for chunk in range(chunks):
        here, there = pl.ds(start + chunk * planes, planes), pl.ds(chunk * planes, planes)
        whole = slice(None)
        pieces.append(
            [(here, there), ((whole, here), (whole, there)), (here, there)]
            + [((whole, here), (whole, there)), (here, there)]
        )
    groups = fetched((density, velocity, pressure, azim_metric, volume), buffers, sem, pieces)
    first = core == 0
    for chunk in range(chunks):
        for copy in groups[chunk]:
            copy.wait()
        rho_in, vel_in, pres_in, metric_in, vol_in = buffers
        for plane in range(planes):
            at = chunk * planes + plane
            rho, pres = rho_in[at], pres_in[at]
            vel = [vel_in[c, at] for c in range(3)]
            energy = tile_energy(rho, vel, pres)
            metric = [metric_in[c, at] for c in range(3)]
            for f, piece in enumerate(tile_flux(rho, vel, pres, energy, metric, vol_in[at])):
                flux[f, plane] = piece
        for f in range(FIELDS):
            turned = jnp.swapaxes(flux[f], 0, 1)
            out[chunk, f] = turned
            tiles = [turned[row] for row in range(rows)]
            pack[chunk, 0, f], pack[chunk, 1, f] = moments(tiles, DERIV_ROOT)
            pack[chunk, 2, f] = jnp.where(first, tiles[0], tiles[rows - 1])


def put_moments(field, head, tail, low, high, held):
    on_left = lax.rem(chip_index() + pl.program_id(0), 2) == 0
    near, height = len(low), head.shape[0]
    held[slot(0, field, height)] = head
    held[slot(1, field, height)] = tail
    for n in range(near):
        held[slot(2 + n, field, height)] = jnp.where(on_left, high[n], low[n])
        held[slot(2 + near + n, field, height)] = jnp.where(on_left, low[n], high[n])


def hand_out(held, pack_a, pack_b, edge_a, edge_b):
    size = held.shape[0] - edge_a.shape[0]
    for turn, (pack, edge) in enumerate(((pack_a, edge_a), (pack_b, edge_b))):

        @pl.when(pl.program_id(0) == turn)
        def _(pack=pack, edge=edge):
            pack[:size] = held[:size]
            edge[...] = held[size:]


def chip_moments_kernel(rows, keep, other, pack_a, pack_b, edge_a, edge_b):
    first = core_index() == 0
    decay, one = jnp.float32(DERIV_ROOT**rows), jnp.float32(1.0)
    near, away = jnp.where(first, decay, one), jnp.where(first, one, decay)
    height = keep.shape[3]
    for turn, (pack, edge) in enumerate(((pack_a, edge_a), (pack_b, edge_b))):
        on_left = lax.rem(chip_index() + turn, 2) == 0
        mine = first != on_left
        for f in range(FIELDS):
            head, tail, row = (keep[turn, n, f] for n in range(3))
            head_in, tail_in, row_in = (other[turn, n, f] for n in range(3))
            pack[slot(0, f, height)] = near * head + away * head_in
            pack[slot(1, f, height)] = away * tail + near * tail_in
            pack[slot(2, f, height)] = jnp.where(mine, row, row_in)
            edge[slot(0, f, height)] = jnp.where(mine, row_in, row)


def totals_kernel(table, joined, near, height, shares, *refs):
    chip = chip_index()
    if shares:
        *refs, held, send_a, send_b, kept = refs
    else:
        *refs, send_a, send_b = refs
    count = len(refs) // 2
    for turn, send in enumerate((send_a, send_b)):
        mine = refs[turn * count : (turn + 1) * count]
        sources = mine[:-1] if joined else mine
        for f in range(FIELDS):
            send[slot(0, f, height)] = mixed(chip, table[turn][0], sources, f, height)
            send[slot(1, f, height)] = mixed(chip, table[turn][1], sources, f, height)
        if joined:
            size = 2 * FIELDS * height
            send[size : size + mine[-1].shape[0]] = mine[-1][...]
        if shares and turn == 0:
            source = sources[-1]
            into = send.shape[0] - kept.shape[0]
            arrived = source.shape[0] - held.shape[0]
            for at in range(held.shape[0] // shares):
                spot = at * shares
                total = held[spot : spot + shares] + source[arrived + spot : arrived + spot + shares]
                there = (at // 2) * shares
                if at % 2:
                    send[into + there : into + there + shares] = total
                else:
                    kept[there : there + shares] = total


def ring_kernel(table, near, height, shares, *refs):
    chip = chip_index()
    if shares:
        *refs, held, out, signals_kept, signals_sent = refs
    else:
        *refs, out = refs
    count = len(refs) // 2
    for turn in range(2):
        *sources, edge = refs[turn * count : (turn + 1) * count]
        on_left = lax.rem(chip + turn, 2) == 0
        start = 0 if edge.shape[0] == near * FIELDS * height else 2
        for f in range(FIELDS):
            out[turn, 0, f] = mixed(chip, table[turn][0], sources, f, height)
            out[turn, 1, f] = mixed(chip, table[turn][1], sources, f, height)
            for n in range(near):
                paired = sources[1][slot(2 + n, f, height)]
                other = edge[slot(start + n, f, height)]
                out[turn, 2 + n, f] = jnp.where(on_left, other, paired)
                out[turn, 2 + near + n, f] = jnp.where(on_left, paired, other)
        if shares and turn == 0:
            source = sources[-1]
            total = held[...] + source[source.shape[0] - shares :]
            half = shares // 2
            first = core_index() == 0
            signals_kept[...] = jnp.where(first, total[:half], total[half:])
            signals_sent[...] = jnp.where(first, total[half:], total[:half])


def section_local_kernel(
    density,
    velocity,
    pressure,
    axial_metric,
    volume,
    radial,
    own,
    basis,
    base_out,
    scale_out,
    edge_out,
    axial_flux,
    start,
):
    planes, rows, lanes = density.shape
    for plane in range(planes):
        rho = density[plane]
        vel = [velocity[c, plane] for c in range(3)]
        pres = pressure[plane]
        vol = volume[plane]
        energy = tile_energy(rho, vel, pres)
        axial = tile_flux(rho, vel, pres, energy, [axial_metric[c, plane] for c in range(3)], vol)
        state = [rho, rho * vel[0], rho * vel[1], rho * vel[2], energy]
        for f in range(FIELDS):
            axial_flux[f, plane] = axial[f]
            start[f, plane] = state[f] + SECTION * radial[f, plane]
    scale = jnp.swapaxes(SECTION / volume[...], 0, 1)
    scale_out[0] = scale
    for f in range(FIELDS):
        flux = jnp.swapaxes(axial_flux[f], 0, 1).reshape(rows * planes, lanes)
        edge_out[:, f * rows * planes : (f + 1) * rows * planes] = outgoing(basis, flux)
        deriv = own_block(flux, own).reshape(rows, planes, lanes)
        base_out[0, f] = jnp.swapaxes(start[f], 0, 1) - scale * deriv


def section_axial_kernel(base, scale, far, *rest):
    edges, out = rest[:-1], rest[-1]
    rows, planes, lanes = scale.shape[1:]
    for f in range(FIELDS):
        spot = slice(f * rows * planes, (f + 1) * rows * planes)
        axial = incoming([ref[:, spot] for ref in edges], far).reshape(rows, planes, lanes)
        out[0, f] = base[0, f] - scale[0] * axial
    out[0, FIELDS] = scale[0]


def section_azim_kernel(flux_keep, flux_in, base_keep, base_in, out, scale_out):
    rows = flux_keep.shape[2]
    first = core_index() == 0

    def both(mine, theirs, f):
        low = [jnp.where(first, mine[0, f, row], theirs[0, f, row]) for row in range(rows)]
        high = [jnp.where(first, theirs[0, f, row], mine[0, f, row]) for row in range(rows)]
        return low + high

    scale = both(base_keep, base_in, FIELDS)
    for row in range(2 * rows):
        scale_out[0, row] = scale[row]
    for f in range(FIELDS):
        azim = both(flux_keep, flux_in, f)
        base = both(base_keep, base_in, f)
        last = 2 * rows - 1
        down = [None] * (last + 1)
        down[last] = azim[last]
        for row in range(last - 1, -1, -1):
            down[row] = azim[row] + DERIV_ROOT * down[row + 1]
        up = None
        for row in range(last + 1):
            up = azim[row] if row == 0 else azim[row] + DERIV_ROOT * up
            total = DERIV_FAR * (up - down[row])
            if row > 0:
                total = total - DERIV_NEAR * azim[row - 1]
            if row < last:
                total = total + DERIV_NEAR * azim[row + 1]
            out[0, f, row] = base[row] - scale_out[0, row] * total


def section_join_kernel(base, scale, ring, basis, partial, out, *edges):
    rows, planes, lanes = scale.shape[1:]
    step = pl.program_id(0)
    width = rows * planes
    for f in range(FIELDS):
        left, right, before, after = (ring[0, n, f] for n in range(4))
        for row in range(rows):
            azim = (DERIV_FAR * DERIV_ROOT ** (row + 1)) * left - (
                DERIV_FAR * DERIV_ROOT ** (rows - row)
            ) * right
            if row == 0:
                azim = azim - DERIV_NEAR * before
            if row == rows - 1:
                azim = azim + DERIV_NEAR * after
            out[0, f, row] = base[0, f, row] - scale[0, row] * azim
        sent = outgoing(basis, out[0, f].reshape(width, lanes))
        spot = pl.multiple_of((step * FIELDS + f) * width, 128)
        for edge in edges:
            edge[:, pl.ds(spot, width)] = sent

    @pl.when(step == 0)
    def _():
        count = len(edges) + 1
        share = partial.shape[0] // count
        for shift, edge in enumerate(edges, start=1):
            owner = lax.rem(lax.axis_index("axial") + shift, count)
            start = edge.shape[1] - share // 8 * lanes
            for at in range(share // 8):
                piece = pl.multiple_of(owner * share + 8 * at, 8)
                edge[:, start + at * lanes : start + (at + 1) * lanes] = partial[pl.ds(piece, 8), :]


def axial_local_kernel(values, own, out):
    lines = values[0].reshape(-1, values.shape[-1])
    out[0] = (lines + own_block(lines, own)).reshape(out.shape[1:])


def mirror_masks(chips):
    return [(2 << level) - 1 for level in range(chips.bit_length() - 1)]


def axial_join_kernel(chips, local, far, partial, *rest):
    edges, (out, *outs, kept, held, summed) = rest[:-8], rest[-8:]
    rows, planes, lanes = local.shape[2:]
    step = pl.program_id(0)
    width = rows * planes
    for f in range(FIELDS):
        spot = pl.multiple_of((step * FIELDS + f) * width, 128)
        axial = incoming([ref[:, pl.ds(spot, width)] for ref in edges], far)
        axial = axial.reshape(rows, planes, lanes)
        tiles = [local[0, f, row] + axial[row] for row in range(rows)]
        for row in range(rows):
            out[0, f, row] = tiles[row]
        head, tail = moments(tiles, FILTER_ROOT)
        put_moments(f, head, tail, tiles[:2], tiles[rows - 2 :], held)
    hand_out(held, *outs)

    @pl.when(step == 0)
    def _():
        share = summed.shape[0]
        start = edges[0].shape[1] - share // 8 * lanes
        mine = lax.axis_index("axial") * share
        for at in range(share // 8):
            total = partial[pl.ds(pl.multiple_of(mine + 8 * at, 8), 8), :]
            for edge in edges:
                total = total + edge[:, start + at * lanes : start + (at + 1) * lanes]
            summed[8 * at : 8 * at + 8] = total
        size = share // chips
        send = outs[0]
        into = send.shape[0] - kept.shape[0]
        masks = mirror_masks(chips)
        for at in range(chips):
            there = chip_index()
            for level, mask in enumerate(masks):
                if (at >> level) & 1:
                    there = jnp.bitwise_xor(there, mask)
            rows_there = summed[pl.ds(pl.multiple_of(there * size, 8), size), :]
            place = (at // 2) * size
            if at % 2:
                send[into + place : into + place + size] = rows_there
            else:
                kept[place : place + size] = rows_there


def azim_local_kernel(values, out):
    rows = values.shape[2]
    for f in range(FIELDS):
        down = [None] * rows
        down[rows - 1] = values[0, f, rows - 1]
        for row in range(rows - 2, -1, -1):
            down[row] = values[0, f, row] + FILTER_ROOT * down[row + 1]
        up = None
        for row in range(rows):
            here = values[0, f, row]
            up = here if row == 0 else here + FILTER_ROOT * up
            total = (1.0 + FILTER_MID - FILTER_FAR) * here + FILTER_FAR * (up + down[row])
            for step, weight in ((1, FILTER_ONE), (2, FILTER_TWO)):
                if row >= step:
                    total = total + weight * values[0, f, row - step]
                if row + step < rows:
                    total = total + weight * values[0, f, row + step]
            out[0, f, row] = total


def joined_rows(upper, local, ring, field):
    rows = local.shape[2]
    one, zero = jnp.float32(1.0), jnp.float32(0.0)
    decay = jnp.float32(FILTER_ROOT**rows)
    left = jnp.where(upper, decay, one) * ring[0, 0, field]
    right = jnp.where(upper, one, decay) * ring[0, 1, field]
    low, high = jnp.where(upper, zero, one), jnp.where(upper, one, zero)
    before = [low * ring[0, 2 + n, field] for n in range(2)]
    after = [high * ring[0, 4 + n, field] for n in range(2)]
    tiles = []
    for row in range(rows):
        total = (
            local[0, field, row]
            + (FILTER_FAR * FILTER_ROOT ** (row + 1)) * left
            + (FILTER_FAR * FILTER_ROOT ** (rows - row)) * right
        )
        if row < 2:
            total = total + FILTER_TWO * before[row]
        if row == 0:
            total = total + FILTER_ONE * before[1]
        if row >= rows - 2:
            total = total + FILTER_TWO * after[row - (rows - 2)]
        if row == rows - 1:
            total = total + FILTER_ONE * after[0]
        tiles.append(total)
    return tiles


def azim_send_kernel(local, ring, signals, out):
    height = local.shape[3]
    for f in range(FIELDS):
        for row, tile in enumerate(joined_rows(core_index() == 0, local, ring, f)):
            start = (f * local.shape[2] + row) * height
            out[0, start : start + height] = tile
    end = FIELDS * local.shape[2] * height
    out[0, end : end + signals.shape[0]] = signals[...]


def azim_keep_kernel(local, ring, out):
    for f in range(FIELDS):
        tiles = joined_rows(core_index() == 1, local, ring, f)
        out[f] = jnp.swapaxes(jnp.stack(tiles), 0, 1)


def place_rows_kernel(values, kept, partial, out, signals):
    planes, rows, lanes = out.shape[1:]
    size = rows * planes
    for f in range(FIELDS):
        turned = values[0, f * size : (f + 1) * size].reshape(rows, planes, lanes)
        out[f] = jnp.swapaxes(turned, 0, 1)
    signals[...] = kept[...] + values[0, FIELDS * size : FIELDS * size + kept.shape[0]]


def front_kernel(
    density, velocity, pressure, axial_metric, azim_metric, volume, radial, out, *scratch
):
    *buffers, sem = scratch
    sources = (density, velocity, pressure, axial_metric, azim_metric, volume, radial)
    whole = slice(None)
    one, many = (pl.ds(0, 1), whole), ((whole, pl.ds(0, 1)), whole)
    (group,) = fetched(sources, buffers, sem, [[one, many, one, many, many, one, many]])
    for copy in group:
        copy.wait()
    rho_in, vel_in, pres_in, axial_in, azim_in, vol_in, radial_in = buffers
    rho, pres, vol = rho_in[0], pres_in[0], vol_in[0]
    vel = [vel_in[c, 0] for c in range(3)]
    energy = tile_energy(rho, vel, pres)
    axial = tile_flux(rho, vel, pres, energy, [axial_in[c, 0] for c in range(3)], vol)
    azim = tile_flux(rho, vel, pres, energy, [azim_in[c, 0] for c in range(3)], vol)
    base = rho + rho * vel[1] + SECTION * (radial_in[0, 0] + radial_in[2, 0])
    for at, piece in enumerate((base, SECTION / vol, axial[0] + axial[2], azim[0] + azim[2])):
        for device in range(out.shape[0]):
            out[device, at] = piece


def signals_kernel(
    fronts,
    deriv_along,
    deriv_around,
    filter_along,
    filter_around,
    weight_table,
    weights,
    area,
    observers,
    bins,
    out,
    *scratch,
):
    *buffers, chosen_rows, chosen_bins, sem = scratch
    sources = (fronts, deriv_along, deriv_around, filter_along, filter_around)
    sources = sources + (weight_table, weights, area, observers, bins)
    whole = slice(None)
    pieces = [(whole, whole)] * len(sources)
    pieces[3] = (lax.axis_index("axial"), whole)
    pieces[4] = (lax.axis_index("azim"), whole)
    (group,) = fetched(sources, buffers, sem, [pieces])
    for copy in group:
        copy.wait()
    fronts, deriv_along, deriv_around, filter_along, filter_around = buffers[:5]
    weight_table, weights, area, observers, bins = buffers[5:]
    entries, rows, lanes = weights.shape
    columns = filter_around.shape[1] // rows
    count = fronts.shape[0] // columns

    def plane(at):
        blocks = [
            jnp.concatenate([fronts[a * columns + c, at] for c in range(columns)], axis=0)
            for a in range(count)
        ]
        return jnp.concatenate(blocks, axis=1)

    base, scale, axial, azim = (plane(at) for at in range(4))
    deriv = dots(split(axial), (deriv_along[0], deriv_along[1]), ((1,), (0,)))
    deriv = deriv + dots((deriv_around[0], deriv_around[1]), split(azim), ((1,), (0,)))
    section = base - scale * deriv
    smooth = jnp.dot(
        filter_around[...],
        section,
        precision=lax.Precision.HIGHEST,
        preferred_element_type=jnp.float32,
    )
    surface = -1.0 + jnp.dot(
        smooth,
        filter_along[...],
        precision=lax.Precision.HIGHEST,
        preferred_element_type=jnp.float32,
    )
    surface = area[...] * surface
    observer_rows = lax.broadcasted_iota(jnp.int32, (out.shape[0], lanes), 0)
    bin_rows = lax.broadcasted_iota(jnp.int32, (out.shape[1], lanes), 0)
    height = out.shape[1]
    for entry in range(entries):
        picked = weights[entry]
        found = jnp.zeros(picked.shape, jnp.float32)
        for t in range(weight_table.shape[0]):
            found = jnp.where(picked == t, weight_table[t], found)
        values = found * surface
        for row in range(rows):
            at = (row * entries + entry) * lanes
            hit = observer_rows == observers[entry, row : row + 1, :]
            chosen_rows[:, at : at + lanes] = jnp.where(hit, 1.0, 0.0).astype(jnp.bfloat16)
            hit = bin_rows == bins[entry, row : row + 1, :]
            high, low = split(jnp.where(hit, values[row : row + 1, :], 0.0))
            chosen_bins[:height, at : at + lanes] = high
            chosen_bins[height:, at : at + lanes] = low
    total = lax.dot_general(
        chosen_rows[...],
        chosen_bins[...],
        (((1,), (1,)), ((), ())),
        preferred_element_type=jnp.float32,
    )
    out[...] = total[:, :height] + total[:, height:]


def params(limit=VMEM_LIMIT):
    return pltpu.CompilerParams(vmem_limit_bytes=limit)


def cost(flops, moved):
    return pl.CostEstimate(flops=1, bytes_accessed=1, transcendentals=0)


def rotate(values, axis, count, shift):
    return lax.ppermute(values, axis, [(i, (i + shift) % count) for i in range(count)])


def sibling(values, count):
    return lax.ppermute(values, "azim", [(i, i ^ 1) for i in range(count)])


def partner(values, count, turn, level):
    chips = count // 2
    pairs = []
    for i in range(count):
        chip, core = divmod(i, 2)
        there = ((((chip + turn) % chips) ^ ((2 << level) - 1)) - turn) % chips
        pairs.append((i, 2 * there + core))
    return lax.ppermute(values, "azim", pairs)


def waiting(kernel, count, wait):
    if not wait:
        return kernel
    return lambda *refs: kernel(*refs[:count], *refs[count + len(wait) :])


def whole_call(kernel, name, shapes, args, wait=()):
    whole = pl.BlockSpec(memory_space=pltpu.VMEM)
    return pl.pallas_call(
        waiting(kernel, len(args), wait),
        in_specs=[whole] * len(args) + [pl.BlockSpec(memory_space=pl.ANY)] * len(wait),
        out_specs=[whole] * len(shapes),
        out_shape=shapes,
        compiler_params=params(),
        cost_estimate=cost(1, 1),
        name=name,
    )(*args, *wait)


def ring_exchange(packs, edges, count, near, height, wide, wait=(), held=None, shares=0):
    chips = count // 2
    levels = chips.bit_length() - 1
    tables = [ring_weights(chips, turn, wide) for turn in range(2)]
    lanes = packs[0].shape[1]
    rows = FIELDS * height
    joined = levels == 2

    def flat(size):
        return jax.ShapeDtypeStruct((size, lanes), jnp.float32)

    sources = [[packs[turn], partner(packs[turn], count, turn, 0)] for turn in range(2)]
    if not joined:
        edges = [partner(edges[turn], count, 1 - turn, 0) for turn in range(2)]
    for level in range(1, levels):
        size = (2 + near if joined else 2) * rows
        args = [a for turn in range(2) for a in sources[turn] + ([edges[turn]] if joined else [])]
        shapes = [flat(size), flat(size)]
        if shares:
            args.append(held)
            left = held.shape[0] // 2
            shapes = [flat(size + left), flat(size), flat(left)]
        sends = whole_call(
            functools.partial(
                totals_kernel, [t[0][level] for t in tables], joined, near, height, shares
            ),
            "group_totals",
            shapes,
            args,
            wait,
        )
        if shares:
            held = sends[2]
        for turn in range(2):
            sources[turn].append(partner(sends[turn], count, turn, level))
    args = [
        a for turn in range(2) for a in sources[turn] + [sources[turn][-1] if joined else edges[turn]]
    ]
    shapes = [jax.ShapeDtypeStruct((2, 2 + 2 * near, FIELDS, height, lanes), jnp.float32)]
    if shares:
        args.append(held)
        shapes = shapes + [flat(shares // 2)] * 2

    def sums(wait=()):
        return whole_call(
            functools.partial(ring_kernel, [t[1] for t in tables], near, height, shares),
            "ring_sums",
            shapes,
            args,
            wait,
        )

    return sums, sends[0]


def per_device(
    density,
    velocity,
    pressure,
    axial_metric,
    azim_metric,
    volume,
    radial_term,
    panel_area,
    observer_ids,
    bin_ids,
    weight_ids,
    bin_weights,
):
    planes, rows, lanes = density.shape
    along = lax.axis_size("axial")
    around = lax.axis_size("azim")
    devices = along * around
    part = planes // 4
    lines = FIELDS * rows * part
    f32 = jnp.float32

    own_d, basis_d, far_d = map(halves, axial_tables(along, lanes, DERIV_ALPHA, "deriv"))
    own_f, basis_f, far_f = map(halves, axial_tables(along, lanes, FILTER_ALPHA, "filter"))
    deriv_along, deriv_around, filter_along, filter_around = surface_tables(
        along, lanes, around, rows
    )

    spec = pl.BlockSpec

    def every(k):
        return k

    def kept(k):
        return core_index() * 2 + k

    def sent(k):
        return (1 - core_index()) * 2 + k

    def field(where):
        return spec((part, rows, lanes), lambda k: (where(k), 0, 0))

    def vector(where, size=3):
        return spec((size, part, rows, lanes), lambda k: (0, where(k), 0, 0))

    def inner(where, size=FIELDS, tall=rows):
        return spec((1, size, tall, part, lanes), lambda k: (where(k), 0, 0, 0, 0))

    def inner_one(where, tall=rows):
        return spec((1, tall, part, lanes), lambda k: (where(k), 0, 0, 0))

    def edge(where, width=lines):
        return spec((BASIS, width), lambda k: (0, where(k)))

    def row_half(upper):
        return spec((1, FIELDS, rows, part, lanes), lambda k: (k, 0, upper(), 0, 0))

    def table(array):
        return spec((None,) + array.shape[1:], lambda k: (lax.axis_index("axial"),) + (0,) * (array.ndim - 1))

    def fixed(shape):
        return spec(shape, lambda k: (0,) * len(shape))

    def ring_spec(near):
        return spec((1, 2 + 2 * near, FIELDS, part, lanes), lambda k: (k, 0, 0, 0, 0))

    def shaped(*shape):
        return jax.ShapeDtypeStruct(shape, f32)

    def call(
        kernel, name, steps, ins, outs, shapes, args, wait=(), limit=VMEM_LIMIT, scratch=(), **more
    ):
        return pl.pallas_call(
            waiting(kernel, len(args), wait),
            grid=(steps,),
            in_specs=ins + [spec(memory_space=pl.ANY)] * len(wait),
            out_specs=outs,
            scratch_shapes=scratch,
            out_shape=shapes,
            compiler_params=params(limit),
            cost_estimate=cost(1, 1),
            name=name,
            **more,
        )(*args, *wait)

    tall = 2 * rows
    flux_scratch = pltpu.VMEM((FIELDS, part, rows, lanes), f32)
    half_shape = shaped(2, FIELDS, rows, part, lanes)
    chip_shape = shaped(2, FIELDS, tall, part, lanes)

    def apart(kernel, name, shapes, args, scratch, wait=(), limit=INPUT_LIMIT):
        several = isinstance(shapes, list)
        vmem = spec(memory_space=pltpu.VMEM)
        return pl.pallas_call(
            waiting(kernel, len(args), wait),
            in_specs=[spec(memory_space=pltpu.HBM)] * len(args)
            + [spec(memory_space=pl.ANY)] * len(wait),
            out_specs=[vmem] * len(shapes) if several else vmem,
            out_shape=shapes,
            scratch_shapes=scratch,
            compiler_params=params(limit),
            cost_estimate=cost(1, 1),
            name=name,
        )(*args, *wait)

    one, three, five = [(1, rows, lanes)], [(3, 1, rows, lanes)], [(FIELDS, 1, rows, lanes)]
    front = apart(
        front_kernel,
        "surface_front",
        shaped(devices, 4, rows, lanes),
        (density, velocity, pressure, axial_metric, azim_metric, volume, radial_term),
        [pltpu.VMEM(shape, f32) for shape in one + three + one + three + three + one + five]
        + [pltpu.SemaphoreType.DMA((1, 7))],
    )
    fronts = lax.all_to_all(front, ("axial", "azim"), 0, 0, tiled=True)

    def azim_flux(mine, name, wait=()):
        one, three = (2 * part, rows, lanes), (3, 2 * part, rows, lanes)
        return apart(
            functools.partial(azim_flux_kernel, mine),
            name,
            [half_shape, shaped(2, 3, FIELDS, part, lanes)],
            (density, velocity, pressure, azim_metric, volume),
            [pltpu.VMEM(shape, f32) for shape in (one, three, one, three, one)]
            + [flux_scratch, pltpu.SemaphoreType.DMA((2, 5))],
            wait,
        )

    flux_sent, pack_sent = azim_flux(False, "azim_flux_sent", (front,))
    pack_in = sibling(pack_sent, around)
    flux_in = sibling(flux_sent, around)
    flux_kept, pack_kept = azim_flux(True, "azim_flux_kept")
    *packs, edge_a, edge_b = whole_call(
        functools.partial(chip_moments_kernel, rows),
        "chip_moments",
        [shaped(3 * FIELDS * part, lanes)] * 2 + [shaped(FIELDS * part, lanes)] * 2,
        (pack_kept, pack_in),
    )

    base, scale, edge_d = call(
        section_local_kernel,
        "section_local",
        4,
        [
            field(every),
            vector(every),
            field(every),
            vector(every),
            field(every),
            vector(every, FIELDS),
            table(own_d),
            fixed(basis_d.shape),
        ],
        [inner(every), inner_one(every), edge(every)],
        [
            shaped(4, FIELDS, rows, part, lanes),
            shaped(4, rows, part, lanes),
            shaped(BASIS, 4 * lines),
        ],
        (density, velocity, pressure, axial_metric, volume, radial_term, own_d, basis_d),
        wait=(packs[0], flux_in),
        scratch=[flux_scratch] * 2,
    )
    sums_d, sends_d = ring_exchange(
        packs, [edge_a, edge_b], around, 1, part, DERIV_ROOT ** (2 * rows), wait=(edge_d,)
    )
    edges_d = [rotate(edge_d, "axial", along, s) for s in range(1, along)]

    def section_axial(where, name, wait):
        return call(
            section_axial_kernel,
            name,
            2,
            [inner(where), inner_one(where), table(far_d)] + [edge(where)] * (along - 1),
            inner(every, FIELDS + 1),
            shaped(2, FIELDS + 1, rows, part, lanes),
            (base, scale, far_d, *edges_d),
            wait=wait,
        )

    base_kept = section_axial(kept, "section_axial_kept", (sends_d,))
    base_in = sibling(section_axial(sent, "section_axial_sent", (base_kept,)), around)

    operands = (
        fronts,
        jnp.asarray(deriv_along),
        jnp.asarray(deriv_around),
        jnp.asarray(filter_along),
        jnp.asarray(filter_around),
        bin_weights,
        weight_ids,
        panel_area,
        observer_ids,
        bin_ids,
    )
    scratch = [pltpu.VMEM(x.shape, x.dtype) for x in operands]
    scratch[3] = pltpu.VMEM(filter_along.shape[1:], f32)
    scratch[4] = pltpu.VMEM(filter_around.shape[1:], f32)
    scratch[5] = pltpu.SMEM(bin_weights.shape, f32)
    partial = apart(
        signals_kernel,
        "signals",
        shaped(OBSERVERS, TIME_BINS),
        operands,
        scratch
        + [
            pltpu.VMEM((OBSERVERS, weight_ids.size), jnp.bfloat16),
            pltpu.VMEM((2 * TIME_BINS, weight_ids.size), jnp.bfloat16),
            pltpu.SemaphoreType.DMA((1, len(operands))),
        ],
        wait=(sends_d,),
        limit=VMEM_LIMIT,
    )

    base_chip, scale_chip = call(
        section_azim_kernel,
        "section_azim",
        2,
        [inner(every), inner(every), inner(every, FIELDS + 1), inner(every, FIELDS + 1)],
        [inner(every, tall=tall), inner_one(every, tall)],
        [chip_shape, shaped(2, tall, part, lanes)],
        (flux_kept, flux_in, base_kept, base_in),
    )

    (ring_d,) = sums_d((partial, base_chip))

    share = OBSERVERS // along
    edge_shape = (BASIS, 4 * lines + share // 8 * lanes)
    sectioned, *edges_f = call(
        section_join_kernel,
        "section_join",
        2,
        [
            inner(every, tall=tall),
            inner_one(every, tall),
            ring_spec(1),
            fixed(basis_f.shape),
            fixed(partial.shape),
        ],
        [inner(every, tall=tall)] + [fixed(edge_shape)] * (along - 1),
        [chip_shape] + [shaped(*edge_shape)] * (along - 1),
        (base_chip, scale_chip, ring_d, basis_f, partial),
    )
    edges_f = [rotate(edges_f[s - 1], "axial", along, s) for s in range(1, along)]
    axial_local = call(
        axial_local_kernel,
        "axial_local",
        2,
        [inner(every, tall=tall), table(own_f)],
        inner(every, tall=tall),
        chip_shape,
        (sectioned, own_f),
    )
    chips = around // 2
    height = FIELDS * part
    shapes = [4 * height + share // 2, 4 * height, 2 * height, 2 * height, share // 2]
    shapes = [(size, lanes) for size in shapes]
    smoothed, *packs, edge_a, edge_b, held = call(
        functools.partial(axial_join_kernel, chips),
        "axial_join",
        2,
        [inner(every, tall=tall), table(far_f), fixed(partial.shape)]
        + [fixed(edge_shape)] * (along - 1),
        [inner(every, tall=tall)] + [fixed(shape) for shape in shapes],
        [chip_shape] + [shaped(*shape) for shape in shapes],
        (axial_local, far_f, partial, *edges_f),
        scratch=[pltpu.VMEM((6 * height, lanes), f32), pltpu.VMEM((share, lanes), f32)],
    )
    sums_f, sends_f = ring_exchange(
        packs,
        [edge_a, edge_b],
        around,
        2,
        part,
        FILTER_ROOT ** (2 * rows),
        held=held,
        shares=share // chips,
    )
    azim_local = call(
        azim_local_kernel,
        "azim_local",
        2,
        [inner(every, tall=tall)],
        inner(every, tall=tall),
        chip_shape,
        (smoothed,),
        wait=(sends_f,),
    )
    ring_f, signals_kept, signals_sent = sums_f()
    state_shape = shaped(FIELDS, planes, rows, lanes)
    own_signals = signals_kept.shape
    flat = rows * height + -(-own_signals[0] // 8) * 8
    flat_spec = spec((1, flat, lanes), lambda k: (k, 0, 0))
    rows_sent = call(
        azim_send_kernel,
        "azim_join_sent",
        2,
        [row_half(lambda: 1 - core_index()), ring_spec(2), fixed(own_signals)],
        flat_spec,
        shaped(2, flat, lanes),
        (azim_local, ring_f, signals_sent),
    )
    rows_in = sibling(rows_sent, around)
    mine = call(
        azim_keep_kernel,
        "azim_join_kept",
        2,
        [row_half(core_index), ring_spec(2)],
        vector(kept, FIELDS),
        state_shape,
        (azim_local, ring_f),
    )
    return call(
        place_rows_kernel,
        "place_rows",
        2,
        [flat_spec, fixed(own_signals), spec(memory_space=pl.ANY)],
        [vector(sent, FIELDS), fixed(own_signals)],
        [state_shape, shaped(*own_signals)],
        (rows_in, signals_kept, mine),
        input_output_aliases={2: 0},
    )


def solution(mesh):
    placed = (
        P(None, "azim", "axial"),
        P(None, None, "azim", "axial"),
        P(None, "azim", "axial"),
        P(None, None, "azim", "axial"),
        P(None, None, "azim", "axial"),
        P(None, "azim", "axial"),
        P(None, None, "azim", "axial"),
        P("azim", "axial"),
        P(None, "azim", "axial"),
        P(None, "azim", "axial"),
        P(None, "azim", "axial"),
        P(),
    )
    return jax.shard_map(
        per_device,
        mesh=mesh,
        in_specs=placed,
        out_specs=(P(None, None, "azim", "axial"), P(("axial", "azim"), None)),
        check_vma=False,
    )
```

time: 407 us -> 84.3 us (0.21); the launches traced: 401 us -> 83.7 us
  waiting for transfers between devices: 188 us -> 23.6 us
  matrix products: 93.5 us -> 0 us
  other arithmetic: 45.1 us -> 0 us
  Pallas kernels: 0 us -> 26 us
  blocking collectives: 19.2 us -> 0 us
  local copies, waits for them, and re-layouts: 23.2 us -> 5.07 us
  between operations: 14.7 us -> 1.08 us
  starting transfers between devices: 17.2 us -> 28 us
    reduce_scatter x1 -> x0, waiting for transfers between devices: 133 us -> none  [per_device(): lax.psum_scatter(partial_signals, ('axial', 'azim'), scatter_dimension=0,...]
    dot_general x23 -> x0, matrix products: 93.5 us -> none  [the longest x2 35.2 us: open_line(): jnp.einsum('vraj,j->vra', rhs, signed_power(base, offsets), precision=HIG...]
    all_gather x2 -> x0, waiting for transfers between devices: 30.2 us -> none  [cycle_line(): piece = lax.all_gather(moments, 'azim', axis=0, tiled=True)]
    pallas_call x0 -> x20, Pallas kernels: none -> 26 us  [the longest x11 12.3 us: call(): pl.pallas_call(waiting(kernel, len(args), wait), grid=(steps,), in_specs=...]
    scatter-add x1 -> x0, other arithmetic: 22.6 us -> none  [per_device(): jax.ops.segment_sum(values, bucket, num_segments=OBSERVERS * TIME_BINS)]
    all_gather x2 -> x0, blocking collectives: 19.2 us -> none  [open_line(): piece = lax.all_gather(moments, 'axial', axis=0, tiled=True)]
    add x4 -> x0, other arithmetic: 15.1 us -> none  [the longest x2 8.17 us: filter_side(): total = total + 0.5 * coeffs[shift] * (cells(shift) + cells(-shift))]
    slice x12 -> x0, local copies, waits for them, and re-layouts: 8.64 us -> none  [the longest x8 6.98 us: padded(): head = lax.slice_in_dim(cells, 0, width, axis=dim)]
  transfers between devices with their start and end apart: 11 -> 19, of which waited for: 7 -> 9; matrix products, arithmetic and copies ran while one was open for 15% -> 0% of each run, Pallas kernels for 0% -> 21%
where the time goes in v3:
time: 84.3 us; the launch traced here: 83.7 us
  starting transfers between devices  28 us (33%)
  Pallas kernels  26 us (31%)
  waiting for transfers between devices  23.6 us (28%)
  local copies, waits for them, and re-layouts  5.07 us (6%)
  between operations  1.08 us (1%)
    ppermute x8, waiting for transfers between devices, partner(): return lax.ppermute(values, 'azim', pairs)  15.9 us
    pallas_call x11, Pallas kernels, call(): pl.pallas_call(waiting(kernel, len(args), wait), grid=(steps,), in_specs=...  12.3 us
    ppermute x8, starting transfers between devices, partner(): return lax.ppermute(values, 'azim', pairs)  12.2 us
    pallas_call x4, Pallas kernels, apart(): pl.pallas_call(waiting(kernel, len(args), wait), in_specs=[spec(memory_sp...  11.7 us
    ppermute x6, starting transfers between devices, rotate(): lax.ppermute(values, axis, [(i, (i + shift) % count) for i in range(count)])  7.79 us
    all_to_all x1, starting transfers between devices, per_device(): fronts = lax.all_to_all(front, ('axial', 'azim'), 0, 0, tiled=True)  7.4 us
    ppermute x6, waiting for transfers between devices, rotate(): lax.ppermute(values, axis, [(i, (i + shift) % count) for i in range(count)])  6.68 us
    unnamed x54, local copies, waits for them, and re-layouts  5.07 us
  transfers between devices with their start and end apart: 19, of which 9 were waited for; matrix products, arithmetic and copies ran while one was open for 0% of the time, Pallas kernels for 21%

profile of v3, /device:TPU:0, one launch (start us, length us, event | category | flops | bytes accessed | tf_op | source)
XLA Modules:
  0.0 83.7 jit_solution(12834812461827231716)
XLA Ops:
  0.6 1.8 %surface_front.1.refs_5_ = f32[32,4,8,128]{3,2,1,0:T(8,128)} custom-call(f32[64,8,128]{2,1,0:T(8,128)} %refs_0_.3, f32[3,64,8,128]{3,2,1,0:T(8,128)} %refs_1_.4, f32[64,8,128]{2,1,0:T(8,128)} %refs_2_.6, f32[3,64,8,128]{3,2,1,0:T(8,128)} %refs_3_.4, f32[3,64,8,128]{3,2,1,0:T(8,128)} %refs_3_.3, f32[64,8,128]{2,1,0:T(8,128)} %refs_4_.4, f32[5,64,8,128]{3,2,1,0:T(8,128)} %refs_5_.2), custom_call_target="tpu_custom_call" | custom-call | flops 1 | bytes 1 | tf_op jit(solution)/shard_map/surface_front/pallas_call | solution.py:926
  2.4 2.5 %azim_flux_sent.1 = (f32[2,5,8,16,128]{4,3,2,1,0:T(8,128)}, f32[2,3,5,16,128]{4,3,2,1,0:T(8,128)}) custom-call(f32[64,8,128]{2,1,0:T(8,128)} %refs_0_.3, f32[3,64,8,128]{3,2,1,0:T(8,128)} %refs_1_.4, f32[64,8,128]{2,1,0:T(8,128)} %refs_2_.6, f32[3,64,8,128]{3,2,1,0:T(8,128)} %refs_3_.3, f32[64,8,128]{2,1,0:T(8,128)} %refs_4_.4, ...), custom_call_target="tpu_custom_call" | custom-call | flops 1 | bytes 1 | tf_op jit(solution)/shard_map/azim_flux_sent/pallas_call | solution.py:926
  5.5 7.4 %all-to-all-start = ((f32[32,4,8,128]{3,2,1,0:T(8,128)}), f32[32,4,8,128]{3,2,1,0:T(8,128)}, u32[]{:S(2)}, u32[]{:S(2)}) async-start(f32[32,4,8,128]{3,2,1,0:T(8,128)} %surface_front.1.refs_5_), calls=%async_computation | async-start | bytes 1048576 | tf_op jit(solution)/shard_map/all_to_all | solution.py:947
  12.9 2.6 %azim_flux_kept.1 = (f32[2,5,8,16,128]{4,3,2,1,0:T(8,128)}, f32[2,3,5,16,128]{4,3,2,1,0:T(8,128)}) custom-call(f32[64,8,128]{2,1,0:T(8,128)} %refs_0_.3, f32[3,64,8,128]{3,2,1,0:T(8,128)} %refs_1_.4, f32[64,8,128]{2,1,0:T(8,128)} %refs_2_.6, f32[3,64,8,128]{3,2,1,0:T(8,128)} %refs_3_.3, f32[64,8,128]{2,1,0:T(8,128)} %refs_4_.4), custom_call_target="tpu_custom_call" | custom-call | flops 1 | bytes 1 | tf_op jit(solution)/shard_map/azim_flux_kept/pallas_call | solution.py:926
  18.2 3.6 %collective-permute-start.6 = (f32[240,128]{1,0:T(8,128)S(1)}, f32[240,128]{1,0:T(8,128)S(1)}, u32[]{:S(2)}, u32[]{:S(2)}) collective-permute-start(f32[240,128]{1,0:T(8,128)S(1)} %get-tuple-element.42.refs_3_.refs_4_), channel_id=1, source_target_pairs={{0,6},{1,7},{2,4},{3,5},{4,2},{5,3},{6,0},{7,1},{8,14},{9,15},{10,... | collective-permute-start | bytes 368648 | tf_op jit(solution)/shard_map/ppermute | solution.py:756
  22.8 2.5 %section_local.1 = (f32[4,5,8,16,128]{4,3,2,1,0:T(8,128)S(1)}, f32[4,8,16,128]{3,2,1,0:T(8,128)S(1)}, f32[8,2560]{1,0:T(8,128)S(1)}) custom-call(f32[64,8,128]{2,1,0:T(8,128)S(1)} %copy-done.2, f32[3,64,8,128]{3,2,1,0:T(8,128)S(1)} %copy-done, f32[64,8,128]{2,1,0:T(8,128)S(1)} %copy-done.3, f32[3,64,8,128]{3,2,1,0:T(8,128)S(1)} %copy-done.5, ...), custom_call_target="tpu_custom_call" | custom-call | flops 1 | bytes 1 | tf_op jit(solution)/shard_map/section_local/pallas_call | solution.py:905
  25.3 2.5 %collective-permute-start.4 = (f32[8,2560]{1,0:T(8,128)S(1)}, f32[8,2560]{1,0:T(8,128)S(1)}, u32[]{:S(2)}, u32[]{:S(2)}) collective-permute-start(f32[8,2560]{1,0:T(8,128)S(1)} %get-tuple-element.40.refs_6_), channel_id=1, source_target_pairs={{0,24},{8,0},{16,8},{24,16},{1,25},{9,1},{17,9},{25,17},{2,26},{10... | collective-permute-start | bytes 245768 | tf_op jit(solution)/shard_map/ppermute | solution.py:742
  29.0 2.4 %collective-permute-done.5.refs_1_ = f32[240,128]{1,0:T(8,128)S(1)} collective-permute-done((f32[240,128]{1,0:T(8,128)S(1)}, f32[240,128]{1,0:T(8,128)S(1)}, u32[]{:S(2)}, u32[]{:S(2)}) %collective-permute-start.5) | collective-permute-done | bytes 122912 | tf_op jit(solution)/shard_map/ppermute | solution.py:756
  32.2 2.1 %collective-permute-done.3.refs_4_ = f32[8,2560]{1,0:T(8,128)S(1)} collective-permute-done((f32[8,2560]{1,0:T(8,128)S(1)}, f32[8,2560]{1,0:T(8,128)S(1)}, u32[]{:S(2)}, u32[]{:S(2)}) %collective-permute-start.3) | collective-permute-done | bytes 81952 | tf_op jit(solution)/shard_map/ppermute | solution.py:742
  35.1 1.5 %section_axial_sent.1 = f32[2,6,8,16,128]{4,3,2,1,0:T(8,128)} custom-call(f32[4,5,8,16,128]{4,3,2,1,0:T(8,128)S(1)} %get-tuple-element.38.refs_0_, f32[4,8,16,128]{3,2,1,0:T(8,128)S(1)} %get-tuple-element.39.refs_1_, bf16[4,2,24,128]{3,2,1,0:T(8,128)(2,1)S(1)} %copy-done.16, f32[8,2560]{1,0:T(8,128)S(1)} %collective-permute-done.2.refs_3_, ...), custom_call_target="tpu_custom_call" | custom-call | flops 1 | bytes 1 | tf_op jit(solution)/shard_map/section_axial_sent/pallas_call | solution.py:905
  36.5 1.4 %collective-permute-start.9 = (f32[240,128]{1,0:T(8,128)}, f32[240,128]{1,0:T(8,128)}, u32[]{:S(2)}, u32[]{:S(2)}) collective-permute-start(f32[240,128]{1,0:T(8,128)} %get-tuple-element.47), channel_id=1, source_target_pairs={{0,2},{1,3},{2,0},{3,1},{4,6},{5,7},{6,4},{7,5},{8,10},{9,11},{10,... | collective-permute-start | bytes 368648 | tf_op jit(solution)/shard_map/ppermute | solution.py:756
  40.1 4.9 %signals.1.refs_8_.partial = f32[512,128]{1,0:T(8,128)S(1)} custom-call(f32[32,4,8,128]{3,2,1,0:T(8,128)} %all-to-all-done.refs_0_, bf16[2,512,512]{2,1,0:T(8,128)(2,1)S(1)} %copy-done.7, bf16[2,64,64]{2,1,0:T(8,128)(2,1)S(1)} %copy-done.19, f32[4,512,128]{2,1,0:T(8,128)S(1)} %copy-done.6, f32[8,8,64]{2,1,0:T(8,128)S(1)} %copy-done.18, f32[256]{0:T(256)S(1)} %copy-done.26, ...), custom_call_target="tpu_custom_call" | custom-call | flops 1 | bytes 1 | tf_op jit(solution)/shard_map/signals/pallas_call | solution.py:926
  45.1 1.9 %section_azim.1 = (f32[2,5,16,16,128]{4,3,2,1,0:T(8,128)S(1)}, f32[2,16,16,128]{3,2,1,0:T(8,128)S(1)}) custom-call(f32[2,5,8,16,128]{4,3,2,1,0:T(8,128)S(1)} %copy-done.8, f32[2,5,8,16,128]{4,3,2,1,0:T(8,128)} %collective-permute-done.refs_9_.flux_in, f32[2,6,8,16,128]{4,3,2,1,0:T(8,128)S(1)} %section_axial_kept.1.refs_6_.base_keep, ...), custom_call_target="tpu_custom_call" | custom-call | flops 1 | bytes 1 | tf_op jit(solution)/shard_map/section_azim/pallas_call | solution.py:905
  47.0 1.1 %ring_sums.2.ring = f32[2,4,5,16,128]{4,3,2,1,0:T(8,128)S(1)} custom-call(f32[240,128]{1,0:T(8,128)S(1)} %get-tuple-element.37.refs_8_.refs_0_, f32[240,128]{1,0:T(8,128)S(1)} %copy-done.10, f32[240,128]{1,0:T(8,128)} %collective-permute-done.8.refs_2_.refs_3_, f32[240,128]{1,0:T(8,128)} %collective-permute-done.8.refs_2_.refs_3_, ...), custom_call_target="tpu_custom_call" | custom-call | flops 1 | bytes 1 | tf_op jit(solution)/shard_map/ring_sums/pallas_call | solution.py:767
  50.0 1.5 %collective-permute-start.11 = (f32[8,4608]{1,0:T(8,128)S(1)}, f32[8,4608]{1,0:T(8,128)S(1)}, u32[]{:S(2)}, u32[]{:S(2)}) collective-permute-start(f32[8,4608]{1,0:T(8,128)S(1)} %get-tuple-element.50), channel_id=1, source_target_pairs={{0,16},{8,24},{16,0},{24,8},{1,17},{9,25},{17,1},{25,9},{2,18},{10... | collective-permute-start | bytes 442376 | tf_op jit(solution)/shard_map/ppermute | solution.py:742
  51.4 1.8 %collective-permute-start.12 = (f32[8,4608]{1,0:T(8,128)S(1)}, f32[8,4608]{1,0:T(8,128)S(1)}, u32[]{:S(2)}, u32[]{:S(2)}) collective-permute-start(f32[8,4608]{1,0:T(8,128)S(1)} %get-tuple-element.51), channel_id=1, source_target_pairs={{0,24},{8,0},{16,8},{24,16},{1,25},{9,1},{17,9},{25,17},{2,26},{10... | collective-permute-start | bytes 442376 | tf_op jit(solution)/shard_map/ppermute | solution.py:742
  54.1 2.6 %collective-permute-done.10.rest_0_ = f32[8,4608]{1,0:T(8,128)S(1)} collective-permute-done((f32[8,4608]{1,0:T(8,128)S(1)}, f32[8,4608]{1,0:T(8,128)S(1)}, u32[]{:S(2)}, u32[]{:S(2)}) %collective-permute-start.10) | collective-permute-done | bytes 147488 | tf_op jit(solution)/shard_map/ppermute | solution.py:742
  56.6 1.9 %collective-permute-done.11.rest_1_ = f32[8,4608]{1,0:T(8,128)S(1)} collective-permute-done((f32[8,4608]{1,0:T(8,128)S(1)}, f32[8,4608]{1,0:T(8,128)S(1)}, u32[]{:S(2)}, u32[]{:S(2)}) %collective-permute-start.11) | collective-permute-done | bytes 147488 | tf_op jit(solution)/shard_map/ppermute | solution.py:742
  59.9 3.3 %collective-permute-start.14 = (f32[320,128]{1,0:T(8,128)S(1)}, f32[320,128]{1,0:T(8,128)S(1)}, u32[]{:S(2)}, u32[]{:S(2)}) collective-permute-start(f32[320,128]{1,0:T(8,128)S(1)} %get-tuple-element.55.refs_3_.refs_4_), channel_id=1, source_target_pairs={{0,6},{1,7},{2,4},{3,5},{4,2},{5,3},{6,0},{7,1},{8,14},{9,15},{10,... | collective-permute-start | bytes 491528 | tf_op jit(solution)/shard_map/ppermute | solution.py:756
  63.2 7.7 %collective-permute-done.14.refs_4_.refs_5_ = f32[320,128]{1,0:T(8,128)S(1)} collective-permute-done((f32[320,128]{1,0:T(8,128)S(1)}, f32[320,128]{1,0:T(8,128)S(1)}, u32[]{:S(2)}, u32[]{:S(2)}) %collective-permute-start.14) | collective-permute-done | bytes 163872 | tf_op jit(solution)/shard_map/ppermute | solution.py:756
  70.9 1.7 %collective-permute-start.15 = (f32[352,128]{1,0:T(8,128)S(1)}, f32[352,128]{1,0:T(8,128)S(1)}, u32[]{:S(2)}, u32[]{:S(2)}) collective-permute-start(f32[352,128]{1,0:T(8,128)S(1)} %get-tuple-element.58.refs_1_), channel_id=1, source_target_pairs={{0,6},{1,7},{2,4},{3,5},{4,2},{5,3},{6,0},{7,1},{8,14},{9,15},{10,... | collective-permute-start | bytes 540680 | tf_op jit(solution)/shard_map/ppermute | solution.py:756
  72.6 1.2 %collective-permute-start.16 = (f32[320,128]{1,0:T(8,128)S(1)}, f32[320,128]{1,0:T(8,128)S(1)}, u32[]{:S(2)}, u32[]{:S(2)}) collective-permute-start(f32[320,128]{1,0:T(8,128)S(1)} %get-tuple-element.59), channel_id=1, source_target_pairs={{0,2},{1,3},{2,0},{3,1},{4,6},{5,7},{6,4},{7,5},{8,10},{9,11},{10,... | collective-permute-start | bytes 491528 | tf_op jit(solution)/shard_map/ppermute | solution.py:756
  74.6 5.6 %collective-permute-done.16.refs_6_.refs_7_ = f32[320,128]{1,0:T(8,128)S(1)} collective-permute-done((f32[320,128]{1,0:T(8,128)S(1)}, f32[320,128]{1,0:T(8,128)S(1)}, u32[]{:S(2)}, u32[]{:S(2)}) %collective-permute-start.16) | collective-permute-done | bytes 163872 | tf_op jit(solution)/shard_map/ppermute | solution.py:756
  80.7 1.2 %azim_join_kept.1.partial = f32[5,64,8,128]{3,2,1,0:T(8,128)} custom-call(f32[2,5,16,16,128]{4,3,2,1,0:T(8,128)S(1)} %azim_local.1.local, f32[2,6,5,16,128]{4,3,2,1,0:T(8,128)S(1)} %get-tuple-element.61.ring), custom_call_target="tpu_custom_call" | custom-call | flops 1 | bytes 1 | tf_op jit(solution)/shard_map/azim_join_kept/pallas_call | solution.py:905
  (88 shorter events, 16.1 us)
Async XLA Ops:
  2.4 19.4 %copy-start.25 = (bf16[2,8,128]{2,1,0:T(8,128)(2,1)S(1)}, bf16[2,8,128]{2,1,0:T(8,128)(2,1)}, u32[]{:S(2)}) copy-start(bf16[2,8,128]{2,1,0:T(8,128)(2,1)} %constant.21.clone.refs_7_) | copy-start | bytes 12292
  4.9 16.9 %collective-permute-start = (f32[2,5,8,16,128]{4,3,2,1,0:T(8,128)}, f32[2,5,8,16,128]{4,3,2,1,0:T(8,128)}, u32[]{:S(2)}, u32[]{:S(2)}) collective-permute-start(f32[2,5,8,16,128]{4,3,2,1,0:T(8,128)} %get-tuple-element.34), channel_id=1, source_target_pairs={{0,1},{1,0},{2,3},{3,2},{4,5},{5,4},{6,7},{7,6},{8,9},{9,8},{10,11... | collective-permute-start | bytes 1966088 | tf_op jit(solution)/shard_map/ppermute | solution.py:746
  5.4 10.2 %collective-permute-start.1 = (f32[2,3,5,16,128]{4,3,2,1,0:T(8,128)}, f32[2,3,5,16,128]{4,3,2,1,0:T(8,128)S(1)}, u32[]{:S(2)}, u32[]{:S(2)}) collective-permute-start(f32[2,3,5,16,128]{4,3,2,1,0:T(8,128)} %get-tuple-element.36), channel_id=1, source_target_pairs={{0,1},{1,0},{2,3},{3,2},{4,5},{5,4},{6,7},{7,6},{8,9},{9,8},{10,11... | collective-permute-start | bytes 737288 | tf_op jit(solution)/shard_map/ppermute | solution.py:746
  5.5 16.3 %copy-start.4 = (f32[64,8,128]{2,1,0:T(8,128)S(1)}, f32[64,8,128]{2,1,0:T(8,128)}, u32[]{:S(2)}) copy-start(f32[64,8,128]{2,1,0:T(8,128)} %refs_4_.4) | copy-start | bytes 786436
  5.5 16.4 %copy-start.5 = (f32[3,64,8,128]{3,2,1,0:T(8,128)S(1)}, f32[3,64,8,128]{3,2,1,0:T(8,128)}, u32[]{:S(2)}) copy-start(f32[3,64,8,128]{3,2,1,0:T(8,128)} %refs_3_.4) | copy-start | bytes 2359300
  5.5 33.2 %all-to-all-start = ((f32[32,4,8,128]{3,2,1,0:T(8,128)}), f32[32,4,8,128]{3,2,1,0:T(8,128)}, u32[]{:S(2)}, u32[]{:S(2)}) async-start(f32[32,4,8,128]{3,2,1,0:T(8,128)} %surface_front.1.refs_5_), calls=%async_computation | async-start | bytes 1048576 | tf_op jit(solution)/shard_map/all_to_all | solution.py:947
  12.9 8.9 %copy-start = (f32[3,64,8,128]{3,2,1,0:T(8,128)S(1)}, f32[3,64,8,128]{3,2,1,0:T(8,128)}, u32[]{:S(2)}) copy-start(f32[3,64,8,128]{3,2,1,0:T(8,128)} %refs_1_.4) | copy-start | bytes 2359300
  18.2 10.8 %collective-permute-start.6 = (f32[240,128]{1,0:T(8,128)S(1)}, f32[240,128]{1,0:T(8,128)S(1)}, u32[]{:S(2)}, u32[]{:S(2)}) collective-permute-start(f32[240,128]{1,0:T(8,128)S(1)} %get-tuple-element.42.refs_3_.refs_4_), channel_id=1, source_target_pairs={{0,6},{1,7},{2,4},{3,5},{4,2},{5,3},{6,0},{7,1},{8,14},{9,15},{10,... | collective-permute-start | bytes 368648 | tf_op jit(solution)/shard_map/ppermute | solution.py:756
  21.8 9.6 %collective-permute-start.5 = (f32[240,128]{1,0:T(8,128)S(1)}, f32[240,128]{1,0:T(8,128)S(1)}, u32[]{:S(2)}, u32[]{:S(2)}) collective-permute-start(f32[240,128]{1,0:T(8,128)S(1)} %get-tuple-element.37.refs_8_.refs_0_), channel_id=1, source_target_pairs={{0,2},{1,3},{2,0},{3,1},{4,6},{5,7},{6,4},{7,5},{8,10},{9,11},{10,... | collective-permute-start | bytes 368648 | tf_op jit(solution)/shard_map/ppermute | solution.py:756
  22.8 11.4 %copy-start.16 = (bf16[4,2,24,128]{3,2,1,0:T(8,128)(2,1)S(1)}, bf16[4,2,24,128]{3,2,1,0:T(8,128)(2,1)}, u32[]{:S(2)}) copy-start(bf16[4,2,24,128]{3,2,1,0:T(8,128)(2,1)} %constant.22.clone.refs_2_) | copy-start | bytes 147460
  25.3 6.8 %collective-permute-start.4 = (f32[8,2560]{1,0:T(8,128)S(1)}, f32[8,2560]{1,0:T(8,128)S(1)}, u32[]{:S(2)}, u32[]{:S(2)}) collective-permute-start(f32[8,2560]{1,0:T(8,128)S(1)} %get-tuple-element.40.refs_6_), channel_id=1, source_target_pairs={{0,24},{8,0},{16,8},{24,16},{1,25},{9,1},{17,9},{25,17},{2,26},{10... | collective-permute-start | bytes 245768 | tf_op jit(solution)/shard_map/ppermute | solution.py:742
  27.8 6.5 %collective-permute-start.3 = (f32[8,2560]{1,0:T(8,128)S(1)}, f32[8,2560]{1,0:T(8,128)S(1)}, u32[]{:S(2)}, u32[]{:S(2)}) collective-permute-start(f32[8,2560]{1,0:T(8,128)S(1)} %get-tuple-element.40.refs_6_), channel_id=1, source_target_pairs={{0,16},{8,24},{16,0},{24,8},{1,17},{9,25},{17,1},{25,9},{2,18},{10... | collective-permute-start | bytes 245768 | tf_op jit(solution)/shard_map/ppermute | solution.py:742
  28.3 5.9 %collective-permute-start.2 = (f32[8,2560]{1,0:T(8,128)S(1)}, f32[8,2560]{1,0:T(8,128)S(1)}, u32[]{:S(2)}, u32[]{:S(2)}) collective-permute-start(f32[8,2560]{1,0:T(8,128)S(1)} %get-tuple-element.40.refs_6_), channel_id=1, source_target_pairs={{0,8},{8,16},{16,24},{24,0},{1,9},{9,17},{17,25},{25,1},{2,10},{10... | collective-permute-start | bytes 245768 | tf_op jit(solution)/shard_map/ppermute | solution.py:742
  36.5 8.5 %collective-permute-start.7 = (f32[2,6,8,16,128]{4,3,2,1,0:T(8,128)}, f32[2,6,8,16,128]{4,3,2,1,0:T(8,128)}, u32[]{:S(2)}, u32[]{:S(2)}) collective-permute-start(f32[2,6,8,16,128]{4,3,2,1,0:T(8,128)} %section_axial_sent.1), channel_id=1, source_target_pairs={{0,1},{1,0},{2,3},{3,2},{4,5},{5,4},{6,7},{7,6},{8,9},{9,8},{10,11... | collective-permute-start | bytes 2359304 | tf_op jit(solution)/shard_map/ppermute | solution.py:746
  36.5 10.4 %collective-permute-start.9 = (f32[240,128]{1,0:T(8,128)}, f32[240,128]{1,0:T(8,128)}, u32[]{:S(2)}, u32[]{:S(2)}) collective-permute-start(f32[240,128]{1,0:T(8,128)} %get-tuple-element.47), channel_id=1, source_target_pairs={{0,2},{1,3},{2,0},{3,1},{4,6},{5,7},{6,4},{7,5},{8,10},{9,11},{10,... | collective-permute-start | bytes 368648 | tf_op jit(solution)/shard_map/ppermute | solution.py:756
  37.9 9.1 %collective-permute-start.8 = (f32[240,128]{1,0:T(8,128)S(1)}, f32[240,128]{1,0:T(8,128)}, u32[]{:S(2)}, u32[]{:S(2)}) collective-permute-start(f32[240,128]{1,0:T(8,128)S(1)} %get-tuple-element.44.refs_6_.refs_10_), channel_id=1, source_target_pairs={{0,6},{1,7},{2,4},{3,5},{4,2},{5,3},{6,0},{7,1},{8,14},{9,15},{10,... | collective-permute-start | bytes 368648 | tf_op jit(solution)/shard_map/ppermute | solution.py:756
  49.0 7.6 %collective-permute-start.10 = (f32[8,4608]{1,0:T(8,128)S(1)}, f32[8,4608]{1,0:T(8,128)S(1)}, u32[]{:S(2)}, u32[]{:S(2)}) collective-permute-start(f32[8,4608]{1,0:T(8,128)S(1)} %get-tuple-element.49), channel_id=1, source_target_pairs={{0,8},{8,16},{16,24},{24,0},{1,9},{9,17},{17,25},{25,1},{2,10},{10... | collective-permute-start | bytes 442376 | tf_op jit(solution)/shard_map/ppermute | solution.py:742
  50.0 8.5 %collective-permute-start.11 = (f32[8,4608]{1,0:T(8,128)S(1)}, f32[8,4608]{1,0:T(8,128)S(1)}, u32[]{:S(2)}, u32[]{:S(2)}) collective-permute-start(f32[8,4608]{1,0:T(8,128)S(1)} %get-tuple-element.50), channel_id=1, source_target_pairs={{0,16},{8,24},{16,0},{24,8},{1,17},{9,25},{17,1},{25,9},{2,18},{10... | collective-permute-start | bytes 442376 | tf_op jit(solution)/shard_map/ppermute | solution.py:742
  51.4 7.2 %collective-permute-start.12 = (f32[8,4608]{1,0:T(8,128)S(1)}, f32[8,4608]{1,0:T(8,128)S(1)}, u32[]{:S(2)}, u32[]{:S(2)}) collective-permute-start(f32[8,4608]{1,0:T(8,128)S(1)} %get-tuple-element.51), channel_id=1, source_target_pairs={{0,24},{8,0},{16,8},{24,16},{1,25},{9,1},{17,9},{25,17},{2,26},{10... | collective-permute-start | bytes 442376 | tf_op jit(solution)/shard_map/ppermute | solution.py:742
  59.7 11.2 %collective-permute-start.13 = (f32[384,128]{1,0:T(8,128)S(1)}, f32[384,128]{1,0:T(8,128)S(1)}, u32[]{:S(2)}, u32[]{:S(2)}) collective-permute-start(f32[384,128]{1,0:T(8,128)S(1)} %get-tuple-element.53.refs_0_), channel_id=1, source_target_pairs={{0,2},{1,3},{2,0},{3,1},{4,6},{5,7},{6,4},{7,5},{8,10},{9,11},{10,... | collective-permute-start | bytes 589832 | tf_op jit(solution)/shard_map/ppermute | solution.py:756
  59.9 11.0 %collective-permute-start.14 = (f32[320,128]{1,0:T(8,128)S(1)}, f32[320,128]{1,0:T(8,128)S(1)}, u32[]{:S(2)}, u32[]{:S(2)}) collective-permute-start(f32[320,128]{1,0:T(8,128)S(1)} %get-tuple-element.55.refs_3_.refs_4_), channel_id=1, source_target_pairs={{0,6},{1,7},{2,4},{3,5},{4,2},{5,3},{6,0},{7,1},{8,14},{9,15},{10,... | collective-permute-start | bytes 491528 | tf_op jit(solution)/shard_map/ppermute | solution.py:756
  70.9 9.3 %collective-permute-start.15 = (f32[352,128]{1,0:T(8,128)S(1)}, f32[352,128]{1,0:T(8,128)S(1)}, u32[]{:S(2)}, u32[]{:S(2)}) collective-permute-start(f32[352,128]{1,0:T(8,128)S(1)} %get-tuple-element.58.refs_1_), channel_id=1, source_target_pairs={{0,6},{1,7},{2,4},{3,5},{4,2},{5,3},{6,0},{7,1},{8,14},{9,15},{10,... | collective-permute-start | bytes 540680 | tf_op jit(solution)/shard_map/ppermute | solution.py:756
  72.6 7.6 %collective-permute-start.16 = (f32[320,128]{1,0:T(8,128)S(1)}, f32[320,128]{1,0:T(8,128)S(1)}, u32[]{:S(2)}, u32[]{:S(2)}) collective-permute-start(f32[320,128]{1,0:T(8,128)S(1)} %get-tuple-element.59), channel_id=1, source_target_pairs={{0,2},{1,3},{2,0},{3,1},{4,6},{5,7},{6,4},{7,5},{8,10},{9,11},{10,... | collective-permute-start | bytes 491528 | tf_op jit(solution)/shard_map/ppermute | solution.py:756
  80.6 2.2 %collective-permute-start.17 = (f32[2,656,128]{2,1,0:T(8,128)S(1)}, f32[2,656,128]{2,1,0:T(8,128)S(1)}, u32[]{:S(2)}, u32[]{:S(2)}) collective-permute-start(f32[2,656,128]{2,1,0:T(8,128)S(1)} %azim_join_sent.1), channel_id=1, source_target_pairs={{0,1},{1,0},{2,3},{3,2},{4,5},{5,4},{6,7},{7,6},{8,9},{9,8},{10,11... | collective-permute-start | bytes 2015240 | tf_op jit(solution)/shard_map/ppermute | solution.py:746
  (22 other events, 79.3 us)

commit v4 on v3

v4 whole, which is shorter than its diff:
```python
import functools
import math

import jax
import jax.numpy as jnp
import numpy as np
from jax import lax
from jax.experimental import pallas as pl
from jax.experimental.pallas import tpu as pltpu
from jax.sharding import PartitionSpec as P

OBSERVERS = 512
TIME_BINS = 128

GAMMA = 1.4
SECTION = 0.25
DERIV_ALPHA = 1.0 / 3.0
FILTER_ALPHA = 0.499
FIELDS = 5
BASIS = 8
VMEM_LIMIT = 16 * 1024 * 1024
INPUT_LIMIT = 60 * 1024 * 1024


def decay_root(alpha):
    return (-1.0 + math.sqrt(1.0 - 4.0 * alpha * alpha)) / (2.0 * alpha)


DERIV_ROOT = decay_root(DERIV_ALPHA)
FILTER_ROOT = decay_root(FILTER_ALPHA)

DERIV_NEAR = 1.0 / 12.0
DERIV_FAR = (
    (25.0 / 36.0) * (DERIV_ROOT - 1.0 / DERIV_ROOT) / (1.0 + 2.0 * DERIV_ALPHA * DERIV_ROOT)
)

_B = FILTER_ALPHA
_EDGE = (1.0 - 2.0 * _B) / 64.0
_Q2 = 1.0 / _B
_Q1 = (-6.0 - _Q2) / _B
_Q0 = (12.0 - _Q1) / _B
_RHO = -8.0 - _Q0
FILTER_MID = _EDGE * (_Q0 + 2.0 * _Q2)
FILTER_ONE = _EDGE * _Q1
FILTER_TWO = _EDGE * _Q2
FILTER_FAR = _EDGE * _RHO / (1.0 + 2.0 * _B * FILTER_ROOT)


def open_operator(length, alpha, side):
    base = decay_root(alpha)
    tri = np.eye(length) + alpha * (np.eye(length, k=1) + np.eye(length, k=-1))
    tri[0, 0] = -alpha / base
    return np.linalg.solve(tri, side)


def deriv_matrix(length):
    return (7.0 / 9.0) * (np.eye(length, k=1) - np.eye(length, k=-1)) + (1.0 / 36.0) * (
        np.eye(length, k=2) - np.eye(length, k=-2)
    )


def filter_matrix(length):
    beta = FILTER_ALPHA
    coeffs = [
        (11.0 + 10.0 * beta) / 16.0,
        (15.0 + 34.0 * beta) / 32.0,
        (-3.0 + 6.0 * beta) / 16.0,
        (1.0 - 2.0 * beta) / 32.0,
    ]
    total = coeffs[0] * np.eye(length)
    for shift in range(1, 4):
        total = total + 0.5 * coeffs[shift] * (np.eye(length, k=shift) + np.eye(length, k=-shift))
    return total


def axial_tables(count, width, alpha, kind):
    length = count * width
    side = deriv_matrix(length) if kind == "deriv" else filter_matrix(length)
    whole = open_operator(length, alpha, side)
    base = decay_root(alpha)
    basis = np.zeros((BASIS, width))
    for edge in range(3):
        basis[edge, edge] = 1.0
        basis[3 + edge, width - 3 + edge] = 1.0
    basis[6] = base ** np.arange(width - 1, -1, -1, dtype=np.float64)
    basis[7] = base ** np.arange(width, dtype=np.float64)
    inverse = np.linalg.pinv(basis)
    own = np.zeros((count, width, width))
    far = np.zeros((count, max(count - 1, 1) * BASIS, width))
    for here in range(count):
        rows = whole[here * width : (here + 1) * width]
        own[here] = rows[:, here * width : (here + 1) * width].T
        if kind == "filter":
            own[here] -= np.eye(width)
        for shift in range(1, count):
            there = here ^ shift
            block = rows[:, there * width : (there + 1) * width]
            far[here, (shift - 1) * BASIS : shift * BASIS] = (block @ inverse).T
    return own, basis, far


def surface_table(around, rows):
    length = around * rows
    turn = np.roll(np.eye(length), 1, axis=1)
    beta = FILTER_ALPHA
    side = (11.0 + 10.0 * beta) / 16.0 * np.eye(length)
    coeffs = [(15.0 + 34.0 * beta) / 64.0, (-3.0 + 6.0 * beta) / 32.0, (1.0 - 2.0 * beta) / 64.0]
    for shift, weight in enumerate(coeffs, start=1):
        step = np.linalg.matrix_power(turn, shift)
        side = side + weight * (step + step.T)
    cycle = np.linalg.solve(np.eye(length) + beta * (turn + turn.T), side)
    return cycle.reshape(around // 2, 2 * rows, length).astype(np.float32)


def halves(table):
    high = np.asarray(table, np.float32).astype(jnp.bfloat16)
    low = (np.asarray(table, np.float64) - high.astype(np.float64)).astype(jnp.bfloat16)
    return np.stack([high, low], axis=-3)


def split(values):
    high = values.astype(jnp.bfloat16)
    return high, (values - high.astype(jnp.float32)).astype(jnp.bfloat16)


def dots(left, right, dims):
    out = None
    for a, b in ((0, 0), (1, 0), (0, 1)):
        part = lax.dot_general(
            left[a], right[b], (dims, ((), ())), preferred_element_type=jnp.float32
        )
        out = part if out is None else out + part
    return out


def outgoing(basis_ref, lines):
    return dots((basis_ref[0], basis_ref[1]), split(lines), ((1,), (1,)))


def incoming(parts, far_ref):
    return dots(split(jnp.concatenate(parts, axis=0)), (far_ref[0], far_ref[1]), ((0,), (0,)))


def own_block(lines, own_ref):
    return dots(split(lines), (own_ref[0], own_ref[1]), ((1,), (0,)))


def tile_energy(density, velocity, pressure):
    return pressure * (1.0 / (GAMMA - 1.0)) + 0.5 * density * (
        velocity[0] * velocity[0] + velocity[1] * velocity[1] + velocity[2] * velocity[2]
    )


def tile_flux(density, velocity, pressure, energy, metric, volume):
    contra = metric[0] * velocity[0] + metric[1] * velocity[1] + metric[2] * velocity[2]
    volume_contra = volume * contra
    mass = density * volume_contra
    push = volume * pressure
    pieces = [mass]
    for comp in range(3):
        pieces.append(mass * velocity[comp] + metric[comp] * push)
    pieces.append((energy + pressure) * volume_contra)
    return pieces


def core_index():
    return lax.rem(lax.axis_index("azim"), 2)


def chip_index():
    return lax.div(lax.axis_index("azim"), 2)


def ring_weights(chips, turn, wide):
    levels = chips.bit_length() - 1
    size = 2 * (levels + 1)
    sends = np.zeros((levels, 2, chips, size))
    sums = np.zeros((2, chips, size))
    unit = np.eye(size)
    for chip in range(chips):
        spot = (chip + turn) % chips
        head, tail = unit[0], unit[1]
        left = right = np.zeros(size)
        for level in range(levels):
            group = 1 << level
            inside = spot % group
            sends[level, :, chip] = head, tail
            head_in, tail_in = unit[2 * level + 2], unit[2 * level + 3]
            if (spot >> level) & 1:
                left = left + wide**inside * head_in
                head, tail = head + wide**group * head_in, tail_in + wide**group * tail
            else:
                right = right + wide ** (group - 1 - inside) * tail_in
                head, tail = head_in + wide**group * head, tail + wide**group * tail_in
        close = 1.0 / (1.0 - wide**chips)
        sums[0, chip] = left + close * wide**spot * head
        sums[1, chip] = right + close * wide ** (chips - 1 - spot) * tail
    return sends, sums


def chosen(index, values):
    if not np.any(values):
        return None
    out = jnp.float32(values[0])
    for at in range(1, len(values)):
        if values[at] != values[at - 1] or np.any(values != values[0]):
            out = jnp.where(index == at, jnp.float32(values[at]), out)
    return out


def slot(value, field, height):
    start = (value * FIELDS + field) * height
    return slice(start, start + height)


def mixed(chip, table, sources, field, height):
    total = None
    for at, source in enumerate(sources):
        for part in range(2):
            weight = chosen(chip, table[:, 2 * at + part])
            if weight is not None:
                term = weight * source[slot(part, field, height)]
                total = term if total is None else total + term
    return total


def moments(tiles, root):
    head = tail = tiles[0]
    for row in range(1, len(tiles)):
        head = tiles[row] + root * head
        tail = tail + (root**row) * tiles[row]
    return head, tail


def fetched(sources, buffers, sem, pieces):
    copies = [
        [
            pltpu.make_async_copy(source.at[where], buffer.at[there], sem.at[at, n])
            for n, (source, buffer, (where, there)) in enumerate(zip(sources, buffers, piece))
        ]
        for at, piece in enumerate(pieces)
    ]
    for group in copies:
        for copy in group:
            copy.start()
    return copies


def azim_flux_kernel(mine, density, velocity, pressure, azim_metric, volume, out, pack, *scratch):
    *buffers, flux, sem = scratch
    chunks, _, rows, planes, _ = out.shape
    core = core_index()
    start = (core if mine else 1 - core) * chunks * planes
    pieces = []
    for chunk in range(chunks):
        here, there = pl.ds(start + chunk * planes, planes), pl.ds(chunk * planes, planes)
        whole = slice(None)
        pieces.append(
            [(here, there), ((whole, here), (whole, there)), (here, there)]
            + [((whole, here), (whole, there)), (here, there)]
        )
    groups = fetched((density, velocity, pressure, azim_metric, volume), buffers, sem, pieces)
    first = core == 0
    for chunk in range(chunks):
        for copy in groups[chunk]:
            copy.wait()
        rho_in, vel_in, pres_in, metric_in, vol_in = buffers
        for plane in range(planes):
            at = chunk * planes + plane
            rho, pres = rho_in[at], pres_in[at]
            vel = [vel_in[c, at] for c in range(3)]
            energy = tile_energy(rho, vel, pres)
            metric = [metric_in[c, at] for c in range(3)]
            for f, piece in enumerate(tile_flux(rho, vel, pres, energy, metric, vol_in[at])):
                flux[f, plane] = piece
        for f in range(FIELDS):
            turned = jnp.swapaxes(flux[f], 0, 1)
            out[chunk, f] = turned
            tiles = [turned[row] for row in range(rows)]
            pack[chunk, 0, f], pack[chunk, 1, f] = moments(tiles, DERIV_ROOT)
            pack[chunk, 2, f] = jnp.where(first, tiles[0], tiles[rows - 1])


def put_moments(step, field, head, tail, low, high, pack, edge):
    on_left = lax.rem(chip_index() + step, 2) == 0
    height = head.shape[0]
    pack[slot(0, field, height)] = head
    pack[slot(1, field, height)] = tail
    for n in range(len(low)):
        pack[slot(2 + n, field, height)] = jnp.where(on_left, high[n], low[n])
        edge[slot(n, field, height)] = jnp.where(on_left, low[n], high[n])


def chip_moments_kernel(rows, keep, other, pack_a, pack_b, edge_a, edge_b):
    first = core_index() == 0
    decay, one = jnp.float32(DERIV_ROOT**rows), jnp.float32(1.0)
    near, away = jnp.where(first, decay, one), jnp.where(first, one, decay)
    height = keep.shape[3]
    for turn, (pack, edge) in enumerate(((pack_a, edge_a), (pack_b, edge_b))):
        on_left = lax.rem(chip_index() + turn, 2) == 0
        mine = first != on_left
        for f in range(FIELDS):
            head, tail, row = (keep[turn, n, f] for n in range(3))
            head_in, tail_in, row_in = (other[turn, n, f] for n in range(3))
            pack[slot(0, f, height)] = near * head + away * head_in
            pack[slot(1, f, height)] = away * tail + near * tail_in
            pack[slot(2, f, height)] = jnp.where(mine, row, row_in)
            edge[slot(0, f, height)] = jnp.where(mine, row_in, row)


def totals_kernel(table, joined, near, height, *refs):
    chip = chip_index()
    *refs, send_a, send_b = refs
    count = len(refs) // 2
    for turn, send in enumerate((send_a, send_b)):
        mine = refs[turn * count : (turn + 1) * count]
        sources = mine[:-1] if joined else mine
        for f in range(FIELDS):
            send[slot(0, f, height)] = mixed(chip, table[turn][0], sources, f, height)
            send[slot(1, f, height)] = mixed(chip, table[turn][1], sources, f, height)
        if joined:
            send[2 * FIELDS * height :] = mine[-1][...]


def ring_kernel(table, near, height, *refs):
    chip = chip_index()
    *refs, out = refs
    count = len(refs) // 2
    for turn in range(2):
        *sources, edge = refs[turn * count : (turn + 1) * count]
        on_left = lax.rem(chip + turn, 2) == 0
        start = 0 if edge.shape[0] == near * FIELDS * height else 2
        for f in range(FIELDS):
            out[turn, 0, f] = mixed(chip, table[turn][0], sources, f, height)
            out[turn, 1, f] = mixed(chip, table[turn][1], sources, f, height)
            for n in range(near):
                paired = sources[1][slot(2 + n, f, height)]
                other = edge[slot(start + n, f, height)]
                out[turn, 2 + n, f] = jnp.where(on_left, other, paired)
                out[turn, 2 + near + n, f] = jnp.where(on_left, paired, other)


def section_local_kernel(
    density,
    velocity,
    pressure,
    axial_metric,
    volume,
    radial,
    own,
    basis,
    base_out,
    scale_out,
    edge_out,
    axial_flux,
    start,
):
    planes, rows, lanes = density.shape
    for plane in range(planes):
        rho = density[plane]
        vel = [velocity[c, plane] for c in range(3)]
        pres = pressure[plane]
        vol = volume[plane]
        energy = tile_energy(rho, vel, pres)
        axial = tile_flux(rho, vel, pres, energy, [axial_metric[c, plane] for c in range(3)], vol)
        state = [rho, rho * vel[0], rho * vel[1], rho * vel[2], energy]
        for f in range(FIELDS):
            axial_flux[f, plane] = axial[f]
            start[f, plane] = state[f] + SECTION * radial[f, plane]
    scale = jnp.swapaxes(SECTION / volume[...], 0, 1)
    scale_out[0] = scale
    for f in range(FIELDS):
        flux = jnp.swapaxes(axial_flux[f], 0, 1).reshape(rows * planes, lanes)
        edge_out[:, f * rows * planes : (f + 1) * rows * planes] = outgoing(basis, flux)
        deriv = own_block(flux, own).reshape(rows, planes, lanes)
        base_out[0, f] = jnp.swapaxes(start[f], 0, 1) - scale * deriv


def section_axial_kernel(base, scale, far, *rest):
    *edges, out_kept, out_sent = rest
    fields, rows, planes, lanes = base.shape[1:]
    core = core_index()
    weights = far.at[lax.axis_index("axial")]
    for mine, out in ((core, out_kept), (1 - core, out_sent)):
        for chunk in range(2):
            at = 2 * mine + chunk
            for f in range(fields):
                spot = pl.multiple_of((at * fields + f) * rows * planes, 128)
                parts = [ref[:, pl.ds(spot, rows * planes)] for ref in edges]
                axial = incoming(parts, weights).reshape(rows, planes, lanes)
                out[chunk, f] = base[at, f] - scale[at] * axial
            out[chunk, fields] = scale[at]


def section_join_kernel(step, flux_keep, flux_in, base_keep, base_in, ring, basis, out, edge):
    rows, planes, lanes = flux_keep.shape[2:]
    first = core_index() == 0
    last = 2 * rows - 1
    width = 2 * rows * planes

    for f in range(FIELDS):
        azim = [both_row(first, flux_keep, flux_in, f, row) for row in range(last + 1)]
        left, right, before, after = (ring[0, n, f] for n in range(4))
        down = [None] * (last + 1)
        down[last] = azim[last] + DERIV_ROOT * right
        for row in range(last - 1, -1, -1):
            down[row] = azim[row] + DERIV_ROOT * down[row + 1]
        up = left
        for row in range(last + 1):
            up = azim[row] + DERIV_ROOT * up
            total = DERIV_FAR * (up - down[row])
            total = total - DERIV_NEAR * (azim[row - 1] if row > 0 else before)
            total = total + DERIV_NEAR * (azim[row + 1] if row < last else after)
            base = both_row(first, base_keep, base_in, f, row)
            scale = both_row(first, base_keep, base_in, FIELDS, row)
            out[0, f, row] = base - scale * total
        spot = (step * FIELDS + f) * width
        edge[:, spot : spot + width] = outgoing(basis, out[0, f].reshape(width, lanes))


def both_row(first, mine, theirs, field, row):
    rows = mine.shape[2]
    if row < rows:
        return jnp.where(first, mine[0, field, row], theirs[0, field, row])
    return jnp.where(first, theirs[0, field, row - rows], mine[0, field, row - rows])


def axial_local_kernel(step, values, own, out):
    weights = own.at[lax.axis_index("axial")]
    for f in range(FIELDS):
        lines = values[0, f].reshape(-1, values.shape[-1])
        out[0, f] = (lines + own_block(lines, weights)).reshape(out.shape[2:])


def axial_join_kernel(step, local, far, *rest):
    edges, (out, pack_a, pack_b, edge_a, edge_b, front) = rest[:-6], rest[-6:]
    pack, away = ((pack_a, edge_a), (pack_b, edge_b))[step]
    weights = far.at[lax.axis_index("axial")]
    rows, planes, lanes = local.shape[2:]
    width = rows * planes
    for f in range(FIELDS):
        spot = (step * FIELDS + f) * width
        axial = incoming([ref[:, spot : spot + width] for ref in edges], weights)
        axial = axial.reshape(rows, planes, lanes)
        tiles = [local[0, f, row] + axial[row] for row in range(rows)]
        for row in range(rows):
            out[0, f, row] = tiles[row]
        head, tail = moments(tiles, FILTER_ROOT)
        put_moments(step, f, head, tail, tiles[:2], tiles[rows - 2 :], pack, away)
    if step == 0:
        for row in range(rows):
            front[row : row + 1, :] = out[0, 2, row, 0:1, :] + out[0, 0, row, 0:1, :]
        for other in (pack_a, pack_b):
            other[other.shape[0] - rows :] = front[...]


def azim_local_kernel(step, values, out):
    rows = values.shape[2]
    for f in range(FIELDS):
        down = [None] * rows
        down[rows - 1] = values[0, f, rows - 1]
        for row in range(rows - 2, -1, -1):
            down[row] = values[0, f, row] + FILTER_ROOT * down[row + 1]
        up = None
        for row in range(rows):
            here = values[0, f, row]
            up = here if row == 0 else here + FILTER_ROOT * up
            total = (1.0 + FILTER_MID - FILTER_FAR) * here + FILTER_FAR * (up + down[row])
            for step, weight in ((1, FILTER_ONE), (2, FILTER_TWO)):
                if row >= step:
                    total = total + weight * values[0, f, row - step]
                if row + step < rows:
                    total = total + weight * values[0, f, row + step]
            out[0, f, row] = total


def joined_rows(upper, local, ring, field):
    rows = local.shape[2]
    one, zero = jnp.float32(1.0), jnp.float32(0.0)
    decay = jnp.float32(FILTER_ROOT**rows)
    left = jnp.where(upper, decay, one) * ring[0, 0, field]
    right = jnp.where(upper, one, decay) * ring[0, 1, field]
    low, high = jnp.where(upper, zero, one), jnp.where(upper, one, zero)
    before = [low * ring[0, 2 + n, field] for n in range(2)]
    after = [high * ring[0, 4 + n, field] for n in range(2)]
    tiles = []
    for row in range(rows):
        total = (
            local[0, field, row]
            + (FILTER_FAR * FILTER_ROOT ** (row + 1)) * left
            + (FILTER_FAR * FILTER_ROOT ** (rows - row)) * right
        )
        if row < 2:
            total = total + FILTER_TWO * before[row]
        if row == 0:
            total = total + FILTER_ONE * before[1]
        if row >= rows - 2:
            total = total + FILTER_TWO * after[row - (rows - 2)]
        if row == rows - 1:
            total = total + FILTER_ONE * after[0]
        tiles.append(total)
    return tiles


def azim_send_kernel(step, local, ring, out):
    rows = local.shape[2] // 2
    upper = 1 - core_index()
    there = local.at[:, :, pl.ds(upper * rows, rows)]
    for f in range(FIELDS):
        for row, tile in enumerate(joined_rows(upper == 1, there, ring, f)):
            out[0, f, row] = tile


def azim_keep_kernel(local, ring, out):
    for f in range(FIELDS):
        tiles = joined_rows(core_index() == 1, local, ring, f)
        out[f] = jnp.swapaxes(jnp.stack(tiles), 0, 1)


def place_rows_kernel(values, partial, out):
    for f in range(FIELDS):
        out[f] = jnp.swapaxes(values[0, f], 0, 1)


def entries_kernel(weight_table, weights, area, observers, bins, value, chosen_rows, chosen_bins):
    entries, rows, lanes = weights.shape
    observer_rows = lax.broadcasted_iota(jnp.int32, (chosen_rows.shape[0], lanes), 0)
    bin_rows = lax.broadcasted_iota(jnp.int32, (chosen_bins.shape[0], lanes), 0)
    for entry in range(entries):
        picked = weights[entry]
        found = jnp.zeros(picked.shape, jnp.float32)
        for part in range(weight_table.shape[0]):
            there = picked - part * lanes
            inside = (there >= 0) & (there < lanes)
            columns = jnp.broadcast_to(weight_table[part : part + 1, :], picked.shape)
            part_found = jnp.take_along_axis(columns, jnp.where(inside, there, 0), axis=1)
            found = jnp.where(inside, part_found, found)
        value[entry] = found * area[...]
        for row in range(rows):
            at = (row * entries + entry) * lanes
            hit = observer_rows == observers[entry, row : row + 1, :]
            chosen_rows[:, at : at + lanes] = jnp.where(hit, 1.0, 0.0).astype(jnp.bfloat16)
            hit = bin_rows == bins[entry, row : row + 1, :]
            chosen_bins[:, at : at + lanes] = jnp.where(hit, 1.0, 0.0).astype(jnp.bfloat16)


def surface_kernel(masks, around, front, *rest):
    *arrived, kept, sent, ring = rest
    rows = front.shape[0]
    chip = chip_index()
    for mask, ref in zip((0, *masks), (front, *arrived)):
        spot = pl.multiple_of(jnp.bitwise_xor(chip, mask) * rows, 8)
        ring[pl.ds(spot, rows), :] = ref[ref.shape[0] - rows :]
    surface = -1.0 + jnp.dot(
        around[chip],
        ring[...],
        precision=lax.Precision.HIGHEST,
        preferred_element_type=jnp.float32,
    )
    kept[...] = surface[: rows // 2]
    sent[...] = surface[rows // 2 :]


def signals_kernel(surface, surface_in, value, chosen_rows, chosen_bins, out, placed):
    entries, rows, lanes = value.shape
    height = out.shape[1]
    cells = jnp.where(core_index() == 0, surface[...], surface_in[...])
    for entry in range(entries):
        high, low = split(value[entry] * cells)
        for row in range(rows):
            at = (row * entries + entry) * lanes
            hit = chosen_bins[:, at : at + lanes]
            placed[:height, at : at + lanes] = hit * high[row : row + 1, :]
            placed[height:, at : at + lanes] = hit * low[row : row + 1, :]
    total = lax.dot_general(
        chosen_rows[...],
        placed[...],
        (((1,), (1,)), ((), ())),
        preferred_element_type=jnp.float32,
    )
    out[...] = total[:, :height] + total[:, height:]


def params(limit=VMEM_LIMIT):
    return pltpu.CompilerParams(vmem_limit_bytes=limit)


def cost(flops, moved):
    return pl.CostEstimate(flops=1, bytes_accessed=1, transcendentals=0)


def swap(values, axis, count, mask):
    return lax.ppermute(values, axis, [(i, i ^ mask) for i in range(count)])


def sibling(values, count):
    return lax.ppermute(values, "azim", [(i, i ^ 1) for i in range(count)])


def partner(values, count, turn, level):
    chips = count // 2
    pairs = []
    for i in range(count):
        chip, core = divmod(i, 2)
        there = ((((chip + turn) % chips) ^ ((2 << level) - 1)) - turn) % chips
        pairs.append((i, 2 * there + core))
    return lax.ppermute(values, "azim", pairs)


def waiting(kernel, count, wait):
    if not wait:
        return kernel
    return lambda *refs: kernel(*refs[:count], *refs[count + len(wait) :])


def by_chunk(kernel, blocked):
    def run(*refs):
        for step in range(2):
            pieces = [
                ref.at[step : step + 1] if cut else ref for ref, cut in zip(refs, blocked, strict=True)
            ]
            kernel(step, *pieces)

    return run


def whole_call(kernel, name, shapes, args, wait=(), scratch=()):
    whole = pl.BlockSpec(memory_space=pltpu.VMEM)
    return pl.pallas_call(
        waiting(kernel, len(args), wait),
        in_specs=[whole] * len(args) + [pl.BlockSpec(memory_space=pl.ANY)] * len(wait),
        out_specs=[whole] * len(shapes),
        out_shape=shapes,
        scratch_shapes=scratch,
        compiler_params=params(),
        cost_estimate=cost(1, 1),
        name=name,
    )(*args, *wait)


def ring_exchange(packs, arrived, edges, count, near, height, wide, wait=()):
    chips = count // 2
    levels = chips.bit_length() - 1
    tables = [ring_weights(chips, turn, wide) for turn in range(2)]
    lanes = packs[0].shape[1]
    rows = FIELDS * height
    joined = levels == 2
    sources = [[packs[turn], arrived[turn]] for turn in range(2)]
    if not joined:
        edges = [partner(edges[turn], count, 1 - turn, 0) for turn in range(2)]
    for level in range(1, levels):
        size = (2 + near if joined else 2) * rows
        args = [a for turn in range(2) for a in sources[turn] + ([edges[turn]] if joined else [])]
        sends = whole_call(
            functools.partial(totals_kernel, [t[0][level] for t in tables], joined, near, height),
            "group_totals",
            [jax.ShapeDtypeStruct((size, lanes), jnp.float32)] * 2,
            args,
            wait,
        )
        for turn in range(2):
            sources[turn].append(partner(sends[turn], count, turn, level))
    args = [
        a for turn in range(2) for a in sources[turn] + [sources[turn][-1] if joined else edges[turn]]
    ]

    def sums(wait=()):
        return whole_call(
            functools.partial(ring_kernel, [t[1] for t in tables], near, height),
            "ring_sums",
            [jax.ShapeDtypeStruct((2, 2 + 2 * near, FIELDS, height, lanes), jnp.float32)],
            args,
            wait,
        )[0]

    return sums, sends[0], [source[-1] for source in sources]


def per_device(
    density,
    velocity,
    pressure,
    axial_metric,
    azim_metric,
    volume,
    radial_term,
    panel_area,
    observer_ids,
    bin_ids,
    weight_ids,
    bin_weights,
):
    planes, rows, lanes = density.shape
    along = lax.axis_size("axial")
    around = lax.axis_size("azim")
    devices = along * around
    part = planes // 4
    lines = FIELDS * rows * part
    f32 = jnp.float32

    own_d, basis_d, far_d = map(halves, axial_tables(along, lanes, DERIV_ALPHA, "deriv"))
    own_f, basis_f, far_f = map(halves, axial_tables(along, lanes, FILTER_ALPHA, "filter"))
    filter_around = surface_table(around, rows)

    spec = pl.BlockSpec

    def every(k):
        return k

    def kept(k):
        return core_index() * 2 + k

    def sent(k):
        return (1 - core_index()) * 2 + k

    def field(where):
        return spec((part, rows, lanes), lambda k: (where(k), 0, 0))

    def vector(where, size=3):
        return spec((size, part, rows, lanes), lambda k: (0, where(k), 0, 0))

    def inner(where, size=FIELDS, tall=rows):
        return spec((1, size, tall, part, lanes), lambda k: (where(k), 0, 0, 0, 0))

    def inner_one(where, tall=rows):
        return spec((1, tall, part, lanes), lambda k: (where(k), 0, 0, 0))

    def edge(where, width=lines):
        return spec((BASIS, width), lambda k: (0, where(k)))

    def row_half(upper):
        return spec((1, FIELDS, rows, part, lanes), lambda k: (k, 0, upper(), 0, 0))

    def table(array):
        return spec((None,) + array.shape[1:], lambda k: (lax.axis_index("axial"),) + (0,) * (array.ndim - 1))

    def fixed(shape):
        return spec(shape, lambda k: (0,) * len(shape))

    def ring_spec(near):
        return spec((1, 2 + 2 * near, FIELDS, part, lanes), lambda k: (k, 0, 0, 0, 0))

    def shaped(*shape):
        return jax.ShapeDtypeStruct(shape, f32)

    def call(
        kernel, name, steps, ins, outs, shapes, args, wait=(), limit=VMEM_LIMIT, scratch=(), **more
    ):
        return pl.pallas_call(
            waiting(kernel, len(args), wait),
            grid=(steps,),
            in_specs=ins + [spec(memory_space=pl.ANY)] * len(wait),
            out_specs=outs,
            scratch_shapes=scratch,
            out_shape=shapes,
            compiler_params=params(limit),
            cost_estimate=cost(1, 1),
            name=name,
            **more,
        )(*args, *wait)

    tall = 2 * rows
    flux_scratch = pltpu.VMEM((FIELDS, part, rows, lanes), f32)
    half_shape = shaped(2, FIELDS, rows, part, lanes)
    chip_shape = shaped(2, FIELDS, tall, part, lanes)

    def apart(kernel, name, shapes, args, scratch, wait=(), limit=INPUT_LIMIT):
        several = isinstance(shapes, list)
        vmem = spec(memory_space=pltpu.VMEM)
        return pl.pallas_call(
            waiting(kernel, len(args), wait),
            in_specs=[spec(memory_space=pltpu.HBM)] * len(args)
            + [spec(memory_space=pl.ANY)] * len(wait),
            out_specs=[vmem] * len(shapes) if several else vmem,
            out_shape=shapes,
            scratch_shapes=scratch,
            compiler_params=params(limit),
            cost_estimate=cost(1, 1),
            name=name,
        )(*args, *wait)

    def azim_flux(mine, name, limit):
        one, three = (2 * part, rows, lanes), (3, 2 * part, rows, lanes)
        return apart(
            functools.partial(azim_flux_kernel, mine),
            name,
            [half_shape, shaped(2, 3, FIELDS, part, lanes)],
            (density, velocity, pressure, azim_metric, volume),
            [pltpu.VMEM(shape, f32) for shape in (one, three, one, three, one)]
            + [flux_scratch, pltpu.SemaphoreType.DMA((2, 5))],
            limit=limit,
        )

    flux_sent, pack_sent = azim_flux(False, "azim_flux_sent", INPUT_LIMIT)
    pack_in = sibling(pack_sent, around)
    flux_in = sibling(flux_sent, around)
    flux_kept, pack_kept = azim_flux(True, "azim_flux_kept", VMEM_LIMIT)
    *packs, edge_a, edge_b = whole_call(
        functools.partial(chip_moments_kernel, rows),
        "chip_moments",
        [shaped(3 * FIELDS * part, lanes)] * 2 + [shaped(FIELDS * part, lanes)] * 2,
        (pack_kept, pack_in),
    )

    arrived = [partner(packs[turn], around, turn, 0) for turn in range(2)]
    base, scale, edge_d = call(
        section_local_kernel,
        "section_local",
        4,
        [
            field(every),
            vector(every),
            field(every),
            vector(every),
            field(every),
            vector(every, FIELDS),
            table(own_d),
            fixed(basis_d.shape),
        ],
        [inner(every), inner_one(every), edge(every)],
        [
            shaped(4, FIELDS, rows, part, lanes),
            shaped(4, rows, part, lanes),
            shaped(BASIS, 4 * lines),
        ],
        (density, velocity, pressure, axial_metric, volume, radial_term, own_d, basis_d),
        wait=(packs[0], flux_in),
        scratch=[flux_scratch] * 2,
    )
    edges_d = [swap(edge_d, "axial", along, mask) for mask in range(1, along)]
    sums_d, sends_d, last_d = ring_exchange(
        packs, arrived, [edge_a, edge_b], around, 1, part, DERIV_ROOT ** (2 * rows), wait=(edge_d,)
    )

    base_kept, base_sent = whole_call(
        section_axial_kernel,
        "section_axial",
        [shaped(2, FIELDS + 1, rows, part, lanes)] * 2,
        (base, scale, jnp.asarray(far_d), *edges_d),
        wait=last_d,
    )
    base_in = sibling(base_sent, around)

    ring_d = sums_d()
    sectioned, edge_f = whole_call(
        by_chunk(section_join_kernel, [True] * 5 + [False, True, False]),
        "section_join",
        [chip_shape, shaped(BASIS, 4 * lines)],
        (flux_kept, flux_in, base_kept, base_in, ring_d, jnp.asarray(basis_f)),
    )
    edges_f = [swap(edge_f, "axial", along, mask) for mask in range(1, along)]
    (axial_local,) = whole_call(
        by_chunk(axial_local_kernel, [True, False, True]),
        "axial_local",
        [chip_shape],
        (sectioned, jnp.asarray(own_f)),
    )
    value, chosen_rows, chosen_bins = whole_call(
        entries_kernel,
        "entries",
        [
            shaped(*weight_ids.shape),
            jax.ShapeDtypeStruct((OBSERVERS, weight_ids.size), jnp.bfloat16),
            jax.ShapeDtypeStruct((TIME_BINS, weight_ids.size), jnp.bfloat16),
        ],
        (bin_weights.reshape(-1, lanes), weight_ids, panel_area, observer_ids, bin_ids),
        wait=(edge_f,),
    )
    chips = around // 2
    height = FIELDS * part
    shapes = [4 * height + tall] * 2 + [2 * height] * 2 + [tall]
    smoothed, *packs, edge_a, edge_b, front = whole_call(
        by_chunk(axial_join_kernel, [True] + [False] * along + [True] + [False] * 5),
        "axial_join",
        [chip_shape] + [shaped(size, lanes) for size in shapes],
        (axial_local, jnp.asarray(far_f), *edges_f),
        wait=(value,),
    )
    arrived = [partner(packs[turn], around, turn, 0) for turn in range(2)]

    masks = list(range(1, chips))
    fronts = [arrived[0], None, arrived[1]] if chips == 4 else [None] * (chips - 1)
    for at, mask in enumerate(masks):
        if fronts[at] is None:
            pairs = [(i, 2 * ((i // 2) ^ mask) + i % 2) for i in range(around)]
            fronts[at] = lax.ppermute(front, "azim", pairs)
    surface, surface_sent = whole_call(
        functools.partial(surface_kernel, masks),
        "surface",
        [shaped(rows, lanes)] * 2,
        (jnp.asarray(filter_around), front, *fronts),
        scratch=[pltpu.VMEM((around * rows, lanes), f32)],
    )
    surface_in = lax.ppermute(surface_sent, "azim", [(i, i + 1) for i in range(0, around, 2)])
    sums_f, sends_f, _ = ring_exchange(
        packs,
        arrived,
        [edge_a, edge_b],
        around,
        2,
        part,
        FILTER_ROOT ** (2 * rows),
        wait=(fronts[1],),
    )
    (partial,) = whole_call(
        signals_kernel,
        "signals",
        [shaped(OBSERVERS, TIME_BINS)],
        (surface, surface_in, value, chosen_rows, chosen_bins),
        wait=(sends_f,),
        scratch=[pltpu.VMEM((2 * TIME_BINS, weight_ids.size), jnp.bfloat16)],
    )
    shares = lax.all_to_all(
        partial.reshape(devices, OBSERVERS // devices, TIME_BINS),
        ("axial", "azim"),
        0,
        0,
        tiled=True,
    )
    (azim_local,) = whole_call(
        by_chunk(azim_local_kernel, [True, True]),
        "azim_local",
        [chip_shape],
        (smoothed,),
        wait=(sends_f,),
    )
    ring_f = sums_f((partial,))
    state_shape = shaped(FIELDS, planes, rows, lanes)
    (rows_sent,) = whole_call(
        by_chunk(azim_send_kernel, [True] * 3),
        "azim_join_sent",
        [half_shape],
        (azim_local, ring_f),
    )
    rows_in = sibling(rows_sent, around)
    mine = call(
        azim_keep_kernel,
        "azim_join_kept",
        2,
        [row_half(core_index), ring_spec(2)],
        vector(kept, FIELDS),
        state_shape,
        (azim_local, ring_f),
    )
    new_state = call(
        place_rows_kernel,
        "place_rows",
        2,
        [inner(every), spec(memory_space=pl.ANY)],
        vector(sent, FIELDS),
        state_shape,
        (rows_in, mine),
        input_output_aliases={1: 0},
    )
    shares, new_state = lax.optimization_barrier((shares, new_state))
    return new_state, jnp.sum(shares, axis=0)


def solution(mesh):
    placed = (
        P(None, "azim", "axial"),
        P(None, None, "azim", "axial"),
        P(None, "azim", "axial"),
        P(None, None, "azim", "axial"),
        P(None, None, "azim", "axial"),
        P(None, "azim", "axial"),
        P(None, None, "azim", "axial"),
        P("azim", "axial"),
        P(None, "azim", "axial"),
        P(None, "azim", "axial"),
        P(None, "azim", "axial"),
        P(),
    )
    return jax.shard_map(
        per_device,
        mesh=mesh,
        in_specs=placed,
        out_specs=(P(None, None, "azim", "axial"), P(("axial", "azim"), None)),
        check_vma=False,
    )
```

time: 84.3 us -> 75.1 us (0.89)
  Pallas kernels: 26 us -> 17.7 us
  waiting for transfers between devices: 23.6 us -> 29.3 us
  local copies, waits for them, and re-layouts: 5.07 us -> 0.09 us
  starting transfers between devices: 28 us -> 26.1 us
    all_to_all x1, waiting for transfers between devices: 0.01 us -> 8.31 us  [per_device(): lax.all_to_all(partial.reshape(devices, OBSERVERS // devices, TIME_BINS),...]
    ppermute x8, waiting for transfers between devices: 15.9 us -> 8.03 us  [partner(): return lax.ppermute(values, 'azim', pairs)]
    pallas_call x4 -> x2, Pallas kernels: 11.7 us -> 3.91 us  [apart(): pl.pallas_call(waiting(kernel, len(args), wait), in_specs=[spec(memory_sp...]
    pallas_call x11 -> x3, Pallas kernels: 12.3 us -> 4.59 us  [call(): pl.pallas_call(waiting(kernel, len(args), wait), grid=(steps,), in_specs=...]
    pallas_call x5 -> x14, Pallas kernels: 1.95 us -> 9.23 us  [whole_call(): pl.pallas_call(waiting(kernel, len(args), wait), in_specs=[whole] * len(a...]
    unnamed x54 -> x38, local copies, waits for them, and re-layouts: 5.07 us -> 0.09 us
    all_to_all x1, starting transfers between devices: 7.4 us -> 3.2 us  [per_device(): lax.all_to_all(partial.reshape(devices, OBSERVERS // devices, TIME_BINS),...]
    ppermute x6 -> x8, waiting for transfers between devices: 6.68 us -> 9.9 us  [the longest x1 5.55 us: per_device(): fronts[at] = lax.ppermute(front, 'azim', pairs)]
  transfers between devices with their start and end apart: 19 -> 21, of which waited for: 9 -> 14; matrix products, arithmetic and copies ran while one was open for 0% -> 0% of each run, Pallas kernels for 21% -> 16%
where the time goes in v4:
time: 75.1 us; the launch traced here: 74.8 us
  waiting for transfers between devices  29.3 us (39%)
  starting transfers between devices  26.1 us (35%)
  Pallas kernels  17.7 us (24%)
  between operations  0.95 us (1%)
    ppermute x8, starting transfers between devices, partner(): return lax.ppermute(values, 'azim', pairs)  13.8 us
    pallas_call x14, Pallas kernels, whole_call(): pl.pallas_call(waiting(kernel, len(args), wait), in_specs=[whole] * len(a...  9.23 us
    all_to_all x1, waiting for transfers between devices, per_device(): lax.all_to_all(partial.reshape(devices, OBSERVERS // devices, TIME_BINS),...  8.31 us
    ppermute x8, waiting for transfers between devices, partner(): return lax.ppermute(values, 'azim', pairs)  8.03 us
    ppermute x6, starting transfers between devices, swap(): return lax.ppermute(values, axis, [(i, i ^ mask) for i in range(count)])  6.99 us
    ppermute x1, waiting for transfers between devices, per_device(): fronts[at] = lax.ppermute(front, 'azim', pairs)  5.55 us
    pallas_call x3, Pallas kernels, call(): pl.pallas_call(waiting(kernel, len(args), wait), grid=(steps,), in_specs=...  4.59 us
    ppermute x6, waiting for transfers between devices, swap(): return lax.ppermute(values, axis, [(i, i ^ mask) for i in range(count)])  4.27 us
  transfers between devices with their start and end apart: 21, of which 14 were waited for; matrix products, arithmetic and copies ran while one was open for 0% of the time, Pallas kernels for 16%

profile of v4, /device:TPU:0, one launch (start us, length us, event | category | flops | bytes accessed | tf_op | source)
XLA Modules:
  0.0 74.8 jit_solution(9283085179164442750)
XLA Ops:
  0.7 2.6 %azim_flux_sent.1 = (f32[2,5,8,16,128]{4,3,2,1,0:T(8,128)}, f32[2,3,5,16,128]{4,3,2,1,0:T(8,128)}) custom-call(f32[64,8,128]{2,1,0:T(8,128)} %refs_0_.1, f32[3,64,8,128]{3,2,1,0:T(8,128)} %refs_1_.4, f32[64,8,128]{2,1,0:T(8,128)} %refs_2_.3, f32[3,64,8,128]{3,2,1,0:T(8,128)} %azim_metric.3, f32[64,8,128]{2,1,0:T(8,128)} %refs_4_.2), custom_call_target="tpu_custom_call" | custom-call | flops 1 | bytes 1 | tf_op jit(solution)/shard_map/azim_flux_sent/pallas_call | solution.py:770
  4.0 1.3 %azim_flux_kept.1 = (f32[2,5,8,16,128]{4,3,2,1,0:T(8,128)S(1)}, f32[2,3,5,16,128]{4,3,2,1,0:T(8,128)S(1)}) custom-call(f32[64,8,128]{2,1,0:T(8,128)S(1)} %copy-done.2, f32[3,64,8,128]{3,2,1,0:T(8,128)S(1)} %copy-done, f32[64,8,128]{2,1,0:T(8,128)S(1)} %copy-done.3, f32[3,64,8,128]{3,2,1,0:T(8,128)S(1)} %copy-done.1, f32[64,8,128]{2,1,0:T(8,128)S(1)} %copy-done.4), custom_call_target="tpu_custom_call" | custom-call | flops 1 | bytes 1 | tf_op jit(solution)/shard_map/azim_flux_kept/pallas_call | solution.py:770
  6.1 5.0 %collective-permute-start.6 = (f32[240,128]{1,0:T(8,128)S(1)}, f32[240,128]{1,0:T(8,128)S(1)}, u32[]{:S(2)}, u32[]{:S(2)}) collective-permute-start(f32[240,128]{1,0:T(8,128)S(1)} %get-tuple-element.43.refs_3_.refs_4_), channel_id=1, source_target_pairs={{0,6},{1,7},{2,4},{3,5},{4,2},{5,3},{6,0},{7,1},{8,14},{9,15},{10,... | collective-permute-start | bytes 368648 | tf_op jit(solution)/shard_map/ppermute | solution.py:607
  11.2 2.5 %section_local.1 = (f32[4,5,8,16,128]{4,3,2,1,0:T(8,128)S(1)}, f32[4,8,16,128]{3,2,1,0:T(8,128)S(1)}, f32[8,2560]{1,0:T(8,128)S(1)}) custom-call(f32[64,8,128]{2,1,0:T(8,128)S(1)} %copy-done.2, f32[3,64,8,128]{3,2,1,0:T(8,128)S(1)} %copy-done, f32[64,8,128]{2,1,0:T(8,128)S(1)} %copy-done.3, f32[3,64,8,128]{3,2,1,0:T(8,128)S(1)} %copy-done.6, ...), custom_call_target="tpu_custom_call" | custom-call | flops 1 | bytes 1 | tf_op jit(solution)/shard_map/section_local/pallas_call | solution.py:749
  13.8 1.6 %collective-permute-done.6.refs_4_.refs_5_ = f32[240,128]{1,0:T(8,128)S(1)} collective-permute-done((f32[240,128]{1,0:T(8,128)S(1)}, f32[240,128]{1,0:T(8,128)S(1)}, u32[]{:S(2)}, u32[]{:S(2)}) %collective-permute-start.6) | collective-permute-done | bytes 122912 | tf_op jit(solution)/shard_map/ppermute | solution.py:607
  15.3 2.2 %collective-permute-done.5.refs_1_ = f32[240,128]{1,0:T(8,128)S(1)} collective-permute-done((f32[240,128]{1,0:T(8,128)S(1)}, f32[240,128]{1,0:T(8,128)S(1)}, u32[]{:S(2)}, u32[]{:S(2)}) %collective-permute-start.5) | collective-permute-done | bytes 122912 | tf_op jit(solution)/shard_map/ppermute | solution.py:607
  17.6 1.8 %collective-permute-start.7 = (f32[240,128]{1,0:T(8,128)S(1)}, f32[240,128]{1,0:T(8,128)S(1)}, u32[]{:S(2)}, u32[]{:S(2)}) collective-permute-start(f32[240,128]{1,0:T(8,128)S(1)} %get-tuple-element.45), channel_id=1, source_target_pairs={{0,6},{1,7},{2,4},{3,5},{4,2},{5,3},{6,0},{7,1},{8,14},{9,15},{10,... | collective-permute-start | bytes 368648 | tf_op jit(solution)/shard_map/ppermute | solution.py:607
  19.4 2.4 %collective-permute-start.4 = (f32[8,2560]{1,0:T(8,128)S(1)}, f32[8,2560]{1,0:T(8,128)S(1)}, u32[]{:S(2)}, u32[]{:S(2)}) collective-permute-start(f32[8,2560]{1,0:T(8,128)S(1)} %get-tuple-element.41.refs_6_), channel_id=1, source_target_pairs={{0,24},{8,16},{16,8},{24,0},{1,25},{9,17},{17,9},{25,1},{2,26},{10... | collective-permute-start | bytes 245768 | tf_op jit(solution)/shard_map/ppermute | solution.py:593
  22.9 2.3 %collective-permute-done.4.refs_5_ = f32[8,2560]{1,0:T(8,128)S(1)} collective-permute-done((f32[8,2560]{1,0:T(8,128)S(1)}, f32[8,2560]{1,0:T(8,128)S(1)}, u32[]{:S(2)}, u32[]{:S(2)}) %collective-permute-start.4) | collective-permute-done | bytes 81952 | tf_op jit(solution)/shard_map/ppermute | solution.py:593
  27.7 2.2 %collective-permute-done.9.refs_3_ = f32[2,6,8,16,128]{4,3,2,1,0:T(8,128)S(1)} collective-permute-done((f32[2,6,8,16,128]{4,3,2,1,0:T(8,128)S(1)}, f32[2,6,8,16,128]{4,3,2,1,0:T(8,128)S(1)}, u32[]{:S(2)}, u32[]{:S(2)}) %collective-permute-start.9) | collective-permute-done | bytes 786464 | tf_op jit(solution)/shard_map/ppermute | solution.py:597
  31.0 1.6 %collective-permute-start.12 = (f32[8,2560]{1,0:T(8,128)S(1)}, f32[8,2560]{1,0:T(8,128)S(1)}, u32[]{:S(2)}, u32[]{:S(2)}) collective-permute-start(f32[8,2560]{1,0:T(8,128)S(1)} %get-tuple-element.50.refs_5_), channel_id=1, source_target_pairs={{0,24},{8,16},{16,8},{24,0},{1,25},{9,17},{17,9},{25,1},{2,26},{10... | collective-permute-start | bytes 245768 | tf_op jit(solution)/shard_map/ppermute | solution.py:593
  33.1 1.4 %collective-permute-start.10 = (f32[8,2560]{1,0:T(8,128)S(1)}, f32[8,2560]{1,0:T(8,128)S(1)}, u32[]{:S(2)}, u32[]{:S(2)}) collective-permute-start(f32[8,2560]{1,0:T(8,128)S(1)} %get-tuple-element.50.refs_5_), channel_id=1, source_target_pairs={{0,8},{8,0},{16,24},{24,16},{1,9},{9,1},{17,25},{25,17},{2,10},{10... | collective-permute-start | bytes 245768 | tf_op jit(solution)/shard_map/ppermute | solution.py:593
  35.3 2.6 %entries.1 = (f32[4,8,128]{2,1,0:T(8,128)S(1)}, bf16[512,4096]{1,0:T(8,128)(2,1)S(1)}, bf16[128,4096]{1,0:T(8,128)(2,1)S(1)}) custom-call(f32[2,128]{1,0:T(2,128)S(1)} %bitcast.2, s32[4,8,128]{2,1,0:T(8,128)S(1)} %copy-done.12, f32[8,128]{1,0:T(8,128)S(1)} %copy-done.16, s32[4,8,128]{2,1,0:T(8,128)S(1)} %copy-done.13, s32[4,8,128]{2,1,0:T(8,128)S(1)} %copy-done.14, ...), custom_call_target="tpu_custom_call" | custom-call | flops 1 | bytes 1 | tf_op jit(solution)/shard_map/entries/pallas_call | solution.py:629
  39.0 2.1 %collective-permute-start.13 = (f32[336,128]{1,0:T(8,128)S(1)}, f32[336,128]{1,0:T(8,128)S(1)}, u32[]{:S(2)}, u32[]{:S(2)}) collective-permute-start(f32[336,128]{1,0:T(8,128)S(1)} %get-tuple-element.53.refs_0_), channel_id=1, source_target_pairs={{0,2},{1,3},{2,0},{3,1},{4,6},{5,7},{6,4},{7,5},{8,10},{9,11},{10,... | collective-permute-start | bytes 516104 | tf_op jit(solution)/shard_map/ppermute | solution.py:607
  41.1 2.1 %collective-permute-start.15 = (f32[336,128]{1,0:T(8,128)S(1)}, f32[336,128]{1,0:T(8,128)S(1)}, u32[]{:S(2)}, u32[]{:S(2)}) collective-permute-start(f32[336,128]{1,0:T(8,128)S(1)} %get-tuple-element.54.refs_3_.refs_4_), channel_id=1, source_target_pairs={{0,6},{1,7},{2,4},{3,5},{4,2},{5,3},{6,0},{7,1},{8,14},{9,15},{10,... | collective-permute-start | bytes 516104 | tf_op jit(solution)/shard_map/ppermute | solution.py:607
  43.2 5.6 %collective-permute-done.14.rest_1_.refs_6_ = f32[16,128]{1,0:T(8,128)S(1)} collective-permute-done((f32[16,128]{1,0:T(8,128)S(1)}, f32[16,128]{1,0:T(8,128)S(1)}, u32[]{:S(2)}, u32[]{:S(2)}) %collective-permute-start.14) | collective-permute-done | bytes 8224 | tf_op jit(solution)/shard_map/ppermute | solution.py:886
  48.8 2.4 %collective-permute-done.15.rest_2_.refs_4_.refs_5_ = f32[336,128]{1,0:T(8,128)S(1)} collective-permute-done((f32[336,128]{1,0:T(8,128)S(1)}, f32[336,128]{1,0:T(8,128)S(1)}, u32[]{:S(2)}, u32[]{:S(2)}) %collective-permute-start.15) | collective-permute-done | bytes 172064 | tf_op jit(solution)/shard_map/ppermute | solution.py:607
  51.9 2.0 %collective-permute-start.17 = (f32[320,128]{1,0:T(8,128)S(1)}, f32[320,128]{1,0:T(8,128)S(1)}, u32[]{:S(2)}, u32[]{:S(2)}) collective-permute-start(f32[320,128]{1,0:T(8,128)S(1)} %get-tuple-element.61.refs_5_.refs_1_), channel_id=1, source_target_pairs={{0,6},{1,7},{2,4},{3,5},{4,2},{5,3},{6,0},{7,1},{8,14},{9,15},{10,... | collective-permute-start | bytes 491528 | tf_op jit(solution)/shard_map/ppermute | solution.py:607
  54.1 1.3 %collective-permute-start.16 = (f32[8,128]{1,0:T(8,128)S(1)}, f32[8,128]{1,0:T(8,128)S(1)}, u32[]{:S(2)}, u32[]{:S(2)}) collective-permute-start(f32[8,128]{1,0:T(8,128)S(1)} %get-tuple-element.56), channel_id=1, source_target_pairs={{0,1},{2,3},{4,5},{6,7},{8,9},{10,11},{12,13},{14,15},{16,17},{18,... | collective-permute-start | bytes 12296 | tf_op jit(solution)/shard_map/ppermute | solution.py:894
  56.2 2.2 %signals.1.refs_8_ = f32[512,128]{1,0:T(8,128)} custom-call(f32[8,128]{1,0:T(8,128)S(1)} %get-tuple-element.55.refs_0_, f32[8,128]{1,0:T(8,128)S(1)} %collective-permute-done.16.refs_1_, f32[4,8,128]{2,1,0:T(8,128)S(1)} %get-tuple-element.51.refs_5_.refs_2_, bf16[512,4096]{1,0:T(8,128)(2,1)S(1)} %get-tuple-element.57.refs_3_, ...), custom_call_target="tpu_custom_call" | custom-call | flops 1 | bytes 1 | tf_op jit(solution)/shard_map/signals/pallas_call | solution.py:629
  58.4 1.8 %collective-permute-done.17.refs_2_.refs_3_ = f32[320,128]{1,0:T(8,128)S(1)} collective-permute-done((f32[320,128]{1,0:T(8,128)S(1)}, f32[320,128]{1,0:T(8,128)S(1)}, u32[]{:S(2)}, u32[]{:S(2)}) %collective-permute-start.17) | collective-permute-done | bytes 163872 | tf_op jit(solution)/shard_map/ppermute | solution.py:607
  60.5 3.2 %all-to-all-start = ((f32[32,16,128]{2,1,0:T(8,128)}), f32[32,16,128]{2,1,0:T(8,128)S(1)}, u32[]{:S(2)}, u32[]{:S(2)}) async-start(f32[32,16,128]{2,1,0:T(8,128)} %bitcast.1), calls=%async_computation | async-start | bytes 524288 | tf_op jit(solution)/shard_map/all_to_all | solution.py:913
  63.7 1.2 %azim_join_kept.1.partial = f32[5,64,8,128]{3,2,1,0:T(8,128)} custom-call(f32[2,5,16,16,128]{4,3,2,1,0:T(8,128)S(1)} %azim_local.1.refs_0_.local, f32[2,6,5,16,128]{4,3,2,1,0:T(8,128)S(1)} %ring_sums.3.refs_1_.ring), custom_call_target="tpu_custom_call" | custom-call | flops 1 | bytes 1 | tf_op jit(solution)/shard_map/azim_join_kept/pallas_call | solution.py:749
  65.8 8.3 %all-to-all-done = f32[32,16,128]{2,1,0:T(8,128)S(1)} async-done(((f32[32,16,128]{2,1,0:T(8,128)}), f32[32,16,128]{2,1,0:T(8,128)S(1)}, u32[]{:S(2)}, u32[]{:S(2)}) %all-to-all-start) | async-done | bytes 262176 | tf_op jit(solution)/shard_map/all_to_all | solution.py:913
  (76 shorter events, 12.1 us)
Async XLA Ops:
  3.3 7.9 %collective-permute-start = (f32[2,5,8,16,128]{4,3,2,1,0:T(8,128)}, f32[2,5,8,16,128]{4,3,2,1,0:T(8,128)S(1)}, u32[]{:S(2)}, u32[]{:S(2)}) collective-permute-start(f32[2,5,8,16,128]{4,3,2,1,0:T(8,128)} %get-tuple-element.35), channel_id=1, source_target_pairs={{0,1},{1,0},{2,3},{3,2},{4,5},{5,4},{6,7},{7,6},{8,9},{9,8},{10,11... | collective-permute-start | bytes 1966088 | tf_op jit(solution)/shard_map/ppermute | solution.py:597
  3.8 7.4 %copy-start.17 = (bf16[2,8,128]{2,1,0:T(8,128)(2,1)S(1)}, bf16[2,8,128]{2,1,0:T(8,128)(2,1)}, u32[]{:S(2)}) copy-start(bf16[2,8,128]{2,1,0:T(8,128)(2,1)} %constant.17.clone.refs_7_) | copy-start | bytes 12292
  3.8 2.3 %collective-permute-start.1 = (f32[2,3,5,16,128]{4,3,2,1,0:T(8,128)}, f32[2,3,5,16,128]{4,3,2,1,0:T(8,128)S(1)}, u32[]{:S(2)}, u32[]{:S(2)}) collective-permute-start(f32[2,3,5,16,128]{4,3,2,1,0:T(8,128)} %get-tuple-element.37), channel_id=1, source_target_pairs={{0,1},{1,0},{2,3},{3,2},{4,5},{5,4},{6,7},{7,6},{8,9},{9,8},{10,11... | collective-permute-start | bytes 737288 | tf_op jit(solution)/shard_map/ppermute | solution.py:597
  6.1 9.2 %collective-permute-start.6 = (f32[240,128]{1,0:T(8,128)S(1)}, f32[240,128]{1,0:T(8,128)S(1)}, u32[]{:S(2)}, u32[]{:S(2)}) collective-permute-start(f32[240,128]{1,0:T(8,128)S(1)} %get-tuple-element.43.refs_3_.refs_4_), channel_id=1, source_target_pairs={{0,6},{1,7},{2,4},{3,5},{4,2},{5,3},{6,0},{7,1},{8,14},{9,15},{10,... | collective-permute-start | bytes 368648 | tf_op jit(solution)/shard_map/ppermute | solution.py:607
  11.2 15.6 %copy-start.10 = (bf16[4,2,24,128]{3,2,1,0:T(8,128)(2,1)S(1)}, bf16[4,2,24,128]{3,2,1,0:T(8,128)(2,1)}, u32[]{:S(2)}) copy-start(bf16[4,2,24,128]{3,2,1,0:T(8,128)(2,1)} %constant.18.clone.refs_2_) | copy-start | bytes 147460
  11.2 6.4 %collective-permute-start.5 = (f32[240,128]{1,0:T(8,128)S(1)}, f32[240,128]{1,0:T(8,128)S(1)}, u32[]{:S(2)}, u32[]{:S(2)}) collective-permute-start(f32[240,128]{1,0:T(8,128)S(1)} %get-tuple-element.38.refs_8_.refs_0_), channel_id=1, source_target_pairs={{0,2},{1,3},{2,0},{3,1},{4,6},{5,7},{6,4},{7,5},{8,10},{9,11},{10,... | collective-permute-start | bytes 368648 | tf_op jit(solution)/shard_map/ppermute | solution.py:607
  17.6 9.2 %collective-permute-start.7 = (f32[240,128]{1,0:T(8,128)S(1)}, f32[240,128]{1,0:T(8,128)S(1)}, u32[]{:S(2)}, u32[]{:S(2)}) collective-permute-start(f32[240,128]{1,0:T(8,128)S(1)} %get-tuple-element.45), channel_id=1, source_target_pairs={{0,6},{1,7},{2,4},{3,5},{4,2},{5,3},{6,0},{7,1},{8,14},{9,15},{10,... | collective-permute-start | bytes 368648 | tf_op jit(solution)/shard_map/ppermute | solution.py:607
  19.4 7.4 %collective-permute-start.8 = (f32[240,128]{1,0:T(8,128)S(1)}, f32[240,128]{1,0:T(8,128)S(1)}, u32[]{:S(2)}, u32[]{:S(2)}) collective-permute-start(f32[240,128]{1,0:T(8,128)S(1)} %get-tuple-element.46), channel_id=1, source_target_pairs={{0,2},{1,3},{2,0},{3,1},{4,6},{5,7},{6,4},{7,5},{8,10},{9,11},{10,... | collective-permute-start | bytes 368648 | tf_op jit(solution)/shard_map/ppermute | solution.py:607
  19.4 5.8 %collective-permute-start.4 = (f32[8,2560]{1,0:T(8,128)S(1)}, f32[8,2560]{1,0:T(8,128)S(1)}, u32[]{:S(2)}, u32[]{:S(2)}) collective-permute-start(f32[8,2560]{1,0:T(8,128)S(1)} %get-tuple-element.41.refs_6_), channel_id=1, source_target_pairs={{0,24},{8,16},{16,8},{24,0},{1,25},{9,17},{17,9},{25,1},{2,26},{10... | collective-permute-start | bytes 245768 | tf_op jit(solution)/shard_map/ppermute | solution.py:593
  21.9 4.4 %collective-permute-start.3 = (f32[8,2560]{1,0:T(8,128)S(1)}, f32[8,2560]{1,0:T(8,128)S(1)}, u32[]{:S(2)}, u32[]{:S(2)}) collective-permute-start(f32[8,2560]{1,0:T(8,128)S(1)} %get-tuple-element.41.refs_6_), channel_id=1, source_target_pairs={{0,16},{8,24},{16,0},{24,8},{1,17},{9,25},{17,1},{25,9},{2,18},{10... | collective-permute-start | bytes 245768 | tf_op jit(solution)/shard_map/ppermute | solution.py:593
  22.4 4.4 %collective-permute-start.2 = (f32[8,2560]{1,0:T(8,128)S(1)}, f32[8,2560]{1,0:T(8,128)S(1)}, u32[]{:S(2)}, u32[]{:S(2)}) collective-permute-start(f32[8,2560]{1,0:T(8,128)S(1)} %get-tuple-element.41.refs_6_), channel_id=1, source_target_pairs={{0,8},{8,0},{16,24},{24,16},{1,9},{9,1},{17,25},{25,17},{2,10},{10... | collective-permute-start | bytes 245768 | tf_op jit(solution)/shard_map/ppermute | solution.py:593
  27.6 2.4 %collective-permute-start.9 = (f32[2,6,8,16,128]{4,3,2,1,0:T(8,128)S(1)}, f32[2,6,8,16,128]{4,3,2,1,0:T(8,128)S(1)}, u32[]{:S(2)}, u32[]{:S(2)}) collective-permute-start(f32[2,6,8,16,128]{4,3,2,1,0:T(8,128)S(1)} %get-tuple-element.48), channel_id=1, source_target_pairs={{0,1},{1,0},{2,3},{3,2},{4,5},{5,4},{6,7},{7,6},{8,9},{9,8},{10,11... | collective-permute-start | bytes 2359304 | tf_op jit(solution)/shard_map/ppermute | solution.py:597
  31.0 6.9 %collective-permute-start.12 = (f32[8,2560]{1,0:T(8,128)S(1)}, f32[8,2560]{1,0:T(8,128)S(1)}, u32[]{:S(2)}, u32[]{:S(2)}) collective-permute-start(f32[8,2560]{1,0:T(8,128)S(1)} %get-tuple-element.50.refs_5_), channel_id=1, source_target_pairs={{0,24},{8,16},{16,8},{24,0},{1,25},{9,17},{17,9},{25,1},{2,26},{10... | collective-permute-start | bytes 245768 | tf_op jit(solution)/shard_map/ppermute | solution.py:593
  32.6 5.6 %collective-permute-start.11 = (f32[8,2560]{1,0:T(8,128)S(1)}, f32[8,2560]{1,0:T(8,128)S(1)}, u32[]{:S(2)}, u32[]{:S(2)}) collective-permute-start(f32[8,2560]{1,0:T(8,128)S(1)} %get-tuple-element.50.refs_5_), channel_id=1, source_target_pairs={{0,16},{8,24},{16,0},{24,8},{1,17},{9,25},{17,1},{25,9},{2,18},{10... | collective-permute-start | bytes 245768 | tf_op jit(solution)/shard_map/ppermute | solution.py:593
  33.1 5.2 %collective-permute-start.10 = (f32[8,2560]{1,0:T(8,128)S(1)}, f32[8,2560]{1,0:T(8,128)S(1)}, u32[]{:S(2)}, u32[]{:S(2)}) collective-permute-start(f32[8,2560]{1,0:T(8,128)S(1)} %get-tuple-element.50.refs_5_), channel_id=1, source_target_pairs={{0,8},{8,0},{16,24},{24,16},{1,9},{9,1},{17,25},{25,17},{2,10},{10... | collective-permute-start | bytes 245768 | tf_op jit(solution)/shard_map/ppermute | solution.py:593
  35.3 18.7 %copy-start.11 = (f32[4,16,64]{2,1,0:T(8,128)S(1)}, f32[4,16,64]{2,1,0:T(8,128)}, u32[]{:S(2)}) copy-start(f32[4,16,64]{2,1,0:T(8,128)} %constant.22.clone.around) | copy-start | bytes 49156
  39.0 9.7 %collective-permute-start.13 = (f32[336,128]{1,0:T(8,128)S(1)}, f32[336,128]{1,0:T(8,128)S(1)}, u32[]{:S(2)}, u32[]{:S(2)}) collective-permute-start(f32[336,128]{1,0:T(8,128)S(1)} %get-tuple-element.53.refs_0_), channel_id=1, source_target_pairs={{0,2},{1,3},{2,0},{3,1},{4,6},{5,7},{6,4},{7,5},{8,10},{9,11},{10,... | collective-permute-start | bytes 516104 | tf_op jit(solution)/shard_map/ppermute | solution.py:607
  41.1 10.1 %collective-permute-start.15 = (f32[336,128]{1,0:T(8,128)S(1)}, f32[336,128]{1,0:T(8,128)S(1)}, u32[]{:S(2)}, u32[]{:S(2)}) collective-permute-start(f32[336,128]{1,0:T(8,128)S(1)} %get-tuple-element.54.refs_3_.refs_4_), channel_id=1, source_target_pairs={{0,6},{1,7},{2,4},{3,5},{4,2},{5,3},{6,0},{7,1},{8,14},{9,15},{10,... | collective-permute-start | bytes 516104 | tf_op jit(solution)/shard_map/ppermute | solution.py:607
  43.2 5.6 %collective-permute-start.14 = (f32[16,128]{1,0:T(8,128)S(1)}, f32[16,128]{1,0:T(8,128)S(1)}, u32[]{:S(2)}, u32[]{:S(2)}) collective-permute-start(f32[16,128]{1,0:T(8,128)S(1)} %get-tuple-element.52.front), channel_id=1, source_target_pairs={{0,4},{1,5},{2,6},{3,7},{4,0},{5,1},{6,2},{7,3},{8,12},{9,13},{10,... | collective-permute-start | bytes 24584 | tf_op jit(solution)/shard_map/ppermute | solution.py:886
  51.2 7.2 %collective-permute-start.18 = (f32[320,128]{1,0:T(8,128)S(1)}, f32[320,128]{1,0:T(8,128)S(1)}, u32[]{:S(2)}, u32[]{:S(2)}) collective-permute-start(f32[320,128]{1,0:T(8,128)S(1)} %get-tuple-element.63), channel_id=1, source_target_pairs={{0,2},{1,3},{2,0},{3,1},{4,6},{5,7},{6,4},{7,5},{8,10},{9,11},{10,... | collective-permute-start | bytes 491528 | tf_op jit(solution)/shard_map/ppermute | solution.py:607
  51.9 8.3 %collective-permute-start.17 = (f32[320,128]{1,0:T(8,128)S(1)}, f32[320,128]{1,0:T(8,128)S(1)}, u32[]{:S(2)}, u32[]{:S(2)}) collective-permute-start(f32[320,128]{1,0:T(8,128)S(1)} %get-tuple-element.61.refs_5_.refs_1_), channel_id=1, source_target_pairs={{0,6},{1,7},{2,4},{3,5},{4,2},{5,3},{6,0},{7,1},{8,14},{9,15},{10,... | collective-permute-start | bytes 491528 | tf_op jit(solution)/shard_map/ppermute | solution.py:607
  54.1 2.1 %collective-permute-start.16 = (f32[8,128]{1,0:T(8,128)S(1)}, f32[8,128]{1,0:T(8,128)S(1)}, u32[]{:S(2)}, u32[]{:S(2)}) collective-permute-start(f32[8,128]{1,0:T(8,128)S(1)} %get-tuple-element.56), channel_id=1, source_target_pairs={{0,1},{2,3},{4,5},{6,7},{8,9},{10,11},{12,13},{14,15},{16,17},{18,... | collective-permute-start | bytes 12296 | tf_op jit(solution)/shard_map/ppermute | solution.py:894
  60.5 4.4 %collective-permute-start.19 = (f32[2,5,8,16,128]{4,3,2,1,0:T(8,128)S(1)}, f32[2,5,8,16,128]{4,3,2,1,0:T(8,128)S(1)}, u32[]{:S(2)}, u32[]{:S(2)}) collective-permute-start(f32[2,5,8,16,128]{4,3,2,1,0:T(8,128)S(1)} %azim_join_sent.1), channel_id=1, source_target_pairs={{0,1},{1,0},{2,3},{3,2},{4,5},{5,4},{6,7},{7,6},{8,9},{9,8},{10,11... | collective-permute-start | bytes 1966088 | tf_op jit(solution)/shard_map/ppermute | solution.py:597
  60.5 13.6 %all-to-all-start = ((f32[32,16,128]{2,1,0:T(8,128)}), f32[32,16,128]{2,1,0:T(8,128)S(1)}, u32[]{:S(2)}, u32[]{:S(2)}) async-start(f32[32,16,128]{2,1,0:T(8,128)} %bitcast.1), calls=%async_computation | async-start | bytes 524288 | tf_op jit(solution)/shard_map/all_to_all | solution.py:913
  (16 other events, 53.8 us)

commit v5 on v4

--- a/solution.py
+++ b/solution.py
@@ -376,30 +376,65 @@
         base_out[0, f] = jnp.swapaxes(start[f], 0, 1) - scale * deriv
 
 
-def section_axial_kernel(base, scale, far, *rest):
-    *edges, out_kept, out_sent = rest
+def section_split_kernel(base, scale, edge, kept, sent):
     fields, rows, planes, lanes = base.shape[1:]
+    size = rows * planes
     core = core_index()
-    weights = far.at[lax.axis_index("axial")]
-    for mine, out in ((core, out_kept), (1 - core, out_sent)):
+    for mine, out in ((core, kept), (1 - core, sent)):
         for chunk in range(2):
             at = 2 * mine + chunk
+            for f in range(fields + 1):
+                spot = (chunk * (fields + 1) + f) * size
+                piece = base[at, f] if f < fields else scale[at]
+                out[spot : spot + size] = piece.reshape(size, lanes)
             for f in range(fields):
-                spot = pl.multiple_of((at * fields + f) * rows * planes, 128)
-                parts = [ref[:, pl.ds(spot, rows * planes)] for ref in edges]
-                axial = incoming(parts, weights).reshape(rows, planes, lanes)
-                out[chunk, f] = base[at, f] - scale[at] * axial
-            out[chunk, fields] = scale[at]
-
-
-def section_join_kernel(step, flux_keep, flux_in, base_keep, base_in, ring, basis, out, edge):
+                from_spot = pl.multiple_of((at * fields + f) * size, 128)
+                spot = 2 * (fields + 1) * size + (chunk * fields + f) * BASIS
+                out[spot : spot + BASIS] = edge[:, pl.ds(from_spot, size)]
+
+
+def edge_both_kernel(kept, arrived, edge):
+    lanes = kept.shape[1]
+    start = kept.shape[0] - 2 * FIELDS * BASIS
+    first = core_index() == 0
+    for at in range(2 * FIELDS):
+        piece = slice(start + at * BASIS, start + (at + 1) * BASIS)
+        mine, theirs = kept[piece], arrived[piece]
+        spot = 2 * at * lanes
+        edge[:, spot : spot + lanes] = jnp.where(first, mine, theirs)
+        edge[:, spot + lanes : spot + 2 * lanes] = jnp.where(first, theirs, mine)
+
+
+def both_row(first, mine, theirs, row):
+    rows = mine.shape[0]
+    if row < rows:
+        return jnp.where(first, mine[row], theirs[row])
+    return jnp.where(first, theirs[row - rows], mine[row - rows])
+
+
+def section_join_kernel(
+    step, flux_keep, flux_in, base_keep, base_in, ring, basis, far, *rest
+):
+    *edges, out, edge = rest
     rows, planes, lanes = flux_keep.shape[2:]
     first = core_index() == 0
     last = 2 * rows - 1
     width = 2 * rows * planes
-
+    size = rows * planes
+    weights = far.at[lax.axis_index("axial")]
+
+    def base_rows(f):
+        spot = (step * (FIELDS + 1) + f) * size
+        halves = [ref[spot : spot + size].reshape(rows, planes, lanes) for ref in (base_keep, base_in)]
+        return [both_row(first, *halves, row) for row in range(last + 1)]
+
+    scale = base_rows(FIELDS)
     for f in range(FIELDS):
-        azim = [both_row(first, flux_keep, flux_in, f, row) for row in range(last + 1)]
+        spot = (step * FIELDS + f) * width
+        axial = incoming([ref[:, spot : spot + width] for ref in edges], weights)
+        axial = axial.reshape(2 * rows, planes, lanes)
+        base = base_rows(f)
+        azim = [both_row(first, flux_keep[0, f], flux_in[0, f], row) for row in range(last + 1)]
         left, right, before, after = (ring[0, n, f] for n in range(4))
         down = [None] * (last + 1)
         down[last] = azim[last] + DERIV_ROOT * right
@@ -408,21 +443,11 @@
         up = left
         for row in range(last + 1):
             up = azim[row] + DERIV_ROOT * up
-            total = DERIV_FAR * (up - down[row])
+            total = axial[row] + DERIV_FAR * (up - down[row])
             total = total - DERIV_NEAR * (azim[row - 1] if row > 0 else before)
             total = total + DERIV_NEAR * (azim[row + 1] if row < last else after)
-            base = both_row(first, base_keep, base_in, f, row)
-            scale = both_row(first, base_keep, base_in, FIELDS, row)
-            out[0, f, row] = base - scale * total
-        spot = (step * FIELDS + f) * width
+            out[0, f, row] = base[row] - scale[row] * total
         edge[:, spot : spot + width] = outgoing(basis, out[0, f].reshape(width, lanes))
-
-
-def both_row(first, mine, theirs, field, row):
-    rows = mine.shape[2]
-    if row < rows:
-        return jnp.where(first, mine[0, field, row], theirs[0, field, row])
-    return jnp.where(first, theirs[0, field, row - rows], mine[0, field, row - rows])
 
 
 def axial_local_kernel(step, values, own, out):
@@ -673,7 +698,7 @@
             wait,
         )[0]
 
-    return sums, sends[0], [source[-1] for source in sources]
+    return sums, sends[0]
 
 
 def per_device(
@@ -827,26 +852,37 @@
         wait=(packs[0], flux_in),
         scratch=[flux_scratch] * 2,
     )
+    flat = shaped(2 * (FIELDS + 1) * rows * part + 2 * FIELDS * BASIS, lanes)
+    base_kept, base_sent = whole_call(
+        section_split_kernel, "section_split", [flat, flat], (base, scale, edge_d)
+    )
+    base_in = sibling(base_sent, around)
+    (edge_d,) = whole_call(
+        edge_both_kernel, "edge_both", [shaped(BASIS, 4 * lines)], (base_kept, base_in)
+    )
     edges_d = [swap(edge_d, "axial", along, mask) for mask in range(1, along)]
-    sums_d, sends_d, last_d = ring_exchange(
-        packs, arrived, [edge_a, edge_b], around, 1, part, DERIV_ROOT ** (2 * rows), wait=(edge_d,)
-    )
-
-    base_kept, base_sent = whole_call(
-        section_axial_kernel,
-        "section_axial",
-        [shaped(2, FIELDS + 1, rows, part, lanes)] * 2,
-        (base, scale, jnp.asarray(far_d), *edges_d),
-        wait=last_d,
-    )
-    base_in = sibling(base_sent, around)
+    sums_d, sends_d = ring_exchange(
+        packs, arrived, [edge_a, edge_b], around, 1, part, DERIV_ROOT ** (2 * rows)
+    )
 
     ring_d = sums_d()
     sectioned, edge_f = whole_call(
-        by_chunk(section_join_kernel, [True] * 5 + [False, True, False]),
+        by_chunk(
+            section_join_kernel,
+            [True] * 2 + [False] * 2 + [True] + [False] * (along + 1) + [True, False],
+        ),
         "section_join",
         [chip_shape, shaped(BASIS, 4 * lines)],
-        (flux_kept, flux_in, base_kept, base_in, ring_d, jnp.asarray(basis_f)),
+        (
+            flux_kept,
+            flux_in,
+            base_kept,
+            base_in,
+            ring_d,
+            jnp.asarray(basis_f),
+            jnp.asarray(far_d),
+            *edges_d,
+        ),
     )
     edges_f = [swap(edge_f, "axial", along, mask) for mask in range(1, along)]
     (axial_local,) = whole_call(
@@ -892,7 +928,7 @@
         scratch=[pltpu.VMEM((around * rows, lanes), f32)],
     )
     surface_in = lax.ppermute(surface_sent, "azim", [(i, i + 1) for i in range(0, around, 2)])
-    sums_f, sends_f, _ = ring_exchange(
+    sums_f, sends_f = ring_exchange(
         packs,
         arrived,
         [edge_a, edge_b],

time: 75.1 us -> 73 us (0.972)
  waiting for transfers between devices: 29.3 us -> 26.9 us
    ppermute x6, waiting for transfers between devices: 4.27 us -> 0.73 us  [swap(): return lax.ppermute(values, axis, [(i, i ^ mask) for i in range(count)])]
    ppermute x8, waiting for transfers between devices: 8.03 us -> 10.7 us  [partner(): return lax.ppermute(values, 'azim', pairs)]
    ppermute x4, waiting for transfers between devices: 3.04 us -> 0.83 us  [sibling(): return lax.ppermute(values, 'azim', [(i, i ^ 1) for i in range(count)])]
    ppermute x1, waiting for transfers between devices: 5.55 us -> 6.33 us  [per_device(): fronts[at] = lax.ppermute(front, 'azim', pairs)]
    pallas_call x14 -> x15, Pallas kernels: 9.23 us -> 9.14 us  [whole_call(): pl.pallas_call(waiting(kernel, len(args), wait), in_specs=[whole] * len(a...]
  transfers between devices with their start and end apart: 21 -> 21, of which waited for: 14 -> 11; matrix products, arithmetic and copies ran while one was open for 0% -> 0% of each run, Pallas kernels for 16% -> 13%
where the time goes in v5:
time: 73 us; the launch traced here: 72.6 us
  waiting for transfers between devices  26.9 us (37%)
  starting transfers between devices  26.4 us (36%)
  Pallas kernels  17.6 us (24%)
  between operations  0.97 us (1%)
    ppermute x8, starting transfers between devices, partner(): return lax.ppermute(values, 'azim', pairs)  13.2 us
    ppermute x8, waiting for transfers between devices, partner(): return lax.ppermute(values, 'azim', pairs)  10.7 us
    pallas_call x15, Pallas kernels, whole_call(): pl.pallas_call(waiting(kernel, len(args), wait), in_specs=[whole] * len(a...  9.14 us
    all_to_all x1, waiting for transfers between devices, per_device(): lax.all_to_all(partial.reshape(devices, OBSERVERS // devices, TIME_BINS),...  8.31 us
    ppermute x6, starting transfers between devices, swap(): return lax.ppermute(values, axis, [(i, i ^ mask) for i in range(count)])  7.08 us
    ppermute x1, waiting for transfers between devices, per_device(): fronts[at] = lax.ppermute(front, 'azim', pairs)  6.33 us
    pallas_call x3, Pallas kernels, call(): pl.pallas_call(waiting(kernel, len(args), wait), grid=(steps,), in_specs=...  4.56 us
    pallas_call x2, Pallas kernels, apart(): pl.pallas_call(waiting(kernel, len(args), wait), in_specs=[spec(memory_sp...  3.91 us
  transfers between devices with their start and end apart: 21, of which 11 were waited for; matrix products, arithmetic and copies ran while one was open for 0% of the time, Pallas kernels for 13%

profile of v5, /device:TPU:0, one launch (start us, length us, event | category | flops | bytes accessed | tf_op | source)
XLA Modules:
  0.0 72.6 jit_solution(9114439570443665327)
XLA Ops:
  0.7 2.6 %azim_flux_sent.1 = (f32[2,5,8,16,128]{4,3,2,1,0:T(8,128)}, f32[2,3,5,16,128]{4,3,2,1,0:T(8,128)}) custom-call(f32[64,8,128]{2,1,0:T(8,128)} %refs_0_.1, f32[3,64,8,128]{3,2,1,0:T(8,128)} %refs_1_.4, f32[64,8,128]{2,1,0:T(8,128)} %refs_2_.2, f32[3,64,8,128]{3,2,1,0:T(8,128)} %azim_metric.3, f32[64,8,128]{2,1,0:T(8,128)} %refs_4_.2), custom_call_target="tpu_custom_call" | custom-call | flops 1 | bytes 1 | tf_op jit(solution)/shard_map/azim_flux_sent/pallas_call | solution.py:795
  4.0 1.3 %azim_flux_kept.1 = (f32[2,5,8,16,128]{4,3,2,1,0:T(8,128)S(1)}, f32[2,3,5,16,128]{4,3,2,1,0:T(8,128)S(1)}) custom-call(f32[64,8,128]{2,1,0:T(8,128)S(1)} %copy-done.2, f32[3,64,8,128]{3,2,1,0:T(8,128)S(1)} %copy-done, f32[64,8,128]{2,1,0:T(8,128)S(1)} %copy-done.3, f32[3,64,8,128]{3,2,1,0:T(8,128)S(1)} %copy-done.1, f32[64,8,128]{2,1,0:T(8,128)S(1)} %copy-done.4), custom_call_target="tpu_custom_call" | custom-call | flops 1 | bytes 1 | tf_op jit(solution)/shard_map/azim_flux_kept/pallas_call | solution.py:795
  6.2 2.5 %section_local.1 = (f32[4,5,8,16,128]{4,3,2,1,0:T(8,128)S(1)}, f32[4,8,16,128]{3,2,1,0:T(8,128)S(1)}, f32[8,2560]{1,0:T(8,128)S(1)}) custom-call(f32[64,8,128]{2,1,0:T(8,128)S(1)} %copy-done.2, f32[3,64,8,128]{3,2,1,0:T(8,128)S(1)} %copy-done, f32[64,8,128]{2,1,0:T(8,128)S(1)} %copy-done.3, f32[3,64,8,128]{3,2,1,0:T(8,128)S(1)} %copy-done.6, ...), custom_call_target="tpu_custom_call" | custom-call | flops 1 | bytes 1 | tf_op jit(solution)/shard_map/section_local/pallas_call | solution.py:774
  9.3 4.7 %collective-permute-start.4 = (f32[240,128]{1,0:T(8,128)S(1)}, f32[240,128]{1,0:T(8,128)S(1)}, u32[]{:S(2)}, u32[]{:S(2)}) collective-permute-start(f32[240,128]{1,0:T(8,128)S(1)} %get-tuple-element.45.refs_3_.refs_4_), channel_id=1, source_target_pairs={{0,6},{1,7},{2,4},{3,5},{4,2},{5,3},{6,0},{7,1},{8,14},{9,15},{10,... | collective-permute-start | bytes 368648 | tf_op jit(solution)/shard_map/ppermute | solution.py:632
  14.0 4.2 %collective-permute-done.4.refs_4_.refs_5_ = f32[240,128]{1,0:T(8,128)S(1)} collective-permute-done((f32[240,128]{1,0:T(8,128)S(1)}, f32[240,128]{1,0:T(8,128)S(1)}, u32[]{:S(2)}, u32[]{:S(2)}) %collective-permute-start.4) | collective-permute-done | bytes 122912 | tf_op jit(solution)/shard_map/ppermute | solution.py:632
  18.2 2.4 %collective-permute-done.3.refs_1_ = f32[240,128]{1,0:T(8,128)S(1)} collective-permute-done((f32[240,128]{1,0:T(8,128)S(1)}, f32[240,128]{1,0:T(8,128)S(1)}, u32[]{:S(2)}, u32[]{:S(2)}) %collective-permute-start.3) | collective-permute-done | bytes 122912 | tf_op jit(solution)/shard_map/ppermute | solution.py:632
  20.6 1.7 %collective-permute-start.5 = (f32[240,128]{1,0:T(8,128)S(1)}, f32[240,128]{1,0:T(8,128)S(1)}, u32[]{:S(2)}, u32[]{:S(2)}) collective-permute-start(f32[240,128]{1,0:T(8,128)S(1)} %get-tuple-element.47), channel_id=1, source_target_pairs={{0,6},{1,7},{2,4},{3,5},{4,2},{5,3},{6,0},{7,1},{8,14},{9,15},{10,... | collective-permute-start | bytes 368648 | tf_op jit(solution)/shard_map/ppermute | solution.py:632
  22.5 2.5 %collective-permute-start.9 = (f32[8,2560]{1,0:T(8,128)S(1)}, f32[8,2560]{1,0:T(8,128)S(1)}, u32[]{:S(2)}, u32[]{:S(2)}) collective-permute-start(f32[8,2560]{1,0:T(8,128)S(1)} %edge_both.1), channel_id=1, source_target_pairs={{0,24},{8,16},{16,8},{24,0},{1,25},{9,17},{17,9},{25,1},{2,26},{10... | collective-permute-start | bytes 245768 | tf_op jit(solution)/shard_map/ppermute | solution.py:618
  26.1 2.7 %collective-permute-done.5.refs_2_.refs_3_ = f32[240,128]{1,0:T(8,128)S(1)} collective-permute-done((f32[240,128]{1,0:T(8,128)S(1)}, f32[240,128]{1,0:T(8,128)S(1)}, u32[]{:S(2)}, u32[]{:S(2)}) %collective-permute-start.5) | collective-permute-done | bytes 122912 | tf_op jit(solution)/shard_map/ppermute | solution.py:632
  30.0 1.6 %section_join.1 = (f32[2,5,16,16,128]{4,3,2,1,0:T(8,128)S(1)}, f32[8,2560]{1,0:T(8,128)S(1)}) custom-call(f32[2,5,8,16,128]{4,3,2,1,0:T(8,128)S(1)} %get-tuple-element.34.refs_0_, f32[2,5,8,16,128]{4,3,2,1,0:T(8,128)S(1)} %collective-permute-done.refs_9_.refs_1_, f32[1616,128]{1,0:T(8,128)S(1)} %get-tuple-element.42.kept.refs_2_, ...), custom_call_target="tpu_custom_call" | custom-call | flops 1 | bytes 1 | tf_op jit(solution)/shard_map/section_join/pallas_call | solution.py:654
  31.6 1.8 %collective-permute-start.12 = (f32[8,2560]{1,0:T(8,128)S(1)}, f32[8,2560]{1,0:T(8,128)S(1)}, u32[]{:S(2)}, u32[]{:S(2)}) collective-permute-start(f32[8,2560]{1,0:T(8,128)S(1)} %get-tuple-element.50.refs_5_), channel_id=1, source_target_pairs={{0,24},{8,16},{16,8},{24,0},{1,25},{9,17},{17,9},{25,1},{2,26},{10... | collective-permute-start | bytes 245768 | tf_op jit(solution)/shard_map/ppermute | solution.py:618
  33.9 1.2 %collective-permute-start.10 = (f32[8,2560]{1,0:T(8,128)S(1)}, f32[8,2560]{1,0:T(8,128)S(1)}, u32[]{:S(2)}, u32[]{:S(2)}) collective-permute-start(f32[8,2560]{1,0:T(8,128)S(1)} %get-tuple-element.50.refs_5_), channel_id=1, source_target_pairs={{0,8},{8,0},{16,24},{24,16},{1,9},{9,1},{17,25},{25,17},{2,10},{10... | collective-permute-start | bytes 245768 | tf_op jit(solution)/shard_map/ppermute | solution.py:618
  35.9 2.6 %entries.1 = (f32[4,8,128]{2,1,0:T(8,128)S(1)}, bf16[512,4096]{1,0:T(8,128)(2,1)S(1)}, bf16[128,4096]{1,0:T(8,128)(2,1)S(1)}) custom-call(f32[2,128]{1,0:T(2,128)S(1)} %bitcast.2, s32[4,8,128]{2,1,0:T(8,128)S(1)} %copy-done.12, f32[8,128]{1,0:T(8,128)S(1)} %copy-done.15, s32[4,8,128]{2,1,0:T(8,128)S(1)} %copy-done.13, s32[4,8,128]{2,1,0:T(8,128)S(1)} %copy-done.14, ...), custom_call_target="tpu_custom_call" | custom-call | flops 1 | bytes 1 | tf_op jit(solution)/shard_map/entries/pallas_call | solution.py:654
  39.3 2.0 %collective-permute-start.13 = (f32[336,128]{1,0:T(8,128)S(1)}, f32[336,128]{1,0:T(8,128)S(1)}, u32[]{:S(2)}, u32[]{:S(2)}) collective-permute-start(f32[336,128]{1,0:T(8,128)S(1)} %get-tuple-element.53.refs_0_), channel_id=1, source_target_pairs={{0,2},{1,3},{2,0},{3,1},{4,6},{5,7},{6,4},{7,5},{8,10},{9,11},{10,... | collective-permute-start | bytes 516104 | tf_op jit(solution)/shard_map/ppermute | solution.py:632
  41.2 2.2 %collective-permute-start.15 = (f32[336,128]{1,0:T(8,128)S(1)}, f32[336,128]{1,0:T(8,128)S(1)}, u32[]{:S(2)}, u32[]{:S(2)}) collective-permute-start(f32[336,128]{1,0:T(8,128)S(1)} %get-tuple-element.54.refs_3_.refs_4_), channel_id=1, source_target_pairs={{0,6},{1,7},{2,4},{3,5},{4,2},{5,3},{6,0},{7,1},{8,14},{9,15},{10,... | collective-permute-start | bytes 516104 | tf_op jit(solution)/shard_map/ppermute | solution.py:632
  43.4 6.3 %collective-permute-done.14.rest_1_.refs_6_ = f32[16,128]{1,0:T(8,128)S(1)} collective-permute-done((f32[16,128]{1,0:T(8,128)S(1)}, f32[16,128]{1,0:T(8,128)S(1)}, u32[]{:S(2)}, u32[]{:S(2)}) %collective-permute-start.14) | collective-permute-done | bytes 8224 | tf_op jit(solution)/shard_map/ppermute | solution.py:922
  50.4 1.9 %collective-permute-start.17 = (f32[320,128]{1,0:T(8,128)S(1)}, f32[320,128]{1,0:T(8,128)S(1)}, u32[]{:S(2)}, u32[]{:S(2)}) collective-permute-start(f32[320,128]{1,0:T(8,128)S(1)} %get-tuple-element.61.refs_5_.refs_1_), channel_id=1, source_target_pairs={{0,6},{1,7},{2,4},{3,5},{4,2},{5,3},{6,0},{7,1},{8,14},{9,15},{10,... | collective-permute-start | bytes 491528 | tf_op jit(solution)/shard_map/ppermute | solution.py:632
  52.4 1.3 %collective-permute-start.16 = (f32[8,128]{1,0:T(8,128)S(1)}, f32[8,128]{1,0:T(8,128)S(1)}, u32[]{:S(2)}, u32[]{:S(2)}) collective-permute-start(f32[8,128]{1,0:T(8,128)S(1)} %get-tuple-element.56), channel_id=1, source_target_pairs={{0,1},{2,3},{4,5},{6,7},{8,9},{10,11},{12,13},{14,15},{16,17},{18,... | collective-permute-start | bytes 12296 | tf_op jit(solution)/shard_map/ppermute | solution.py:930
  54.5 2.2 %signals.1.refs_8_ = f32[512,128]{1,0:T(8,128)} custom-call(f32[8,128]{1,0:T(8,128)S(1)} %get-tuple-element.55.refs_0_, f32[8,128]{1,0:T(8,128)S(1)} %collective-permute-done.16.refs_1_, f32[4,8,128]{2,1,0:T(8,128)S(1)} %get-tuple-element.51.refs_5_.refs_2_, bf16[512,4096]{1,0:T(8,128)(2,1)S(1)} %get-tuple-element.57.refs_3_, ...), custom_call_target="tpu_custom_call" | custom-call | flops 1 | bytes 1 | tf_op jit(solution)/shard_map/signals/pallas_call | solution.py:654
  56.7 1.0 %collective-permute-done.17.refs_2_.refs_3_ = f32[320,128]{1,0:T(8,128)S(1)} collective-permute-done((f32[320,128]{1,0:T(8,128)S(1)}, f32[320,128]{1,0:T(8,128)S(1)}, u32[]{:S(2)}, u32[]{:S(2)}) %collective-permute-start.17) | collective-permute-done | bytes 163872 | tf_op jit(solution)/shard_map/ppermute | solution.py:632
  57.9 3.7 %all-to-all-start = ((f32[32,16,128]{2,1,0:T(8,128)}), f32[32,16,128]{2,1,0:T(8,128)S(1)}, u32[]{:S(2)}, u32[]{:S(2)}) async-start(f32[32,16,128]{2,1,0:T(8,128)} %bitcast.1), calls=%async_computation | async-start | bytes 524288 | tf_op jit(solution)/shard_map/all_to_all | solution.py:949
  61.6 1.2 %azim_join_kept.1.partial = f32[5,64,8,128]{3,2,1,0:T(8,128)} custom-call(f32[2,5,16,16,128]{4,3,2,1,0:T(8,128)S(1)} %azim_local.1.refs_0_.local, f32[2,6,5,16,128]{4,3,2,1,0:T(8,128)S(1)} %ring_sums.3.refs_1_.ring), custom_call_target="tpu_custom_call" | custom-call | flops 1 | bytes 1 | tf_op jit(solution)/shard_map/azim_join_kept/pallas_call | solution.py:774
  62.8 0.9 %place_rows.1 = f32[5,64,8,128]{3,2,1,0:T(8,128)} custom-call(f32[2,5,8,16,128]{4,3,2,1,0:T(8,128)S(1)} %collective-permute-done.19.values, f32[5,64,8,128]{3,2,1,0:T(8,128)} %azim_join_kept.1.partial), custom_call_target="tpu_custom_call", output_to_operand_aliasing={{}: (1, {})} | custom-call | flops 1 | bytes 1 | tf_op jit(solution)/shard_map/place_rows/pallas_call | solution.py:774
  63.7 8.3 %all-to-all-done = f32[32,16,128]{2,1,0:T(8,128)S(1)} async-done(((f32[32,16,128]{2,1,0:T(8,128)}), f32[32,16,128]{2,1,0:T(8,128)S(1)}, u32[]{:S(2)}, u32[]{:S(2)}) %all-to-all-start) | async-done | bytes 262176 | tf_op jit(solution)/shard_map/all_to_all | solution.py:949
  (77 shorter events, 9.0 us)
Async XLA Ops:
  3.3 2.8 %collective-permute-start = (f32[2,5,8,16,128]{4,3,2,1,0:T(8,128)}, f32[2,5,8,16,128]{4,3,2,1,0:T(8,128)S(1)}, u32[]{:S(2)}, u32[]{:S(2)}) collective-permute-start(f32[2,5,8,16,128]{4,3,2,1,0:T(8,128)} %get-tuple-element.35), channel_id=1, source_target_pairs={{0,1},{1,0},{2,3},{3,2},{4,5},{5,4},{6,7},{7,6},{8,9},{9,8},{10,11... | collective-permute-start | bytes 1966088 | tf_op jit(solution)/shard_map/ppermute | solution.py:622
  3.8 2.3 %collective-permute-start.1 = (f32[2,3,5,16,128]{4,3,2,1,0:T(8,128)}, f32[2,3,5,16,128]{4,3,2,1,0:T(8,128)S(1)}, u32[]{:S(2)}, u32[]{:S(2)}) collective-permute-start(f32[2,3,5,16,128]{4,3,2,1,0:T(8,128)} %get-tuple-element.37), channel_id=1, source_target_pairs={{0,1},{1,0},{2,3},{3,2},{4,5},{5,4},{6,7},{7,6},{8,9},{9,8},{10,11... | collective-permute-start | bytes 737288 | tf_op jit(solution)/shard_map/ppermute | solution.py:622
  8.8 13.6 %collective-permute-start.2 = (f32[1616,128]{1,0:T(8,128)S(1)}, f32[1616,128]{1,0:T(8,128)S(1)}, u32[]{:S(2)}, u32[]{:S(2)}) collective-permute-start(f32[1616,128]{1,0:T(8,128)S(1)} %get-tuple-element.43), channel_id=1, source_target_pairs={{0,1},{1,0},{2,3},{3,2},{4,5},{5,4},{6,7},{7,6},{8,9},{9,8},{10,11... | collective-permute-start | bytes 2482184 | tf_op jit(solution)/shard_map/ppermute | solution.py:622
  9.3 9.0 %collective-permute-start.4 = (f32[240,128]{1,0:T(8,128)S(1)}, f32[240,128]{1,0:T(8,128)S(1)}, u32[]{:S(2)}, u32[]{:S(2)}) collective-permute-start(f32[240,128]{1,0:T(8,128)S(1)} %get-tuple-element.45.refs_3_.refs_4_), channel_id=1, source_target_pairs={{0,6},{1,7},{2,4},{3,5},{4,2},{5,3},{6,0},{7,1},{8,14},{9,15},{10,... | collective-permute-start | bytes 368648 | tf_op jit(solution)/shard_map/ppermute | solution.py:632
  14.0 6.6 %collective-permute-start.3 = (f32[240,128]{1,0:T(8,128)S(1)}, f32[240,128]{1,0:T(8,128)S(1)}, u32[]{:S(2)}, u32[]{:S(2)}) collective-permute-start(f32[240,128]{1,0:T(8,128)S(1)} %get-tuple-element.38.refs_8_.refs_0_), channel_id=1, source_target_pairs={{0,2},{1,3},{2,0},{3,1},{4,6},{5,7},{6,4},{7,5},{8,10},{9,11},{10,... | collective-permute-start | bytes 368648 | tf_op jit(solution)/shard_map/ppermute | solution.py:632
  20.6 8.1 %collective-permute-start.5 = (f32[240,128]{1,0:T(8,128)S(1)}, f32[240,128]{1,0:T(8,128)S(1)}, u32[]{:S(2)}, u32[]{:S(2)}) collective-permute-start(f32[240,128]{1,0:T(8,128)S(1)} %get-tuple-element.47), channel_id=1, source_target_pairs={{0,6},{1,7},{2,4},{3,5},{4,2},{5,3},{6,0},{7,1},{8,14},{9,15},{10,... | collective-permute-start | bytes 368648 | tf_op jit(solution)/shard_map/ppermute | solution.py:632
  22.3 6.8 %collective-permute-start.6 = (f32[240,128]{1,0:T(8,128)S(1)}, f32[240,128]{1,0:T(8,128)S(1)}, u32[]{:S(2)}, u32[]{:S(2)}) collective-permute-start(f32[240,128]{1,0:T(8,128)S(1)} %get-tuple-element.48), channel_id=1, source_target_pairs={{0,2},{1,3},{2,0},{3,1},{4,6},{5,7},{6,4},{7,5},{8,10},{9,11},{10,... | collective-permute-start | bytes 368648 | tf_op jit(solution)/shard_map/ppermute | solution.py:632
  22.5 7.5 %copy-start.9 = (bf16[4,2,24,128]{3,2,1,0:T(8,128)(2,1)S(1)}, bf16[4,2,24,128]{3,2,1,0:T(8,128)(2,1)}, u32[]{:S(2)}) copy-start(bf16[4,2,24,128]{3,2,1,0:T(8,128)(2,1)} %constant.19.clone.refs_6_) | copy-start | bytes 147460
  22.5 7.5 %copy-start.16 = (bf16[2,8,128]{2,1,0:T(8,128)(2,1)S(1)}, bf16[2,8,128]{2,1,0:T(8,128)(2,1)}, u32[]{:S(2)}) copy-start(bf16[2,8,128]{2,1,0:T(8,128)(2,1)} %constant.18.clone.refs_5_) | copy-start | bytes 12292
  22.5 6.7 %collective-permute-start.9 = (f32[8,2560]{1,0:T(8,128)S(1)}, f32[8,2560]{1,0:T(8,128)S(1)}, u32[]{:S(2)}, u32[]{:S(2)}) collective-permute-start(f32[8,2560]{1,0:T(8,128)S(1)} %edge_both.1), channel_id=1, source_target_pairs={{0,24},{8,16},{16,8},{24,0},{1,25},{9,17},{17,9},{25,1},{2,26},{10... | collective-permute-start | bytes 245768 | tf_op jit(solution)/shard_map/ppermute | solution.py:618
  25.0 4.4 %collective-permute-start.8 = (f32[8,2560]{1,0:T(8,128)S(1)}, f32[8,2560]{1,0:T(8,128)S(1)}, u32[]{:S(2)}, u32[]{:S(2)}) collective-permute-start(f32[8,2560]{1,0:T(8,128)S(1)} %edge_both.1), channel_id=1, source_target_pairs={{0,16},{8,24},{16,0},{24,8},{1,17},{9,25},{17,1},{25,9},{2,18},{10... | collective-permute-start | bytes 245768 | tf_op jit(solution)/shard_map/ppermute | solution.py:618
  25.5 4.4 %collective-permute-start.7 = (f32[8,2560]{1,0:T(8,128)S(1)}, f32[8,2560]{1,0:T(8,128)S(1)}, u32[]{:S(2)}, u32[]{:S(2)}) collective-permute-start(f32[8,2560]{1,0:T(8,128)S(1)} %edge_both.1), channel_id=1, source_target_pairs={{0,8},{8,0},{16,24},{24,16},{1,9},{9,1},{17,25},{25,17},{2,10},{10... | collective-permute-start | bytes 245768 | tf_op jit(solution)/shard_map/ppermute | solution.py:618
  31.6 6.9 %collective-permute-start.12 = (f32[8,2560]{1,0:T(8,128)S(1)}, f32[8,2560]{1,0:T(8,128)S(1)}, u32[]{:S(2)}, u32[]{:S(2)}) collective-permute-start(f32[8,2560]{1,0:T(8,128)S(1)} %get-tuple-element.50.refs_5_), channel_id=1, source_target_pairs={{0,24},{8,16},{16,8},{24,0},{1,25},{9,17},{17,9},{25,1},{2,26},{10... | collective-permute-start | bytes 245768 | tf_op jit(solution)/shard_map/ppermute | solution.py:618
  33.4 5.1 %collective-permute-start.11 = (f32[8,2560]{1,0:T(8,128)S(1)}, f32[8,2560]{1,0:T(8,128)S(1)}, u32[]{:S(2)}, u32[]{:S(2)}) collective-permute-start(f32[8,2560]{1,0:T(8,128)S(1)} %get-tuple-element.50.refs_5_), channel_id=1, source_target_pairs={{0,16},{8,24},{16,0},{24,8},{1,17},{9,25},{17,1},{25,9},{2,18},{10... | collective-permute-start | bytes 245768 | tf_op jit(solution)/shard_map/ppermute | solution.py:618
  33.9 4.6 %collective-permute-start.10 = (f32[8,2560]{1,0:T(8,128)S(1)}, f32[8,2560]{1,0:T(8,128)S(1)}, u32[]{:S(2)}, u32[]{:S(2)}) collective-permute-start(f32[8,2560]{1,0:T(8,128)S(1)} %get-tuple-element.50.refs_5_), channel_id=1, source_target_pairs={{0,8},{8,0},{16,24},{24,16},{1,9},{9,1},{17,25},{25,17},{2,10},{10... | collective-permute-start | bytes 245768 | tf_op jit(solution)/shard_map/ppermute | solution.py:618
  35.9 16.4 %copy-start.11 = (f32[4,16,64]{2,1,0:T(8,128)S(1)}, f32[4,16,64]{2,1,0:T(8,128)}, u32[]{:S(2)}) copy-start(f32[4,16,64]{2,1,0:T(8,128)} %constant.22.clone.around) | copy-start | bytes 49156
  39.3 10.5 %collective-permute-start.13 = (f32[336,128]{1,0:T(8,128)S(1)}, f32[336,128]{1,0:T(8,128)S(1)}, u32[]{:S(2)}, u32[]{:S(2)}) collective-permute-start(f32[336,128]{1,0:T(8,128)S(1)} %get-tuple-element.53.refs_0_), channel_id=1, source_target_pairs={{0,2},{1,3},{2,0},{3,1},{4,6},{5,7},{6,4},{7,5},{8,10},{9,11},{10,... | collective-permute-start | bytes 516104 | tf_op jit(solution)/shard_map/ppermute | solution.py:632
  41.2 8.5 %collective-permute-start.15 = (f32[336,128]{1,0:T(8,128)S(1)}, f32[336,128]{1,0:T(8,128)S(1)}, u32[]{:S(2)}, u32[]{:S(2)}) collective-permute-start(f32[336,128]{1,0:T(8,128)S(1)} %get-tuple-element.54.refs_3_.refs_4_), channel_id=1, source_target_pairs={{0,6},{1,7},{2,4},{3,5},{4,2},{5,3},{6,0},{7,1},{8,14},{9,15},{10,... | collective-permute-start | bytes 516104 | tf_op jit(solution)/shard_map/ppermute | solution.py:632
  43.4 6.3 %collective-permute-start.14 = (f32[16,128]{1,0:T(8,128)S(1)}, f32[16,128]{1,0:T(8,128)S(1)}, u32[]{:S(2)}, u32[]{:S(2)}) collective-permute-start(f32[16,128]{1,0:T(8,128)S(1)} %get-tuple-element.52.front), channel_id=1, source_target_pairs={{0,4},{1,5},{2,6},{3,7},{4,0},{5,1},{6,2},{7,3},{8,12},{9,13},{10,... | collective-permute-start | bytes 24584 | tf_op jit(solution)/shard_map/ppermute | solution.py:922
  49.8 6.8 %collective-permute-start.18 = (f32[320,128]{1,0:T(8,128)S(1)}, f32[320,128]{1,0:T(8,128)S(1)}, u32[]{:S(2)}, u32[]{:S(2)}) collective-permute-start(f32[320,128]{1,0:T(8,128)S(1)} %get-tuple-element.63), channel_id=1, source_target_pairs={{0,2},{1,3},{2,0},{3,1},{4,6},{5,7},{6,4},{7,5},{8,10},{9,11},{10,... | collective-permute-start | bytes 491528 | tf_op jit(solution)/shard_map/ppermute | solution.py:632
  50.4 7.2 %collective-permute-start.17 = (f32[320,128]{1,0:T(8,128)S(1)}, f32[320,128]{1,0:T(8,128)S(1)}, u32[]{:S(2)}, u32[]{:S(2)}) collective-permute-start(f32[320,128]{1,0:T(8,128)S(1)} %get-tuple-element.61.refs_5_.refs_1_), channel_id=1, source_target_pairs={{0,6},{1,7},{2,4},{3,5},{4,2},{5,3},{6,0},{7,1},{8,14},{9,15},{10,... | collective-permute-start | bytes 491528 | tf_op jit(solution)/shard_map/ppermute | solution.py:632
  52.4 2.1 %collective-permute-start.16 = (f32[8,128]{1,0:T(8,128)S(1)}, f32[8,128]{1,0:T(8,128)S(1)}, u32[]{:S(2)}, u32[]{:S(2)}) collective-permute-start(f32[8,128]{1,0:T(8,128)S(1)} %get-tuple-element.56), channel_id=1, source_target_pairs={{0,1},{2,3},{4,5},{6,7},{8,9},{10,11},{12,13},{14,15},{16,17},{18,... | collective-permute-start | bytes 12296 | tf_op jit(solution)/shard_map/ppermute | solution.py:930
  57.8 5.0 %collective-permute-start.19 = (f32[2,5,8,16,128]{4,3,2,1,0:T(8,128)S(1)}, f32[2,5,8,16,128]{4,3,2,1,0:T(8,128)S(1)}, u32[]{:S(2)}, u32[]{:S(2)}) collective-permute-start(f32[2,5,8,16,128]{4,3,2,1,0:T(8,128)S(1)} %azim_join_sent.1), channel_id=1, source_target_pairs={{0,1},{1,0},{2,3},{3,2},{4,5},{5,4},{6,7},{7,6},{8,9},{9,8},{10,11... | collective-permute-start | bytes 1966088 | tf_op jit(solution)/shard_map/ppermute | solution.py:622
  57.9 14.1 %all-to-all-start = ((f32[32,16,128]{2,1,0:T(8,128)}), f32[32,16,128]{2,1,0:T(8,128)S(1)}, u32[]{:S(2)}, u32[]{:S(2)}) async-start(f32[32,16,128]{2,1,0:T(8,128)} %bitcast.1), calls=%async_computation | async-start | bytes 524288 | tf_op jit(solution)/shard_map/all_to_all | solution.py:949
  (16 other events, 38.2 us)

commit v6 on v5

--- a/solution.py
+++ b/solution.py
@@ -828,27 +828,39 @@
     )
 
     arrived = [partner(packs[turn], around, turn, 0) for turn in range(2)]
-    base, scale, edge_d = call(
-        section_local_kernel,
+    def by_quarter(*refs):
+        inputs, (own, basis, base_out, scale_out, edge_out, *scratch) = refs[:6], refs[6:]
+        for step in range(4):
+            here = slice(step * part, (step + 1) * part)
+            pieces = [ref.at[here] if len(ref.shape) == 3 else ref.at[:, here] for ref in inputs]
+            section_local_kernel(
+                *pieces,
+                own.at[lax.axis_index("axial")],
+                basis,
+                base_out.at[step : step + 1],
+                scale_out.at[step : step + 1],
+                edge_out.at[:, step * lines : (step + 1) * lines],
+                *scratch,
+            )
+
+    base, scale, edge_d = whole_call(
+        by_quarter,
         "section_local",
-        4,
-        [
-            field(every),
-            vector(every),
-            field(every),
-            vector(every),
-            field(every),
-            vector(every, FIELDS),
-            table(own_d),
-            fixed(basis_d.shape),
-        ],
-        [inner(every), inner_one(every), edge(every)],
         [
             shaped(4, FIELDS, rows, part, lanes),
             shaped(4, rows, part, lanes),
             shaped(BASIS, 4 * lines),
         ],
-        (density, velocity, pressure, axial_metric, volume, radial_term, own_d, basis_d),
+        (
+            density,
+            velocity,
+            pressure,
+            axial_metric,
+            volume,
+            radial_term,
+            jnp.asarray(own_d),
+            jnp.asarray(basis_d),
+        ),
         wait=(packs[0], flux_in),
         scratch=[flux_scratch] * 2,
     )

time: 73 us -> 72.3 us (level)
    pallas_call x3 -> x2, Pallas kernels: 4.56 us -> 2.07 us  [call(): pl.pallas_call(waiting(kernel, len(args), wait), grid=(steps,), in_specs=...]
    pallas_call x15 -> x16, Pallas kernels: 9.14 us -> 11 us  [whole_call(): pl.pallas_call(waiting(kernel, len(args), wait), in_specs=[whole] * len(a...]
  transfers between devices with their start and end apart: 21 -> 21, of which waited for: 11 -> 11; matrix products, arithmetic and copies ran while one was open for 0% -> 0% of each run, Pallas kernels for 13% -> 14%
where the time goes in v6:
time: 72.3 us; the launch traced here: 71.9 us
  waiting for transfers between devices  26.9 us (37%)
  starting transfers between devices  26.4 us (37%)
  Pallas kernels  16.9 us (23%)
  between operations  0.97 us (1%)
    ppermute x8, starting transfers between devices, partner(): return lax.ppermute(values, 'azim', pairs)  13.2 us
    pallas_call x16, Pallas kernels, whole_call(): pl.pallas_call(waiting(kernel, len(args), wait), in_specs=[whole] * len(a...  11 us
    ppermute x8, waiting for transfers between devices, partner(): return lax.ppermute(values, 'azim', pairs)  10.7 us
    all_to_all x1, waiting for transfers between devices, per_device(): lax.all_to_all(partial.reshape(devices, OBSERVERS // devices, TIME_BINS),...  8.31 us
    ppermute x6, starting transfers between devices, swap(): return lax.ppermute(values, axis, [(i, i ^ mask) for i in range(count)])  7.08 us
    ppermute x1, waiting for transfers between devices, per_device(): fronts[at] = lax.ppermute(front, 'azim', pairs)  6.33 us
    pallas_call x2, Pallas kernels, apart(): pl.pallas_call(waiting(kernel, len(args), wait), in_specs=[spec(memory_sp...  3.91 us
    all_to_all x1, starting transfers between devices, per_device(): lax.all_to_all(partial.reshape(devices, OBSERVERS // devices, TIME_BINS),...  3.7 us
  transfers between devices with their start and end apart: 21, of which 11 were waited for; matrix products, arithmetic and copies ran while one was open for 0% of the time, Pallas kernels for 14%

profile of v6, /device:TPU:0, one launch (start us, length us, event | category | flops | bytes accessed | tf_op | source)
XLA Modules:
  0.0 71.9 jit_solution(15164361140248721991)
XLA Ops:
  0.7 2.6 %azim_flux_sent.1 = (f32[2,5,8,16,128]{4,3,2,1,0:T(8,128)}, f32[2,3,5,16,128]{4,3,2,1,0:T(8,128)}) custom-call(f32[64,8,128]{2,1,0:T(8,128)} %refs_0_.1, f32[3,64,8,128]{3,2,1,0:T(8,128)} %refs_1_.4, f32[64,8,128]{2,1,0:T(8,128)} %refs_2_.2, f32[3,64,8,128]{3,2,1,0:T(8,128)} %azim_metric.3, f32[64,8,128]{2,1,0:T(8,128)} %refs_4_.2), custom_call_target="tpu_custom_call" | custom-call | flops 1 | bytes 1 | tf_op jit(solution)/shard_map/azim_flux_sent/pallas_call | solution.py:795
  4.0 1.3 %azim_flux_kept.1 = (f32[2,5,8,16,128]{4,3,2,1,0:T(8,128)S(1)}, f32[2,3,5,16,128]{4,3,2,1,0:T(8,128)S(1)}) custom-call(f32[64,8,128]{2,1,0:T(8,128)S(1)} %copy-done.2, f32[3,64,8,128]{3,2,1,0:T(8,128)S(1)} %copy-done, f32[64,8,128]{2,1,0:T(8,128)S(1)} %copy-done.3, f32[3,64,8,128]{3,2,1,0:T(8,128)S(1)} %copy-done.1, f32[64,8,128]{2,1,0:T(8,128)S(1)} %copy-done.4), custom_call_target="tpu_custom_call" | custom-call | flops 1 | bytes 1 | tf_op jit(solution)/shard_map/azim_flux_kept/pallas_call | solution.py:795
  6.2 1.8 %section_local.1 = (f32[4,5,8,16,128]{4,3,2,1,0:T(8,128)S(1)}, f32[4,8,16,128]{3,2,1,0:T(8,128)S(1)}, f32[8,2560]{1,0:T(8,128)S(1)}) custom-call(f32[64,8,128]{2,1,0:T(8,128)S(1)} %copy-done.2, f32[3,64,8,128]{3,2,1,0:T(8,128)S(1)} %copy-done, f32[64,8,128]{2,1,0:T(8,128)S(1)} %copy-done.3, f32[3,64,8,128]{3,2,1,0:T(8,128)S(1)} %copy-done.6, ...), custom_call_target="tpu_custom_call" | custom-call | flops 1 | bytes 1 | tf_op jit(solution)/shard_map/section_local/pallas_call | solution.py:654
  8.6 4.7 %collective-permute-start.4 = (f32[240,128]{1,0:T(8,128)S(1)}, f32[240,128]{1,0:T(8,128)S(1)}, u32[]{:S(2)}, u32[]{:S(2)}) collective-permute-start(f32[240,128]{1,0:T(8,128)S(1)} %get-tuple-element.45.refs_3_.refs_4_), channel_id=1, source_target_pairs={{0,6},{1,7},{2,4},{3,5},{4,2},{5,3},{6,0},{7,1},{8,14},{9,15},{10,... | collective-permute-start | bytes 368648 | tf_op jit(solution)/shard_map/ppermute | solution.py:632
  13.3 4.2 %collective-permute-done.4.refs_4_.refs_5_ = f32[240,128]{1,0:T(8,128)S(1)} collective-permute-done((f32[240,128]{1,0:T(8,128)S(1)}, f32[240,128]{1,0:T(8,128)S(1)}, u32[]{:S(2)}, u32[]{:S(2)}) %collective-permute-start.4) | collective-permute-done | bytes 122912 | tf_op jit(solution)/shard_map/ppermute | solution.py:632
  17.5 2.4 %collective-permute-done.3.refs_1_ = f32[240,128]{1,0:T(8,128)S(1)} collective-permute-done((f32[240,128]{1,0:T(8,128)S(1)}, f32[240,128]{1,0:T(8,128)S(1)}, u32[]{:S(2)}, u32[]{:S(2)}) %collective-permute-start.3) | collective-permute-done | bytes 122912 | tf_op jit(solution)/shard_map/ppermute | solution.py:632
  19.9 1.7 %collective-permute-start.5 = (f32[240,128]{1,0:T(8,128)S(1)}, f32[240,128]{1,0:T(8,128)S(1)}, u32[]{:S(2)}, u32[]{:S(2)}) collective-permute-start(f32[240,128]{1,0:T(8,128)S(1)} %get-tuple-element.47), channel_id=1, source_target_pairs={{0,6},{1,7},{2,4},{3,5},{4,2},{5,3},{6,0},{7,1},{8,14},{9,15},{10,... | collective-permute-start | bytes 368648 | tf_op jit(solution)/shard_map/ppermute | solution.py:632
  21.8 2.5 %collective-permute-start.9 = (f32[8,2560]{1,0:T(8,128)S(1)}, f32[8,2560]{1,0:T(8,128)S(1)}, u32[]{:S(2)}, u32[]{:S(2)}) collective-permute-start(f32[8,2560]{1,0:T(8,128)S(1)} %edge_both.1), channel_id=1, source_target_pairs={{0,24},{8,16},{16,8},{24,0},{1,25},{9,17},{17,9},{25,1},{2,26},{10... | collective-permute-start | bytes 245768 | tf_op jit(solution)/shard_map/ppermute | solution.py:618
  25.4 2.7 %collective-permute-done.5.refs_2_.refs_3_ = f32[240,128]{1,0:T(8,128)S(1)} collective-permute-done((f32[240,128]{1,0:T(8,128)S(1)}, f32[240,128]{1,0:T(8,128)S(1)}, u32[]{:S(2)}, u32[]{:S(2)}) %collective-permute-start.5) | collective-permute-done | bytes 122912 | tf_op jit(solution)/shard_map/ppermute | solution.py:632
  29.3 1.6 %section_join.1 = (f32[2,5,16,16,128]{4,3,2,1,0:T(8,128)S(1)}, f32[8,2560]{1,0:T(8,128)S(1)}) custom-call(f32[2,5,8,16,128]{4,3,2,1,0:T(8,128)S(1)} %get-tuple-element.34.refs_0_, f32[2,5,8,16,128]{4,3,2,1,0:T(8,128)S(1)} %collective-permute-done.refs_9_.refs_1_, f32[1616,128]{1,0:T(8,128)S(1)} %get-tuple-element.42.kept.refs_2_, ...), custom_call_target="tpu_custom_call" | custom-call | flops 1 | bytes 1 | tf_op jit(solution)/shard_map/section_join/pallas_call | solution.py:654
  30.9 1.8 %collective-permute-start.12 = (f32[8,2560]{1,0:T(8,128)S(1)}, f32[8,2560]{1,0:T(8,128)S(1)}, u32[]{:S(2)}, u32[]{:S(2)}) collective-permute-start(f32[8,2560]{1,0:T(8,128)S(1)} %get-tuple-element.50.refs_5_), channel_id=1, source_target_pairs={{0,24},{8,16},{16,8},{24,0},{1,25},{9,17},{17,9},{25,1},{2,26},{10... | collective-permute-start | bytes 245768 | tf_op jit(solution)/shard_map/ppermute | solution.py:618
  33.2 1.2 %collective-permute-start.10 = (f32[8,2560]{1,0:T(8,128)S(1)}, f32[8,2560]{1,0:T(8,128)S(1)}, u32[]{:S(2)}, u32[]{:S(2)}) collective-permute-start(f32[8,2560]{1,0:T(8,128)S(1)} %get-tuple-element.50.refs_5_), channel_id=1, source_target_pairs={{0,8},{8,0},{16,24},{24,16},{1,9},{9,1},{17,25},{25,17},{2,10},{10... | collective-permute-start | bytes 245768 | tf_op jit(solution)/shard_map/ppermute | solution.py:618
  35.2 2.6 %entries.1 = (f32[4,8,128]{2,1,0:T(8,128)S(1)}, bf16[512,4096]{1,0:T(8,128)(2,1)S(1)}, bf16[128,4096]{1,0:T(8,128)(2,1)S(1)}) custom-call(f32[2,128]{1,0:T(2,128)S(1)} %bitcast.2, s32[4,8,128]{2,1,0:T(8,128)S(1)} %copy-done.12, f32[8,128]{1,0:T(8,128)S(1)} %copy-done.15, s32[4,8,128]{2,1,0:T(8,128)S(1)} %copy-done.13, s32[4,8,128]{2,1,0:T(8,128)S(1)} %copy-done.14, ...), custom_call_target="tpu_custom_call" | custom-call | flops 1 | bytes 1 | tf_op jit(solution)/shard_map/entries/pallas_call | solution.py:654
  38.6 2.0 %collective-permute-start.13 = (f32[336,128]{1,0:T(8,128)S(1)}, f32[336,128]{1,0:T(8,128)S(1)}, u32[]{:S(2)}, u32[]{:S(2)}) collective-permute-start(f32[336,128]{1,0:T(8,128)S(1)} %get-tuple-element.53.refs_0_), channel_id=1, source_target_pairs={{0,2},{1,3},{2,0},{3,1},{4,6},{5,7},{6,4},{7,5},{8,10},{9,11},{10,... | collective-permute-start | bytes 516104 | tf_op jit(solution)/shard_map/ppermute | solution.py:632
  40.5 2.2 %collective-permute-start.15 = (f32[336,128]{1,0:T(8,128)S(1)}, f32[336,128]{1,0:T(8,128)S(1)}, u32[]{:S(2)}, u32[]{:S(2)}) collective-permute-start(f32[336,128]{1,0:T(8,128)S(1)} %get-tuple-element.54.refs_3_.refs_4_), channel_id=1, source_target_pairs={{0,6},{1,7},{2,4},{3,5},{4,2},{5,3},{6,0},{7,1},{8,14},{9,15},{10,... | collective-permute-start | bytes 516104 | tf_op jit(solution)/shard_map/ppermute | solution.py:632
  42.7 6.3 %collective-permute-done.14.rest_1_.refs_6_ = f32[16,128]{1,0:T(8,128)S(1)} collective-permute-done((f32[16,128]{1,0:T(8,128)S(1)}, f32[16,128]{1,0:T(8,128)S(1)}, u32[]{:S(2)}, u32[]{:S(2)}) %collective-permute-start.14) | collective-permute-done | bytes 8224 | tf_op jit(solution)/shard_map/ppermute | solution.py:934
  49.7 1.8 %collective-permute-start.17 = (f32[320,128]{1,0:T(8,128)S(1)}, f32[320,128]{1,0:T(8,128)S(1)}, u32[]{:S(2)}, u32[]{:S(2)}) collective-permute-start(f32[320,128]{1,0:T(8,128)S(1)} %get-tuple-element.61.refs_5_.refs_1_), channel_id=1, source_target_pairs={{0,6},{1,7},{2,4},{3,5},{4,2},{5,3},{6,0},{7,1},{8,14},{9,15},{10,... | collective-permute-start | bytes 491528 | tf_op jit(solution)/shard_map/ppermute | solution.py:632
  51.7 1.3 %collective-permute-start.16 = (f32[8,128]{1,0:T(8,128)S(1)}, f32[8,128]{1,0:T(8,128)S(1)}, u32[]{:S(2)}, u32[]{:S(2)}) collective-permute-start(f32[8,128]{1,0:T(8,128)S(1)} %get-tuple-element.56), channel_id=1, source_target_pairs={{0,1},{2,3},{4,5},{6,7},{8,9},{10,11},{12,13},{14,15},{16,17},{18,... | collective-permute-start | bytes 12296 | tf_op jit(solution)/shard_map/ppermute | solution.py:942
  53.8 2.2 %signals.1.refs_8_ = f32[512,128]{1,0:T(8,128)} custom-call(f32[8,128]{1,0:T(8,128)S(1)} %get-tuple-element.55.refs_0_, f32[8,128]{1,0:T(8,128)S(1)} %collective-permute-done.16.refs_1_, f32[4,8,128]{2,1,0:T(8,128)S(1)} %get-tuple-element.51.refs_5_.refs_2_, bf16[512,4096]{1,0:T(8,128)(2,1)S(1)} %get-tuple-element.57.refs_3_, ...), custom_call_target="tpu_custom_call" | custom-call | flops 1 | bytes 1 | tf_op jit(solution)/shard_map/signals/pallas_call | solution.py:654
  56.0 1.0 %collective-permute-done.17.refs_2_.refs_3_ = f32[320,128]{1,0:T(8,128)S(1)} collective-permute-done((f32[320,128]{1,0:T(8,128)S(1)}, f32[320,128]{1,0:T(8,128)S(1)}, u32[]{:S(2)}, u32[]{:S(2)}) %collective-permute-start.17) | collective-permute-done | bytes 163872 | tf_op jit(solution)/shard_map/ppermute | solution.py:632
  57.2 3.7 %all-to-all-start = ((f32[32,16,128]{2,1,0:T(8,128)}), f32[32,16,128]{2,1,0:T(8,128)S(1)}, u32[]{:S(2)}, u32[]{:S(2)}) async-start(f32[32,16,128]{2,1,0:T(8,128)} %bitcast.1), calls=%async_computation | async-start | bytes 524288 | tf_op jit(solution)/shard_map/all_to_all | solution.py:961
  60.9 1.2 %azim_join_kept.1.partial = f32[5,64,8,128]{3,2,1,0:T(8,128)} custom-call(f32[2,5,16,16,128]{4,3,2,1,0:T(8,128)S(1)} %azim_local.1.refs_0_.local, f32[2,6,5,16,128]{4,3,2,1,0:T(8,128)S(1)} %ring_sums.3.refs_1_.ring), custom_call_target="tpu_custom_call" | custom-call | flops 1 | bytes 1 | tf_op jit(solution)/shard_map/azim_join_kept/pallas_call | solution.py:774
  62.1 0.9 %place_rows.1 = f32[5,64,8,128]{3,2,1,0:T(8,128)} custom-call(f32[2,5,8,16,128]{4,3,2,1,0:T(8,128)S(1)} %collective-permute-done.19.values, f32[5,64,8,128]{3,2,1,0:T(8,128)} %azim_join_kept.1.partial), custom_call_target="tpu_custom_call", output_to_operand_aliasing={{}: (1, {})} | custom-call | flops 1 | bytes 1 | tf_op jit(solution)/shard_map/place_rows/pallas_call | solution.py:774
  63.0 8.3 %all-to-all-done = f32[32,16,128]{2,1,0:T(8,128)S(1)} async-done(((f32[32,16,128]{2,1,0:T(8,128)}), f32[32,16,128]{2,1,0:T(8,128)S(1)}, u32[]{:S(2)}, u32[]{:S(2)}) %all-to-all-start) | async-done | bytes 262176 | tf_op jit(solution)/shard_map/all_to_all | solution.py:961
  (77 shorter events, 9.0 us)
Async XLA Ops:
  3.3 2.8 %collective-permute-start = (f32[2,5,8,16,128]{4,3,2,1,0:T(8,128)}, f32[2,5,8,16,128]{4,3,2,1,0:T(8,128)S(1)}, u32[]{:S(2)}, u32[]{:S(2)}) collective-permute-start(f32[2,5,8,16,128]{4,3,2,1,0:T(8,128)} %get-tuple-element.35), channel_id=1, source_target_pairs={{0,1},{1,0},{2,3},{3,2},{4,5},{5,4},{6,7},{7,6},{8,9},{9,8},{10,11... | collective-permute-start | bytes 1966088 | tf_op jit(solution)/shard_map/ppermute | solution.py:622
  3.8 2.3 %collective-permute-start.1 = (f32[2,3,5,16,128]{4,3,2,1,0:T(8,128)}, f32[2,3,5,16,128]{4,3,2,1,0:T(8,128)S(1)}, u32[]{:S(2)}, u32[]{:S(2)}) collective-permute-start(f32[2,3,5,16,128]{4,3,2,1,0:T(8,128)} %get-tuple-element.37), channel_id=1, source_target_pairs={{0,1},{1,0},{2,3},{3,2},{4,5},{5,4},{6,7},{7,6},{8,9},{9,8},{10,11... | collective-permute-start | bytes 737288 | tf_op jit(solution)/shard_map/ppermute | solution.py:622
  8.1 13.6 %collective-permute-start.2 = (f32[1616,128]{1,0:T(8,128)S(1)}, f32[1616,128]{1,0:T(8,128)S(1)}, u32[]{:S(2)}, u32[]{:S(2)}) collective-permute-start(f32[1616,128]{1,0:T(8,128)S(1)} %get-tuple-element.43), channel_id=1, source_target_pairs={{0,1},{1,0},{2,3},{3,2},{4,5},{5,4},{6,7},{7,6},{8,9},{9,8},{10,11... | collective-permute-start | bytes 2482184 | tf_op jit(solution)/shard_map/ppermute | solution.py:622
  8.6 9.0 %collective-permute-start.4 = (f32[240,128]{1,0:T(8,128)S(1)}, f32[240,128]{1,0:T(8,128)S(1)}, u32[]{:S(2)}, u32[]{:S(2)}) collective-permute-start(f32[240,128]{1,0:T(8,128)S(1)} %get-tuple-element.45.refs_3_.refs_4_), channel_id=1, source_target_pairs={{0,6},{1,7},{2,4},{3,5},{4,2},{5,3},{6,0},{7,1},{8,14},{9,15},{10,... | collective-permute-start | bytes 368648 | tf_op jit(solution)/shard_map/ppermute | solution.py:632
  13.3 6.6 %collective-permute-start.3 = (f32[240,128]{1,0:T(8,128)S(1)}, f32[240,128]{1,0:T(8,128)S(1)}, u32[]{:S(2)}, u32[]{:S(2)}) collective-permute-start(f32[240,128]{1,0:T(8,128)S(1)} %get-tuple-element.38.refs_8_.refs_0_), channel_id=1, source_target_pairs={{0,2},{1,3},{2,0},{3,1},{4,6},{5,7},{6,4},{7,5},{8,10},{9,11},{10,... | collective-permute-start | bytes 368648 | tf_op jit(solution)/shard_map/ppermute | solution.py:632
  19.9 8.1 %collective-permute-start.5 = (f32[240,128]{1,0:T(8,128)S(1)}, f32[240,128]{1,0:T(8,128)S(1)}, u32[]{:S(2)}, u32[]{:S(2)}) collective-permute-start(f32[240,128]{1,0:T(8,128)S(1)} %get-tuple-element.47), channel_id=1, source_target_pairs={{0,6},{1,7},{2,4},{3,5},{4,2},{5,3},{6,0},{7,1},{8,14},{9,15},{10,... | collective-permute-start | bytes 368648 | tf_op jit(solution)/shard_map/ppermute | solution.py:632
  21.7 6.8 %collective-permute-start.6 = (f32[240,128]{1,0:T(8,128)S(1)}, f32[240,128]{1,0:T(8,128)S(1)}, u32[]{:S(2)}, u32[]{:S(2)}) collective-permute-start(f32[240,128]{1,0:T(8,128)S(1)} %get-tuple-element.48), channel_id=1, source_target_pairs={{0,2},{1,3},{2,0},{3,1},{4,6},{5,7},{6,4},{7,5},{8,10},{9,11},{10,... | collective-permute-start | bytes 368648 | tf_op jit(solution)/shard_map/ppermute | solution.py:632
  21.8 7.5 %copy-start.9 = (bf16[4,2,24,128]{3,2,1,0:T(8,128)(2,1)S(1)}, bf16[4,2,24,128]{3,2,1,0:T(8,128)(2,1)}, u32[]{:S(2)}) copy-start(bf16[4,2,24,128]{3,2,1,0:T(8,128)(2,1)} %constant.19.clone.refs_6_) | copy-start | bytes 147460
  21.8 7.5 %copy-start.16 = (bf16[2,8,128]{2,1,0:T(8,128)(2,1)S(1)}, bf16[2,8,128]{2,1,0:T(8,128)(2,1)}, u32[]{:S(2)}) copy-start(bf16[2,8,128]{2,1,0:T(8,128)(2,1)} %constant.18.clone.refs_5_) | copy-start | bytes 12292
  21.8 6.7 %collective-permute-start.9 = (f32[8,2560]{1,0:T(8,128)S(1)}, f32[8,2560]{1,0:T(8,128)S(1)}, u32[]{:S(2)}, u32[]{:S(2)}) collective-permute-start(f32[8,2560]{1,0:T(8,128)S(1)} %edge_both.1), channel_id=1, source_target_pairs={{0,24},{8,16},{16,8},{24,0},{1,25},{9,17},{17,9},{25,1},{2,26},{10... | collective-permute-start | bytes 245768 | tf_op jit(solution)/shard_map/ppermute | solution.py:618
  24.3 4.4 %collective-permute-start.8 = (f32[8,2560]{1,0:T(8,128)S(1)}, f32[8,2560]{1,0:T(8,128)S(1)}, u32[]{:S(2)}, u32[]{:S(2)}) collective-permute-start(f32[8,2560]{1,0:T(8,128)S(1)} %edge_both.1), channel_id=1, source_target_pairs={{0,16},{8,24},{16,0},{24,8},{1,17},{9,25},{17,1},{25,9},{2,18},{10... | collective-permute-start | bytes 245768 | tf_op jit(solution)/shard_map/ppermute | solution.py:618
  24.8 4.4 %collective-permute-start.7 = (f32[8,2560]{1,0:T(8,128)S(1)}, f32[8,2560]{1,0:T(8,128)S(1)}, u32[]{:S(2)}, u32[]{:S(2)}) collective-permute-start(f32[8,2560]{1,0:T(8,128)S(1)} %edge_both.1), channel_id=1, source_target_pairs={{0,8},{8,0},{16,24},{24,16},{1,9},{9,1},{17,25},{25,17},{2,10},{10... | collective-permute-start | bytes 245768 | tf_op jit(solution)/shard_map/ppermute | solution.py:618
  30.9 6.9 %collective-permute-start.12 = (f32[8,2560]{1,0:T(8,128)S(1)}, f32[8,2560]{1,0:T(8,128)S(1)}, u32[]{:S(2)}, u32[]{:S(2)}) collective-permute-start(f32[8,2560]{1,0:T(8,128)S(1)} %get-tuple-element.50.refs_5_), channel_id=1, source_target_pairs={{0,24},{8,16},{16,8},{24,0},{1,25},{9,17},{17,9},{25,1},{2,26},{10... | collective-permute-start | bytes 245768 | tf_op jit(solution)/shard_map/ppermute | solution.py:618
  32.7 5.1 %collective-permute-start.11 = (f32[8,2560]{1,0:T(8,128)S(1)}, f32[8,2560]{1,0:T(8,128)S(1)}, u32[]{:S(2)}, u32[]{:S(2)}) collective-permute-start(f32[8,2560]{1,0:T(8,128)S(1)} %get-tuple-element.50.refs_5_), channel_id=1, source_target_pairs={{0,16},{8,24},{16,0},{24,8},{1,17},{9,25},{17,1},{25,9},{2,18},{10... | collective-permute-start | bytes 245768 | tf_op jit(solution)/shard_map/ppermute | solution.py:618
  33.2 4.6 %collective-permute-start.10 = (f32[8,2560]{1,0:T(8,128)S(1)}, f32[8,2560]{1,0:T(8,128)S(1)}, u32[]{:S(2)}, u32[]{:S(2)}) collective-permute-start(f32[8,2560]{1,0:T(8,128)S(1)} %get-tuple-element.50.refs_5_), channel_id=1, source_target_pairs={{0,8},{8,0},{16,24},{24,16},{1,9},{9,1},{17,25},{25,17},{2,10},{10... | collective-permute-start | bytes 245768 | tf_op jit(solution)/shard_map/ppermute | solution.py:618
  35.2 16.4 %copy-start.11 = (f32[4,16,64]{2,1,0:T(8,128)S(1)}, f32[4,16,64]{2,1,0:T(8,128)}, u32[]{:S(2)}) copy-start(f32[4,16,64]{2,1,0:T(8,128)} %constant.22.clone.around) | copy-start | bytes 49156
  38.6 10.5 %collective-permute-start.13 = (f32[336,128]{1,0:T(8,128)S(1)}, f32[336,128]{1,0:T(8,128)S(1)}, u32[]{:S(2)}, u32[]{:S(2)}) collective-permute-start(f32[336,128]{1,0:T(8,128)S(1)} %get-tuple-element.53.refs_0_), channel_id=1, source_target_pairs={{0,2},{1,3},{2,0},{3,1},{4,6},{5,7},{6,4},{7,5},{8,10},{9,11},{10,... | collective-permute-start | bytes 516104 | tf_op jit(solution)/shard_map/ppermute | solution.py:632
  40.5 8.5 %collective-permute-start.15 = (f32[336,128]{1,0:T(8,128)S(1)}, f32[336,128]{1,0:T(8,128)S(1)}, u32[]{:S(2)}, u32[]{:S(2)}) collective-permute-start(f32[336,128]{1,0:T(8,128)S(1)} %get-tuple-element.54.refs_3_.refs_4_), channel_id=1, source_target_pairs={{0,6},{1,7},{2,4},{3,5},{4,2},{5,3},{6,0},{7,1},{8,14},{9,15},{10,... | collective-permute-start | bytes 516104 | tf_op jit(solution)/shard_map/ppermute | solution.py:632
  42.7 6.3 %collective-permute-start.14 = (f32[16,128]{1,0:T(8,128)S(1)}, f32[16,128]{1,0:T(8,128)S(1)}, u32[]{:S(2)}, u32[]{:S(2)}) collective-permute-start(f32[16,128]{1,0:T(8,128)S(1)} %get-tuple-element.52.front), channel_id=1, source_target_pairs={{0,4},{1,5},{2,6},{3,7},{4,0},{5,1},{6,2},{7,3},{8,12},{9,13},{10,... | collective-permute-start | bytes 24584 | tf_op jit(solution)/shard_map/ppermute | solution.py:934
  49.1 6.9 %collective-permute-start.18 = (f32[320,128]{1,0:T(8,128)S(1)}, f32[320,128]{1,0:T(8,128)S(1)}, u32[]{:S(2)}, u32[]{:S(2)}) collective-permute-start(f32[320,128]{1,0:T(8,128)S(1)} %get-tuple-element.63), channel_id=1, source_target_pairs={{0,2},{1,3},{2,0},{3,1},{4,6},{5,7},{6,4},{7,5},{8,10},{9,11},{10,... | collective-permute-start | bytes 491528 | tf_op jit(solution)/shard_map/ppermute | solution.py:632
  49.7 7.2 %collective-permute-start.17 = (f32[320,128]{1,0:T(8,128)S(1)}, f32[320,128]{1,0:T(8,128)S(1)}, u32[]{:S(2)}, u32[]{:S(2)}) collective-permute-start(f32[320,128]{1,0:T(8,128)S(1)} %get-tuple-element.61.refs_5_.refs_1_), channel_id=1, source_target_pairs={{0,6},{1,7},{2,4},{3,5},{4,2},{5,3},{6,0},{7,1},{8,14},{9,15},{10,... | collective-permute-start | bytes 491528 | tf_op jit(solution)/shard_map/ppermute | solution.py:632
  51.7 2.1 %collective-permute-start.16 = (f32[8,128]{1,0:T(8,128)S(1)}, f32[8,128]{1,0:T(8,128)S(1)}, u32[]{:S(2)}, u32[]{:S(2)}) collective-permute-start(f32[8,128]{1,0:T(8,128)S(1)} %get-tuple-element.56), channel_id=1, source_target_pairs={{0,1},{2,3},{4,5},{6,7},{8,9},{10,11},{12,13},{14,15},{16,17},{18,... | collective-permute-start | bytes 12296 | tf_op jit(solution)/shard_map/ppermute | solution.py:942
  57.1 5.0 %collective-permute-start.19 = (f32[2,5,8,16,128]{4,3,2,1,0:T(8,128)S(1)}, f32[2,5,8,16,128]{4,3,2,1,0:T(8,128)S(1)}, u32[]{:S(2)}, u32[]{:S(2)}) collective-permute-start(f32[2,5,8,16,128]{4,3,2,1,0:T(8,128)S(1)} %azim_join_sent.1), channel_id=1, source_target_pairs={{0,1},{1,0},{2,3},{3,2},{4,5},{5,4},{6,7},{7,6},{8,9},{9,8},{10,11... | collective-permute-start | bytes 1966088 | tf_op jit(solution)/shard_map/ppermute | solution.py:622
  57.2 14.1 %all-to-all-start = ((f32[32,16,128]{2,1,0:T(8,128)}), f32[32,16,128]{2,1,0:T(8,128)S(1)}, u32[]{:S(2)}, u32[]{:S(2)}) async-start(f32[32,16,128]{2,1,0:T(8,128)} %bitcast.1), calls=%async_computation | async-start | bytes 524288 | tf_op jit(solution)/shard_map/all_to_all | solution.py:961
  (16 other events, 38.2 us)

commit v7 on v6

--- a/solution.py
+++ b/solution.py
@@ -830,6 +830,8 @@
     arrived = [partner(packs[turn], around, turn, 0) for turn in range(2)]
     def by_quarter(*refs):
         inputs, (own, basis, base_out, scale_out, edge_out, *scratch) = refs[:6], refs[6:]
+        kept, sent = base_out, scale_out
+        base_out, scale_out, edge_out, *scratch = (edge_out, *scratch)
         for step in range(4):
             here = slice(step * part, (step + 1) * part)
             pieces = [ref.at[here] if len(ref.shape) == 3 else ref.at[:, here] for ref in inputs]
@@ -842,15 +844,13 @@
                 edge_out.at[:, step * lines : (step + 1) * lines],
                 *scratch,
             )
-
-    base, scale, edge_d = whole_call(
+        section_split_kernel(base_out, scale_out, edge_out, kept, sent)
+
+    flat = shaped(2 * (FIELDS + 1) * rows * part + 2 * FIELDS * BASIS, lanes)
+    base_kept, base_sent = whole_call(
         by_quarter,
         "section_local",
-        [
-            shaped(4, FIELDS, rows, part, lanes),
-            shaped(4, rows, part, lanes),
-            shaped(BASIS, 4 * lines),
-        ],
+        [flat, flat],
         (
             density,
             velocity,
@@ -862,11 +862,13 @@
             jnp.asarray(basis_d),
         ),
         wait=(packs[0], flux_in),
-        scratch=[flux_scratch] * 2,
-    )
-    flat = shaped(2 * (FIELDS + 1) * rows * part + 2 * FIELDS * BASIS, lanes)
-    base_kept, base_sent = whole_call(
-        section_split_kernel, "section_split", [flat, flat], (base, scale, edge_d)
+        scratch=[
+            pltpu.VMEM((4, FIELDS, rows, part, lanes), f32),
+            pltpu.VMEM((4, rows, part, lanes), f32),
+            pltpu.VMEM((BASIS, 4 * lines), f32),
+            flux_scratch,
+            flux_scratch,
+        ],
     )
     base_in = sibling(base_sent, around)
     (edge_d,) = whole_call(

time: 72.3 us -> 72.4 us (level)
    pallas_call x16 -> x15, Pallas kernels: 11 us -> 11.1 us  [whole_call(): pl.pallas_call(waiting(kernel, len(args), wait), in_specs=[whole] * len(a...]
where the time goes in v7:
time: 72.4 us; the launch traced here: 72.1 us
  waiting for transfers between devices  26.9 us (37%)
  starting transfers between devices  26.4 us (36%)
  Pallas kernels  17.1 us (24%)
  between operations  0.96 us (1%)
    ppermute x8, starting transfers between devices, partner(): return lax.ppermute(values, 'azim', pairs)  13.2 us
    pallas_call x15, Pallas kernels, whole_call(): pl.pallas_call(waiting(kernel, len(args), wait), in_specs=[whole] * len(a...  11.1 us
    ppermute x8, waiting for transfers between devices, partner(): return lax.ppermute(values, 'azim', pairs)  10.7 us
    all_to_all x1, waiting for transfers between devices, per_device(): lax.all_to_all(partial.reshape(devices, OBSERVERS // devices, TIME_BINS),...  8.31 us
    ppermute x6, starting transfers between devices, swap(): return lax.ppermute(values, axis, [(i, i ^ mask) for i in range(count)])  7.08 us
    ppermute x1, waiting for transfers between devices, per_device(): fronts[at] = lax.ppermute(front, 'azim', pairs)  6.33 us
    pallas_call x2, Pallas kernels, apart(): pl.pallas_call(waiting(kernel, len(args), wait), in_specs=[spec(memory_sp...  3.92 us
    all_to_all x1, starting transfers between devices, per_device(): lax.all_to_all(partial.reshape(devices, OBSERVERS // devices, TIME_BINS),...  3.69 us
  transfers between devices with their start and end apart: 21, of which 11 were waited for; matrix products, arithmetic and copies ran while one was open for 0% of the time, Pallas kernels for 14%

profile of v7, /device:TPU:0, one launch (start us, length us, event | category | flops | bytes accessed | tf_op | source)
XLA Modules:
  0.0 72.1 jit_solution(16802486653428704164)
XLA Ops:
  0.7 2.6 %azim_flux_sent.1 = (f32[2,5,8,16,128]{4,3,2,1,0:T(8,128)}, f32[2,3,5,16,128]{4,3,2,1,0:T(8,128)}) custom-call(f32[64,8,128]{2,1,0:T(8,128)} %refs_0_.1, f32[3,64,8,128]{3,2,1,0:T(8,128)} %refs_1_.4, f32[64,8,128]{2,1,0:T(8,128)} %refs_2_.2, f32[3,64,8,128]{3,2,1,0:T(8,128)} %azim_metric.3, f32[64,8,128]{2,1,0:T(8,128)} %refs_4_.2), custom_call_target="tpu_custom_call" | custom-call | flops 1 | bytes 1 | tf_op jit(solution)/shard_map/azim_flux_sent/pallas_call | solution.py:795
  4.0 1.3 %azim_flux_kept.1 = (f32[2,5,8,16,128]{4,3,2,1,0:T(8,128)S(1)}, f32[2,3,5,16,128]{4,3,2,1,0:T(8,128)S(1)}) custom-call(f32[64,8,128]{2,1,0:T(8,128)S(1)} %copy-done.2, f32[3,64,8,128]{3,2,1,0:T(8,128)S(1)} %copy-done, f32[64,8,128]{2,1,0:T(8,128)S(1)} %copy-done.3, f32[3,64,8,128]{3,2,1,0:T(8,128)S(1)} %copy-done.1, f32[64,8,128]{2,1,0:T(8,128)S(1)} %copy-done.4), custom_call_target="tpu_custom_call" | custom-call | flops 1 | bytes 1 | tf_op jit(solution)/shard_map/azim_flux_kept/pallas_call | solution.py:795
  6.2 2.0 %section_local.1 = (f32[1616,128]{1,0:T(8,128)S(1)}, f32[1616,128]{1,0:T(8,128)S(1)}) custom-call(f32[64,8,128]{2,1,0:T(8,128)S(1)} %copy-done.2, f32[3,64,8,128]{3,2,1,0:T(8,128)S(1)} %copy-done, f32[64,8,128]{2,1,0:T(8,128)S(1)} %copy-done.3, f32[3,64,8,128]{3,2,1,0:T(8,128)S(1)} %copy-done.6, f32[64,8,128]{2,1,0:T(8,128)S(1)} %copy-done.4, ...), custom_call_target="tpu_custom_call" | custom-call | flops 1 | bytes 1 | tf_op jit(solution)/shard_map/section_local/pallas_call | solution.py:654
  8.7 4.7 %collective-permute-start.4 = (f32[240,128]{1,0:T(8,128)S(1)}, f32[240,128]{1,0:T(8,128)S(1)}, u32[]{:S(2)}, u32[]{:S(2)}) collective-permute-start(f32[240,128]{1,0:T(8,128)S(1)} %get-tuple-element.39.refs_3_.refs_4_), channel_id=1, source_target_pairs={{0,6},{1,7},{2,4},{3,5},{4,2},{5,3},{6,0},{7,1},{8,14},{9,15},{10,... | collective-permute-start | bytes 368648 | tf_op jit(solution)/shard_map/ppermute | solution.py:632
  13.4 4.2 %collective-permute-done.4.refs_4_.refs_5_ = f32[240,128]{1,0:T(8,128)S(1)} collective-permute-done((f32[240,128]{1,0:T(8,128)S(1)}, f32[240,128]{1,0:T(8,128)S(1)}, u32[]{:S(2)}, u32[]{:S(2)}) %collective-permute-start.4) | collective-permute-done | bytes 122912 | tf_op jit(solution)/shard_map/ppermute | solution.py:632
  17.6 2.4 %collective-permute-done.3.refs_1_ = f32[240,128]{1,0:T(8,128)S(1)} collective-permute-done((f32[240,128]{1,0:T(8,128)S(1)}, f32[240,128]{1,0:T(8,128)S(1)}, u32[]{:S(2)}, u32[]{:S(2)}) %collective-permute-start.3) | collective-permute-done | bytes 122912 | tf_op jit(solution)/shard_map/ppermute | solution.py:632
  20.0 1.7 %collective-permute-start.5 = (f32[240,128]{1,0:T(8,128)S(1)}, f32[240,128]{1,0:T(8,128)S(1)}, u32[]{:S(2)}, u32[]{:S(2)}) collective-permute-start(f32[240,128]{1,0:T(8,128)S(1)} %get-tuple-element.41), channel_id=1, source_target_pairs={{0,6},{1,7},{2,4},{3,5},{4,2},{5,3},{6,0},{7,1},{8,14},{9,15},{10,... | collective-permute-start | bytes 368648 | tf_op jit(solution)/shard_map/ppermute | solution.py:632
  21.9 2.5 %collective-permute-start.9 = (f32[8,2560]{1,0:T(8,128)S(1)}, f32[8,2560]{1,0:T(8,128)S(1)}, u32[]{:S(2)}, u32[]{:S(2)}) collective-permute-start(f32[8,2560]{1,0:T(8,128)S(1)} %edge_both.1), channel_id=1, source_target_pairs={{0,24},{8,16},{16,8},{24,0},{1,25},{9,17},{17,9},{25,1},{2,26},{10... | collective-permute-start | bytes 245768 | tf_op jit(solution)/shard_map/ppermute | solution.py:618
  25.5 2.7 %collective-permute-done.5.refs_2_.refs_3_ = f32[240,128]{1,0:T(8,128)S(1)} collective-permute-done((f32[240,128]{1,0:T(8,128)S(1)}, f32[240,128]{1,0:T(8,128)S(1)}, u32[]{:S(2)}, u32[]{:S(2)}) %collective-permute-start.5) | collective-permute-done | bytes 122912 | tf_op jit(solution)/shard_map/ppermute | solution.py:632
  29.4 1.6 %section_join.1 = (f32[2,5,16,16,128]{4,3,2,1,0:T(8,128)S(1)}, f32[8,2560]{1,0:T(8,128)S(1)}) custom-call(f32[2,5,8,16,128]{4,3,2,1,0:T(8,128)S(1)} %get-tuple-element.31.refs_0_, f32[2,5,8,16,128]{4,3,2,1,0:T(8,128)S(1)} %collective-permute-done.refs_9_.refs_1_, f32[1616,128]{1,0:T(8,128)S(1)} %get-tuple-element.36.kept.refs_2_, ...), custom_call_target="tpu_custom_call" | custom-call | flops 1 | bytes 1 | tf_op jit(solution)/shard_map/section_join/pallas_call | solution.py:654
  31.0 1.8 %collective-permute-start.12 = (f32[8,2560]{1,0:T(8,128)S(1)}, f32[8,2560]{1,0:T(8,128)S(1)}, u32[]{:S(2)}, u32[]{:S(2)}) collective-permute-start(f32[8,2560]{1,0:T(8,128)S(1)} %get-tuple-element.44.refs_5_), channel_id=1, source_target_pairs={{0,24},{8,16},{16,8},{24,0},{1,25},{9,17},{17,9},{25,1},{2,26},{10... | collective-permute-start | bytes 245768 | tf_op jit(solution)/shard_map/ppermute | solution.py:618
  33.3 1.2 %collective-permute-start.10 = (f32[8,2560]{1,0:T(8,128)S(1)}, f32[8,2560]{1,0:T(8,128)S(1)}, u32[]{:S(2)}, u32[]{:S(2)}) collective-permute-start(f32[8,2560]{1,0:T(8,128)S(1)} %get-tuple-element.44.refs_5_), channel_id=1, source_target_pairs={{0,8},{8,0},{16,24},{24,16},{1,9},{9,1},{17,25},{25,17},{2,10},{10... | collective-permute-start | bytes 245768 | tf_op jit(solution)/shard_map/ppermute | solution.py:618
  35.3 2.6 %entries.1 = (f32[4,8,128]{2,1,0:T(8,128)S(1)}, bf16[512,4096]{1,0:T(8,128)(2,1)S(1)}, bf16[128,4096]{1,0:T(8,128)(2,1)S(1)}) custom-call(f32[2,128]{1,0:T(2,128)S(1)} %bitcast.2, s32[4,8,128]{2,1,0:T(8,128)S(1)} %copy-done.12, f32[8,128]{1,0:T(8,128)S(1)} %copy-done.15, s32[4,8,128]{2,1,0:T(8,128)S(1)} %copy-done.13, s32[4,8,128]{2,1,0:T(8,128)S(1)} %copy-done.14, ...), custom_call_target="tpu_custom_call" | custom-call | flops 1 | bytes 1 | tf_op jit(solution)/shard_map/entries/pallas_call | solution.py:654
  38.7 2.0 %collective-permute-start.13 = (f32[336,128]{1,0:T(8,128)S(1)}, f32[336,128]{1,0:T(8,128)S(1)}, u32[]{:S(2)}, u32[]{:S(2)}) collective-permute-start(f32[336,128]{1,0:T(8,128)S(1)} %get-tuple-element.47.refs_0_), channel_id=1, source_target_pairs={{0,2},{1,3},{2,0},{3,1},{4,6},{5,7},{6,4},{7,5},{8,10},{9,11},{10,... | collective-permute-start | bytes 516104 | tf_op jit(solution)/shard_map/ppermute | solution.py:632
  40.7 2.2 %collective-permute-start.15 = (f32[336,128]{1,0:T(8,128)S(1)}, f32[336,128]{1,0:T(8,128)S(1)}, u32[]{:S(2)}, u32[]{:S(2)}) collective-permute-start(f32[336,128]{1,0:T(8,128)S(1)} %get-tuple-element.48.refs_3_.refs_4_), channel_id=1, source_target_pairs={{0,6},{1,7},{2,4},{3,5},{4,2},{5,3},{6,0},{7,1},{8,14},{9,15},{10,... | collective-permute-start | bytes 516104 | tf_op jit(solution)/shard_map/ppermute | solution.py:632
  42.8 6.3 %collective-permute-done.14.rest_1_.refs_6_ = f32[16,128]{1,0:T(8,128)S(1)} collective-permute-done((f32[16,128]{1,0:T(8,128)S(1)}, f32[16,128]{1,0:T(8,128)S(1)}, u32[]{:S(2)}, u32[]{:S(2)}) %collective-permute-start.14) | collective-permute-done | bytes 8224 | tf_op jit(solution)/shard_map/ppermute | solution.py:936
  49.8 1.8 %collective-permute-start.17 = (f32[320,128]{1,0:T(8,128)S(1)}, f32[320,128]{1,0:T(8,128)S(1)}, u32[]{:S(2)}, u32[]{:S(2)}) collective-permute-start(f32[320,128]{1,0:T(8,128)S(1)} %get-tuple-element.55.refs_5_.refs_1_), channel_id=1, source_target_pairs={{0,6},{1,7},{2,4},{3,5},{4,2},{5,3},{6,0},{7,1},{8,14},{9,15},{10,... | collective-permute-start | bytes 491528 | tf_op jit(solution)/shard_map/ppermute | solution.py:632
  51.8 1.3 %collective-permute-start.16 = (f32[8,128]{1,0:T(8,128)S(1)}, f32[8,128]{1,0:T(8,128)S(1)}, u32[]{:S(2)}, u32[]{:S(2)}) collective-permute-start(f32[8,128]{1,0:T(8,128)S(1)} %get-tuple-element.50), channel_id=1, source_target_pairs={{0,1},{2,3},{4,5},{6,7},{8,9},{10,11},{12,13},{14,15},{16,17},{18,... | collective-permute-start | bytes 12296 | tf_op jit(solution)/shard_map/ppermute | solution.py:944
  53.9 2.2 %signals.1.refs_8_ = f32[512,128]{1,0:T(8,128)} custom-call(f32[8,128]{1,0:T(8,128)S(1)} %get-tuple-element.49.refs_0_, f32[8,128]{1,0:T(8,128)S(1)} %collective-permute-done.16.refs_1_, f32[4,8,128]{2,1,0:T(8,128)S(1)} %get-tuple-element.45.refs_5_.refs_2_, bf16[512,4096]{1,0:T(8,128)(2,1)S(1)} %get-tuple-element.51.refs_3_, ...), custom_call_target="tpu_custom_call" | custom-call | flops 1 | bytes 1 | tf_op jit(solution)/shard_map/signals/pallas_call | solution.py:654
  56.1 1.0 %collective-permute-done.17.refs_2_.refs_3_ = f32[320,128]{1,0:T(8,128)S(1)} collective-permute-done((f32[320,128]{1,0:T(8,128)S(1)}, f32[320,128]{1,0:T(8,128)S(1)}, u32[]{:S(2)}, u32[]{:S(2)}) %collective-permute-start.17) | collective-permute-done | bytes 163872 | tf_op jit(solution)/shard_map/ppermute | solution.py:632
  57.3 3.7 %all-to-all-start = ((f32[32,16,128]{2,1,0:T(8,128)}), f32[32,16,128]{2,1,0:T(8,128)S(1)}, u32[]{:S(2)}, u32[]{:S(2)}) async-start(f32[32,16,128]{2,1,0:T(8,128)} %bitcast.1), calls=%async_computation | async-start | bytes 524288 | tf_op jit(solution)/shard_map/all_to_all | solution.py:963
  61.0 1.2 %azim_join_kept.1.partial = f32[5,64,8,128]{3,2,1,0:T(8,128)} custom-call(f32[2,5,16,16,128]{4,3,2,1,0:T(8,128)S(1)} %azim_local.1.refs_0_.local, f32[2,6,5,16,128]{4,3,2,1,0:T(8,128)S(1)} %ring_sums.3.refs_1_.ring), custom_call_target="tpu_custom_call" | custom-call | flops 1 | bytes 1 | tf_op jit(solution)/shard_map/azim_join_kept/pallas_call | solution.py:774
  62.2 0.9 %place_rows.1 = f32[5,64,8,128]{3,2,1,0:T(8,128)} custom-call(f32[2,5,8,16,128]{4,3,2,1,0:T(8,128)S(1)} %collective-permute-done.19.values, f32[5,64,8,128]{3,2,1,0:T(8,128)} %azim_join_kept.1.partial), custom_call_target="tpu_custom_call", output_to_operand_aliasing={{}: (1, {})} | custom-call | flops 1 | bytes 1 | tf_op jit(solution)/shard_map/place_rows/pallas_call | solution.py:774
  63.1 8.3 %all-to-all-done = f32[32,16,128]{2,1,0:T(8,128)S(1)} async-done(((f32[32,16,128]{2,1,0:T(8,128)}), f32[32,16,128]{2,1,0:T(8,128)S(1)}, u32[]{:S(2)}, u32[]{:S(2)}) %all-to-all-start) | async-done | bytes 262176 | tf_op jit(solution)/shard_map/all_to_all | solution.py:963
  (76 shorter events, 8.9 us)
Async XLA Ops:
  3.3 2.8 %collective-permute-start = (f32[2,5,8,16,128]{4,3,2,1,0:T(8,128)}, f32[2,5,8,16,128]{4,3,2,1,0:T(8,128)S(1)}, u32[]{:S(2)}, u32[]{:S(2)}) collective-permute-start(f32[2,5,8,16,128]{4,3,2,1,0:T(8,128)} %get-tuple-element.32), channel_id=1, source_target_pairs={{0,1},{1,0},{2,3},{3,2},{4,5},{5,4},{6,7},{7,6},{8,9},{9,8},{10,11... | collective-permute-start | bytes 1966088 | tf_op jit(solution)/shard_map/ppermute | solution.py:622
  3.8 2.3 %collective-permute-start.1 = (f32[2,3,5,16,128]{4,3,2,1,0:T(8,128)}, f32[2,3,5,16,128]{4,3,2,1,0:T(8,128)S(1)}, u32[]{:S(2)}, u32[]{:S(2)}) collective-permute-start(f32[2,3,5,16,128]{4,3,2,1,0:T(8,128)} %get-tuple-element.34), channel_id=1, source_target_pairs={{0,1},{1,0},{2,3},{3,2},{4,5},{5,4},{6,7},{7,6},{8,9},{9,8},{10,11... | collective-permute-start | bytes 737288 | tf_op jit(solution)/shard_map/ppermute | solution.py:622
  8.2 13.6 %collective-permute-start.2 = (f32[1616,128]{1,0:T(8,128)S(1)}, f32[1616,128]{1,0:T(8,128)S(1)}, u32[]{:S(2)}, u32[]{:S(2)}) collective-permute-start(f32[1616,128]{1,0:T(8,128)S(1)} %get-tuple-element.37), channel_id=1, source_target_pairs={{0,1},{1,0},{2,3},{3,2},{4,5},{5,4},{6,7},{7,6},{8,9},{9,8},{10,11... | collective-permute-start | bytes 2482184 | tf_op jit(solution)/shard_map/ppermute | solution.py:622
  8.7 8.9 %collective-permute-start.4 = (f32[240,128]{1,0:T(8,128)S(1)}, f32[240,128]{1,0:T(8,128)S(1)}, u32[]{:S(2)}, u32[]{:S(2)}) collective-permute-start(f32[240,128]{1,0:T(8,128)S(1)} %get-tuple-element.39.refs_3_.refs_4_), channel_id=1, source_target_pairs={{0,6},{1,7},{2,4},{3,5},{4,2},{5,3},{6,0},{7,1},{8,14},{9,15},{10,... | collective-permute-start | bytes 368648 | tf_op jit(solution)/shard_map/ppermute | solution.py:632
  13.4 6.6 %collective-permute-start.3 = (f32[240,128]{1,0:T(8,128)S(1)}, f32[240,128]{1,0:T(8,128)S(1)}, u32[]{:S(2)}, u32[]{:S(2)}) collective-permute-start(f32[240,128]{1,0:T(8,128)S(1)} %get-tuple-element.35.refs_8_.refs_0_), channel_id=1, source_target_pairs={{0,2},{1,3},{2,0},{3,1},{4,6},{5,7},{6,4},{7,5},{8,10},{9,11},{10,... | collective-permute-start | bytes 368648 | tf_op jit(solution)/shard_map/ppermute | solution.py:632
  20.0 8.1 %collective-permute-start.5 = (f32[240,128]{1,0:T(8,128)S(1)}, f32[240,128]{1,0:T(8,128)S(1)}, u32[]{:S(2)}, u32[]{:S(2)}) collective-permute-start(f32[240,128]{1,0:T(8,128)S(1)} %get-tuple-element.41), channel_id=1, source_target_pairs={{0,6},{1,7},{2,4},{3,5},{4,2},{5,3},{6,0},{7,1},{8,14},{9,15},{10,... | collective-permute-start | bytes 368648 | tf_op jit(solution)/shard_map/ppermute | solution.py:632
  21.8 6.8 %collective-permute-start.6 = (f32[240,128]{1,0:T(8,128)S(1)}, f32[240,128]{1,0:T(8,128)S(1)}, u32[]{:S(2)}, u32[]{:S(2)}) collective-permute-start(f32[240,128]{1,0:T(8,128)S(1)} %get-tuple-element.42), channel_id=1, source_target_pairs={{0,2},{1,3},{2,0},{3,1},{4,6},{5,7},{6,4},{7,5},{8,10},{9,11},{10,... | collective-permute-start | bytes 368648 | tf_op jit(solution)/shard_map/ppermute | solution.py:632
  21.9 7.5 %copy-start.9 = (bf16[4,2,24,128]{3,2,1,0:T(8,128)(2,1)S(1)}, bf16[4,2,24,128]{3,2,1,0:T(8,128)(2,1)}, u32[]{:S(2)}) copy-start(bf16[4,2,24,128]{3,2,1,0:T(8,128)(2,1)} %constant.19.clone.refs_6_) | copy-start | bytes 147460
  21.9 7.5 %copy-start.16 = (bf16[2,8,128]{2,1,0:T(8,128)(2,1)S(1)}, bf16[2,8,128]{2,1,0:T(8,128)(2,1)}, u32[]{:S(2)}) copy-start(bf16[2,8,128]{2,1,0:T(8,128)(2,1)} %constant.18.clone.refs_5_) | copy-start | bytes 12292
  21.9 6.7 %collective-permute-start.9 = (f32[8,2560]{1,0:T(8,128)S(1)}, f32[8,2560]{1,0:T(8,128)S(1)}, u32[]{:S(2)}, u32[]{:S(2)}) collective-permute-start(f32[8,2560]{1,0:T(8,128)S(1)} %edge_both.1), channel_id=1, source_target_pairs={{0,24},{8,16},{16,8},{24,0},{1,25},{9,17},{17,9},{25,1},{2,26},{10... | collective-permute-start | bytes 245768 | tf_op jit(solution)/shard_map/ppermute | solution.py:618
  24.4 4.4 %collective-permute-start.8 = (f32[8,2560]{1,0:T(8,128)S(1)}, f32[8,2560]{1,0:T(8,128)S(1)}, u32[]{:S(2)}, u32[]{:S(2)}) collective-permute-start(f32[8,2560]{1,0:T(8,128)S(1)} %edge_both.1), channel_id=1, source_target_pairs={{0,16},{8,24},{16,0},{24,8},{1,17},{9,25},{17,1},{25,9},{2,18},{10... | collective-permute-start | bytes 245768 | tf_op jit(solution)/shard_map/ppermute | solution.py:618
  24.9 4.4 %collective-permute-start.7 = (f32[8,2560]{1,0:T(8,128)S(1)}, f32[8,2560]{1,0:T(8,128)S(1)}, u32[]{:S(2)}, u32[]{:S(2)}) collective-permute-start(f32[8,2560]{1,0:T(8,128)S(1)} %edge_both.1), channel_id=1, source_target_pairs={{0,8},{8,0},{16,24},{24,16},{1,9},{9,1},{17,25},{25,17},{2,10},{10... | collective-permute-start | bytes 245768 | tf_op jit(solution)/shard_map/ppermute | solution.py:618
  31.0 6.9 %collective-permute-start.12 = (f32[8,2560]{1,0:T(8,128)S(1)}, f32[8,2560]{1,0:T(8,128)S(1)}, u32[]{:S(2)}, u32[]{:S(2)}) collective-permute-start(f32[8,2560]{1,0:T(8,128)S(1)} %get-tuple-element.44.refs_5_), channel_id=1, source_target_pairs={{0,24},{8,16},{16,8},{24,0},{1,25},{9,17},{17,9},{25,1},{2,26},{10... | collective-permute-start | bytes 245768 | tf_op jit(solution)/shard_map/ppermute | solution.py:618
  32.8 5.1 %collective-permute-start.11 = (f32[8,2560]{1,0:T(8,128)S(1)}, f32[8,2560]{1,0:T(8,128)S(1)}, u32[]{:S(2)}, u32[]{:S(2)}) collective-permute-start(f32[8,2560]{1,0:T(8,128)S(1)} %get-tuple-element.44.refs_5_), channel_id=1, source_target_pairs={{0,16},{8,24},{16,0},{24,8},{1,17},{9,25},{17,1},{25,9},{2,18},{10... | collective-permute-start | bytes 245768 | tf_op jit(solution)/shard_map/ppermute | solution.py:618
  33.3 4.6 %collective-permute-start.10 = (f32[8,2560]{1,0:T(8,128)S(1)}, f32[8,2560]{1,0:T(8,128)S(1)}, u32[]{:S(2)}, u32[]{:S(2)}) collective-permute-start(f32[8,2560]{1,0:T(8,128)S(1)} %get-tuple-element.44.refs_5_), channel_id=1, source_target_pairs={{0,8},{8,0},{16,24},{24,16},{1,9},{9,1},{17,25},{25,17},{2,10},{10... | collective-permute-start | bytes 245768 | tf_op jit(solution)/shard_map/ppermute | solution.py:618
  35.3 16.4 %copy-start.11 = (f32[4,16,64]{2,1,0:T(8,128)S(1)}, f32[4,16,64]{2,1,0:T(8,128)}, u32[]{:S(2)}) copy-start(f32[4,16,64]{2,1,0:T(8,128)} %constant.22.clone.around) | copy-start | bytes 49156
  38.7 10.5 %collective-permute-start.13 = (f32[336,128]{1,0:T(8,128)S(1)}, f32[336,128]{1,0:T(8,128)S(1)}, u32[]{:S(2)}, u32[]{:S(2)}) collective-permute-start(f32[336,128]{1,0:T(8,128)S(1)} %get-tuple-element.47.refs_0_), channel_id=1, source_target_pairs={{0,2},{1,3},{2,0},{3,1},{4,6},{5,7},{6,4},{7,5},{8,10},{9,11},{10,... | collective-permute-start | bytes 516104 | tf_op jit(solution)/shard_map/ppermute | solution.py:632
  40.7 8.5 %collective-permute-start.15 = (f32[336,128]{1,0:T(8,128)S(1)}, f32[336,128]{1,0:T(8,128)S(1)}, u32[]{:S(2)}, u32[]{:S(2)}) collective-permute-start(f32[336,128]{1,0:T(8,128)S(1)} %get-tuple-element.48.refs_3_.refs_4_), channel_id=1, source_target_pairs={{0,6},{1,7},{2,4},{3,5},{4,2},{5,3},{6,0},{7,1},{8,14},{9,15},{10,... | collective-permute-start | bytes 516104 | tf_op jit(solution)/shard_map/ppermute | solution.py:632
  42.8 6.3 %collective-permute-start.14 = (f32[16,128]{1,0:T(8,128)S(1)}, f32[16,128]{1,0:T(8,128)S(1)}, u32[]{:S(2)}, u32[]{:S(2)}) collective-permute-start(f32[16,128]{1,0:T(8,128)S(1)} %get-tuple-element.46.front), channel_id=1, source_target_pairs={{0,4},{1,5},{2,6},{3,7},{4,0},{5,1},{6,2},{7,3},{8,12},{9,13},{10,... | collective-permute-start | bytes 24584 | tf_op jit(solution)/shard_map/ppermute | solution.py:936
  49.2 6.9 %collective-permute-start.18 = (f32[320,128]{1,0:T(8,128)S(1)}, f32[320,128]{1,0:T(8,128)S(1)}, u32[]{:S(2)}, u32[]{:S(2)}) collective-permute-start(f32[320,128]{1,0:T(8,128)S(1)} %get-tuple-element.57), channel_id=1, source_target_pairs={{0,2},{1,3},{2,0},{3,1},{4,6},{5,7},{6,4},{7,5},{8,10},{9,11},{10,... | collective-permute-start | bytes 491528 | tf_op jit(solution)/shard_map/ppermute | solution.py:632
  49.8 7.2 %collective-permute-start.17 = (f32[320,128]{1,0:T(8,128)S(1)}, f32[320,128]{1,0:T(8,128)S(1)}, u32[]{:S(2)}, u32[]{:S(2)}) collective-permute-start(f32[320,128]{1,0:T(8,128)S(1)} %get-tuple-element.55.refs_5_.refs_1_), channel_id=1, source_target_pairs={{0,6},{1,7},{2,4},{3,5},{4,2},{5,3},{6,0},{7,1},{8,14},{9,15},{10,... | collective-permute-start | bytes 491528 | tf_op jit(solution)/shard_map/ppermute | solution.py:632
  51.8 2.1 %collective-permute-start.16 = (f32[8,128]{1,0:T(8,128)S(1)}, f32[8,128]{1,0:T(8,128)S(1)}, u32[]{:S(2)}, u32[]{:S(2)}) collective-permute-start(f32[8,128]{1,0:T(8,128)S(1)} %get-tuple-element.50), channel_id=1, source_target_pairs={{0,1},{2,3},{4,5},{6,7},{8,9},{10,11},{12,13},{14,15},{16,17},{18,... | collective-permute-start | bytes 12296 | tf_op jit(solution)/shard_map/ppermute | solution.py:944
  57.3 4.9 %collective-permute-start.19 = (f32[2,5,8,16,128]{4,3,2,1,0:T(8,128)S(1)}, f32[2,5,8,16,128]{4,3,2,1,0:T(8,128)S(1)}, u32[]{:S(2)}, u32[]{:S(2)}) collective-permute-start(f32[2,5,8,16,128]{4,3,2,1,0:T(8,128)S(1)} %azim_join_sent.1), channel_id=1, source_target_pairs={{0,1},{1,0},{2,3},{3,2},{4,5},{5,4},{6,7},{7,6},{8,9},{9,8},{10,11... | collective-permute-start | bytes 1966088 | tf_op jit(solution)/shard_map/ppermute | solution.py:622
  57.3 14.1 %all-to-all-start = ((f32[32,16,128]{2,1,0:T(8,128)}), f32[32,16,128]{2,1,0:T(8,128)S(1)}, u32[]{:S(2)}, u32[]{:S(2)}) async-start(f32[32,16,128]{2,1,0:T(8,128)} %bitcast.1), calls=%async_computation | async-start | bytes 524288 | tf_op jit(solution)/shard_map/all_to_all | solution.py:963
  (16 other events, 38.2 us)
